TPU v7x, 32 devices: a whole 2x2x4 slice. The times are simulated.
32 devices in a mesh: space: 16 (over z, x, core), tm: 2 (over y).
Axes of the slice: x: 2, y: 2, z: 4, core: 2. Of those that a mesh axis runs over, the one named last changes fastest.
Arguments:
- query_key: bfloat16 [1, 16384, 64], P(None, 'space'), may hold values from -1.5 to 8
- selection: bfloat16 [1, 16384, 64], P(None, 'space'), may hold values from 0.19921875 to 1
- memory_key: bfloat16 [8, 16384, 64], P('tm', 'space'), may hold values from -1.5 to 1.5
- shrinkage: bfloat16 [8, 16384], P('tm', 'space'), may hold values from 1 to 4
- memory_value: bfloat16 [8, 16384, 512], P('tm', 'space'), may hold values from -6 to 6
- block_list: int32 [128, 6], P('space'), may hold values from 0 to 11, as said below
- block_count: int32 [128], P('space'), may hold values from 1 to 6, as said below
Outputs:
- readout: bfloat16 [1, 16384, 512], P(None, 'space')
Inputs may be any that keep to these rules, and one draw needn't show every extreme that they name: `block_list`: entries of a row are distinct; rows of the first tile name no block under 2, rows of the last tile none of 10 or above. `block_count`: the first block of every tile uses all 6 listed blocks.
All inputs are finite; a program needn't handle non-finite values.
Results may differ from a plain program's by a relative error of at most 0.0061.
Values may be sent and summed in bfloat16 or wider, within the bound.
No kernel may reach another device: no remote copies, remote signals or barrier semaphores. Data moves between devices by JAX's collectives and lax.ppermute only.
A program may use at most 128 MiB of HBM per device.

v0:
```python
import math

import jax
import jax.numpy as jnp
from jax import lax
from jax.sharding import PartitionSpec as P

BS = 128
W = 2


def padded(x, sides, width):
    for axis, dim in sides:
        size, length = (lax.axis_size(axis), x.shape[dim])
        up = [(i, (i + 1) % size) for i in range(size - 1)]
        down = [(j, i) for i, j in up]
        last = lax.slice_in_dim(x, length - width, length, axis=dim)
        initial = lax.slice_in_dim(x, 0, width, axis=dim)
        before = lax.ppermute(last, axis, up)
        after = lax.ppermute(initial, axis, down)
        x = jnp.concatenate([before, x, after], axis=dim)
    return x


def shards(query_key, selection, memory_key, shrinkage, memory_value, block_list, block_count):
    frames = memory_key.shape[0]
    frames_q = query_key.shape[0]
    pixels = query_key.shape[1]
    key_width = query_key.shape[2]
    value_width = memory_value.shape[2]
    n_blocks = pixels // BS
    n_listed = block_list.shape[1]
    window = n_blocks + 2 * W
    score_scale = 1.0 / math.sqrt(key_width)
    near_key, near_value, near_shrink = (
        padded(memory_key, (("space", 1),), W * BS),
        padded(memory_value, (("space", 1),), W * BS),
        padded(shrinkage, (("space", 1),), W * BS),
    )
    key_square = (near_key.astype(jnp.float32) ** 2).astype(jnp.bfloat16)
    key_blocks = near_key.reshape(frames, window, BS, key_width)
    square_blocks = key_square.reshape(frames, window, BS, key_width)
    value_blocks = near_value.reshape(frames, window, BS, value_width)
    shrink_blocks = near_shrink.reshape(frames, window, BS)
    query_f = query_key.astype(jnp.float32)
    select_f = selection.astype(jnp.float32)
    query_sel = (2.0 * query_f * select_f).astype(jnp.bfloat16)
    self_term = jnp.sum(select_f * query_f * query_f, axis=-1)
    per_step = max((divisor for divisor in (1, 2, 3, 4) if n_blocks % divisor == 0))
    groups = n_blocks // per_step
    query_groups = query_sel.reshape(frames_q, groups, per_step, BS, key_width).transpose(
        1, 2, 0, 3, 4
    )
    select_groups = selection.reshape(frames_q, groups, per_step, BS, key_width).transpose(
        1, 2, 0, 3, 4
    )
    self_groups = self_term.reshape(frames_q, groups, per_step, BS).transpose(1, 2, 0, 3)
    list_groups = block_list.reshape(groups, per_step, n_listed)
    count_groups = block_count.reshape(groups, per_step)

    def score_group(inputs):
        query_grp, select_grp, self_grp, listed = inputs
        squares = jnp.take(square_blocks, listed, axis=1)
        key_rows = jnp.take(key_blocks, listed, axis=1)
        shrink = jnp.take(shrink_blocks, listed, axis=1).astype(jnp.float32).transpose(1, 0, 2, 3)
        quad_term = jnp.einsum(
            "gqrc,fgjnc->gqrfjn", select_grp, squares, preferred_element_type=jnp.float32
        )
        cross_term = jnp.einsum(
            "gqrc,fgjnc->gqrfjn", query_grp, key_rows, preferred_element_type=jnp.float32
        )
        return (
            -shrink[:, None, None]
            * (quad_term - cross_term + self_grp[..., None, None, None])
            * score_scale
        )

    scores = lax.map(score_group, (query_groups, select_groups, self_groups, list_groups))
    usable = (jnp.arange(n_listed, dtype=jnp.int32)[None, None, :] < count_groups[..., None])[
        :, :, None, None, None, :, None
    ]
    local_top = jnp.max(jnp.where(usable, scores, -jnp.inf), axis=(4, 5, 6))

    def read_group(inputs):
        scores_grp, top_grp, usable_grp, listed = inputs
        weights = jnp.where(
            usable_grp,
            jnp.exp(scores_grp - top_grp[..., None, None, None]),
            jnp.zeros_like(scores_grp),
        )
        group_total = jnp.sum(weights, axis=(3, 4, 5))
        values = jnp.take(value_blocks, listed, axis=1)
        group_sum = jnp.einsum(
            "gqrfjn,fgjnv->gqrv",
            weights.astype(jnp.bfloat16),
            values,
            preferred_element_type=jnp.float32,
        )
        return (group_sum, group_total)

    summed, row_total = lax.map(read_group, (scores, local_top, usable, list_groups))
    summed = summed.transpose(2, 0, 1, 3, 4).reshape(frames_q, pixels, value_width)
    row_total = row_total.transpose(2, 0, 1, 3).reshape(frames_q, pixels)
    group_top = local_top.transpose(2, 0, 1, 3).reshape(frames_q, pixels)
    row_top = lax.pmax(group_top, "tm")
    factor = jnp.exp(group_top - row_top)
    summed_all, total_all = lax.psum((summed * factor[..., None], row_total * factor), "tm")
    return (summed_all / total_all[..., None]).astype(jnp.bfloat16)


def solution(mesh):
    in_specs = (
        P(None, "space", None),
        P(None, "space", None),
        P("tm", "space", None),
        P("tm", "space"),
        P("tm", "space", None),
        P("space", None),
        P("space"),
    )
    out_specs = P(None, "space", None)
    return jax.shard_map(shards, mesh=mesh, in_specs=in_specs, out_specs=out_specs, check_vma=False)
```

profile of v0, /device:TPU:25, one launch (start us, length us, event | category | flops | bytes accessed | tf_op | source)
XLA Modules:
  0.0 225.6 jit_solution(15376629082681298847)
XLA Ops:
  6.5 1.0 fusion.35
  7.5 3.7 %collective-permute-start.2 = (bf16[4,256,64]{1,2,0:T(8,128)(2,1)S(1)}, bf16[4,256,64]{1,2,0:T(8,128)(2,1)S(1)}, u32[]{:S(2)}, u32[]{:S(2)}) collective-permute-start(bf16[4,256,64]{1,2,0:T(8,128)(2,1)S(1)} %get-tuple-element.150), channel_id=1, source_target_pairs={{0,2},{2,4},{4,6},{6,8},{8,10},{10,12},{12,14},{14,16},{16,18},{18... | collective-permute-start | bytes 393224 | tf_op jit(solution)/shard_map/ppermute | solution.py:19
  11.2 1.9 collective-permute-start.3
  13.1 0.7 fusion.36
  13.9 3.6 %collective-permute-start = (bf16[4,256]{1,0:T(4,128)(2,1)S(1)}, bf16[4,256]{1,0:T(4,128)(2,1)S(1)}, u32[]{:S(2)}, u32[]{:S(2)}) collective-permute-start(bf16[4,256]{1,0:T(4,128)(2,1)S(1)} %get-tuple-element.154), channel_id=1, source_target_pairs={{0,2},{2,4},{4,6},{6,8},{8,10},{10,12},{12,14},{14,16},{16,18},{18... | collective-permute-start | bytes 6152 | tf_op jit(solution)/shard_map/ppermute | solution.py:19
  17.5 1.9 collective-permute-start.1
  19.4 3.0 %fusion.34 = (bf16[4,256,512]{2,1,0:T(8,128)(2,1)}, bf16[4,256,512]{2,1,0:T(8,128)(2,1)}) fusion(bf16[4,1024,512]{2,1,0:T(8,128)(2,1)} %param.17), kind=kLoop, calls=%fused_computation.65 | loop fusion | bytes 4194304 | tf_op jit(solution)/shard_map/slice | solution.py:17
  22.4 3.6 %collective-permute-start.4 = (bf16[4,256,512]{2,1,0:T(8,128)(2,1)}, bf16[4,256,512]{2,1,0:T(8,128)(2,1)}, u32[]{:S(2)}, u32[]{:S(2)}) collective-permute-start(bf16[4,256,512]{2,1,0:T(8,128)(2,1)} %get-tuple-element.148), channel_id=1, source_target_pairs={{0,2},{2,4},{4,6},{6,8},{8,10},{10,12},{12,14},{14,16},{16,18},{18... | collective-permute-start | bytes 3145736 | tf_op jit(solution)/shard_map/ppermute | solution.py:19
  26.1 0.7 lt.69
  26.8 0.6 iota_compare_fusion
  27.4 1.6 fusion.32
  29.1 0.6 iota_compare_fusion.1
  29.7 1.0 transpose_reshape.9
  30.8 2.6 %collective-permute-start.5 = (bf16[4,256,512]{2,1,0:T(8,128)(2,1)}, bf16[4,256,512]{2,1,0:T(8,128)(2,1)}, u32[]{:S(2)}, u32[]{:S(2)}) collective-permute-start(bf16[4,256,512]{2,1,0:T(8,128)(2,1)} %get-tuple-element.149), channel_id=1, source_target_pairs={{2,0},{4,2},{6,4},{8,6},{10,8},{12,10},{14,12},{16,14},{18,16},{20... | collective-permute-start | bytes 3145736 | tf_op jit(solution)/shard_map/ppermute | solution.py:20
  33.4 0.7 maximum_bitcast_fusion
  34.1 1.1 pad_maximum_fusion.1
  35.2 0.9 copy.17
  36.1 1.6 multiply_convert_fusion
  37.7 52.1 %while.22 = (s32[]{:T(128)}, f32[2,4,1,128,4,6,128]{6,3,5,4,1,2,0:T(8,128)}, s32[2,4,6]{2,1,0:T(4,128)}, bf16[4,12,128]{2,0,1:T(4,128)(2,1)S(1)}, bf16[2,4,1,128...) while((s32[]{:T(128)}, ...), condition=%wide.region_2.4_spmd, body=%wide.region_1.3_spmd.sunk | while | flops 410556640 | bytes 41590792 | solution.py:78
  37.7 0.7 compare_and_fusion.4
  38.5 0.4 copy-done
  38.9 2.6 %gather_fusion = bf16[24,4,128,64]{3,2,1,0:T(8,128)(2,1)S(1)} fusion(bf16[4,12,128,64]{3,2,1,0:T(8,128)(2,1)} %get-tuple-element.293, s32[1024]{0:T(1024)S(1)} %pad_clamp_fusion.6), kind=kCustom, calls=%fused_computation.clone.clone.1 | custom fusion | bytes 3145824 | tf_op jit(solution)/shard_map/while/body/eval_jaxpr/jit(_take)/gather | solution.py:63
  41.4 2.4 %copy.59 = bf16[4,6,4,128,64]{3,4,1,2,0:T(8,128)(2,1)} copy(bf16[4,6,4,128,64]{4,3,2,1,0:T(8,128)(2,1)S(1)} %bitcast.141) | data formatting | bytes 3145728 | tf_op jit(solution)/shard_map/while/body/eval_jaxpr/jit(_take)/gather | solution.py:63
  43.9 5.0 %fusion.52 = f32[4,128,4,6,128]{4,1,3,2,0:T(8,128)} fusion(bf16[4,6,4,128,64]{3,4,1,2,0:T(8,128)(2,1)} %copy.59, pred[4,6]{1,0:T(4,128)(4,1)S(1)} %get-tuple-element.257, bf16[1,4,1,128,64]{3,1,0,4,2:T(4,128)(2,1)S(1)} %get-tuple-element.258), kind=kOutput, calls=%fused_computation.28.clone.1 | convolution fusion | flops 202113024 | bytes 7929880 | tf_op jit(solution)/shard_map/while/body/eval_jaxpr/gqrc,fgjnc->gqrfjn/dot_general | solution.py:66
  49.0 0.7 compare_select_fusion.7
  49.7 0.1 reshape.269
  49.8 0.6 gather_fusion.1
  50.4 0.1 negate_bitcast_fusion.2
  50.5 2.7 %gather_fusion.2 = bf16[24,4,128,64]{3,2,1,0:T(8,128)(2,1)S(1)} fusion(bf16[4,12,128,64]{3,2,1,0:T(8,128)(2,1)} %copy-done, s32[1024]{0:T(1024)} %copy-done.4), kind=kCustom, calls=%fused_computation.2.clone.clone.1 | custom fusion | bytes 3145824 | tf_op jit(solution)/shard_map/while/body/eval_jaxpr/jit(_take)/gather | solution.py:64
  53.2 2.4 %copy.61 = bf16[4,6,4,128,64]{3,4,1,2,0:T(8,128)(2,1)} copy(bf16[4,6,4,128,64]{4,3,2,1,0:T(8,128)(2,1)S(1)} %bitcast.140) | data formatting | bytes 3145728 | tf_op jit(solution)/shard_map/while/body/eval_jaxpr/jit(_take)/gather | solution.py:64
  55.6 0.7 dynamic-slice_bitcast_fusion.6
  56.3 7.5 %bitcast_dynamic-update-slice_fusion.2 = f32[2,4,1,128,4,6,128]{6,3,5,4,1,2,0:T(8,128)} fusion(f32[2,4,1,128,4,6,128]{6,3,5,4,1,2,0:T(8,128)} %get-tuple-element.279, s32[]{:T(128)} %get-tuple-element.278, f32[4,128,4,6,128]{4,1,3,2,0:T(8,128)} %fusion.52, f32[4,128]{1,0:T(4,128)S(1)} %dynamic-slice_bitcast_fusion.6, ...), kind=kOutput, calls=%fused_computation.26.clone.1 | convolution fusion | flops 208404480 | bytes 14273048 | tf_op jit(solution)/shard_map/while/body/eval_jaxpr/gqrc,fgjnc->gqrfjn/dot_general | solution.py:69
  63.8 0.7 compare_and_fusion.4
  64.5 0.4 copy-done
  64.9 2.6 %gather_fusion = bf16[24,4,128,64]{3,2,1,0:T(8,128)(2,1)S(1)} fusion(bf16[4,12,128,64]{3,2,1,0:T(8,128)(2,1)} %get-tuple-element.293, s32[1024]{0:T(1024)S(1)} %pad_clamp_fusion.6), kind=kCustom, calls=%fused_computation.clone.clone.1 | custom fusion | bytes 3145824 | tf_op jit(solution)/shard_map/while/body/eval_jaxpr/jit(_take)/gather | solution.py:63
  67.5 2.4 %copy.59 = bf16[4,6,4,128,64]{3,4,1,2,0:T(8,128)(2,1)} copy(bf16[4,6,4,128,64]{4,3,2,1,0:T(8,128)(2,1)S(1)} %bitcast.141) | data formatting | bytes 3145728 | tf_op jit(solution)/shard_map/while/body/eval_jaxpr/jit(_take)/gather | solution.py:63
  70.0 5.0 %fusion.52 = f32[4,128,4,6,128]{4,1,3,2,0:T(8,128)} fusion(bf16[4,6,4,128,64]{3,4,1,2,0:T(8,128)(2,1)} %copy.59, pred[4,6]{1,0:T(4,128)(4,1)S(1)} %get-tuple-element.257, bf16[1,4,1,128,64]{3,1,0,4,2:T(4,128)(2,1)S(1)} %get-tuple-element.258), kind=kOutput, calls=%fused_computation.28.clone.1 | convolution fusion | flops 202113024 | bytes 7929880 | tf_op jit(solution)/shard_map/while/body/eval_jaxpr/gqrc,fgjnc->gqrfjn/dot_general | solution.py:66
  75.0 0.7 compare_select_fusion.7
  75.8 0.6 gather_fusion.1
  76.4 0.1 negate_bitcast_fusion.2
  76.5 2.7 %gather_fusion.2 = bf16[24,4,128,64]{3,2,1,0:T(8,128)(2,1)S(1)} fusion(bf16[4,12,128,64]{3,2,1,0:T(8,128)(2,1)} %copy-done, s32[1024]{0:T(1024)} %copy-done.4), kind=kCustom, calls=%fused_computation.2.clone.clone.1 | custom fusion | bytes 3145824 | tf_op jit(solution)/shard_map/while/body/eval_jaxpr/jit(_take)/gather | solution.py:64
  79.2 2.4 %copy.61 = bf16[4,6,4,128,64]{3,4,1,2,0:T(8,128)(2,1)} copy(bf16[4,6,4,128,64]{4,3,2,1,0:T(8,128)(2,1)S(1)} %bitcast.140) | data formatting | bytes 3145728 | tf_op jit(solution)/shard_map/while/body/eval_jaxpr/jit(_take)/gather | solution.py:64
  81.7 0.7 dynamic-slice_bitcast_fusion.6
  82.3 7.4 %bitcast_dynamic-update-slice_fusion.2 = f32[2,4,1,128,4,6,128]{6,3,5,4,1,2,0:T(8,128)} fusion(f32[2,4,1,128,4,6,128]{6,3,5,4,1,2,0:T(8,128)} %get-tuple-element.279, s32[]{:T(128)} %get-tuple-element.278, f32[4,128,4,6,128]{4,1,3,2,0:T(8,128)} %fusion.52, f32[4,128]{1,0:T(4,128)S(1)} %dynamic-slice_bitcast_fusion.6, ...), kind=kOutput, calls=%fused_computation.26.clone.1 | convolution fusion | flops 208404480 | bytes 14273048 | tf_op jit(solution)/shard_map/while/body/eval_jaxpr/gqrc,fgjnc->gqrfjn/dot_general | solution.py:69
  89.8 5.6 %select_reduce_fusion = f32[2,4,128]{2,1,0:T(4,128)S(1)} fusion(f32[2,4,1,128,4,6,128]{6,3,5,4,1,2,0:T(8,128)} %get-tuple-element.302, pred[2,4,6]{2,1,0:T(4,128)(4,1)} %iota_compare_fusion), kind=kLoop, calls=%fused_computation.49 | loop fusion | flops 6290432 | bytes 12587056 | tf_op jit(solution)/shard_map/reduce_max | solution.py:82
  95.3 3.8 %pmax.7 = f32[1,1024]{1,0:T(1,128)S(1)} all-reduce(f32[1,1024]{1,0:T(1,128)S(1)} %bitcast.147), channel_id=1, replica_groups=mesh['space'=16,'tm'=2] {'tm'}, use_global_device_ids=true, to_apply=%region_7.9 | all-reduce | flops 1024 | bytes 8192 | tf_op jit(solution)/shard_map/pmax | solution.py:105
  99.2 6.0 %pad_maximum_fusion = bf16[4,1536,512]{2,1,0:T(8,128)(2,1)} fusion(bf16[4,256,512]{2,1,0:T(8,128)(2,1)} %collective-permute-done.5, bf16[4,1024,512]{2,1,0:T(8,128)(2,1)} %param.17, bf16[4,256,512]{2,1,0:T(8,128)(2,1)} %collective-permute-done.4), kind=kLoop, calls=%fused_computation.50 | loop fusion | flops 18874368 | bytes 12582912 | tf_op jit(solution)/shard_map/concatenate | solution.py:21
  105.2 42.9 %while.23 = (s32[]{:T(128)}, f32[2,4,1,128,512]{4,3,1,2,0:T(8,128)S(1)}, f32[2,4,1,128]{3,2,1,0:T(1,128)S(1)}, pred[2,4,1,1,1,6,1]{5,1,6,4,3,2,0:T(4,128)(4,1)S(...) while((s32[]{:T(128)}, ...), condition=%wide.region_6.8_spmd, body=%wide.region_4.7_spmd.sunk | while | flops 1626342144 | bytes 101733264 | solution.py:101
  105.2 0.7 compare_select_fusion.8
  106.0 8.8 %gather_fusion.3 = bf16[24,4,128,512]{3,2,1,0:T(8,128)(2,1)} fusion(bf16[4,12,128,512]{3,2,1,0:T(8,128)(2,1)} %get-tuple-element.323, s32[1024]{0:T(1024)S(1)} %pad_clamp_fusion.8), kind=kCustom, calls=%fused_computation.1.clone.1 | custom fusion | bytes 25165920 | tf_op jit(solution)/shard_map/while/body/eval_jaxpr/jit(_take)/gather | solution.py:92
  114.8 0.7 compare_and_fusion.5
  115.5 8.2 %fusion.57 = f32[2,4,1,128,512]{4,3,1,2,0:T(8,128)S(1)} fusion(f32[2,4,1,128,512]{4,3,1,2,0:T(8,128)S(1)} %get-tuple-element.308, s32[]{:T(128)} %get-tuple-element.307, bf16[4,6,4,128,512]{4,3,2,1,0:T(8,128)(2,1)} %bitcast.139, pred[4,6]{1,0:T(4,128)(4,1)S(1)} %compare_and_fusion.5, f32[2,4,1,128,4,6,128]{6,3,5,4,1,2,0:T(8,128)} %get-tuple-element.320, ...), kind=kOutput, calls=%fused_computation.18.clone.1 | convolution fusion | flops 1621622784 | bytes 19927040 | tf_op jit(solution)/shard_map/while/body/eval_jaxpr/gqrfjn,fgjnv->gqrv/dot_general | solution.py:93
  123.7 1.8 copy-done.2
  125.5 1.2 fusion.58
  126.7 0.7 compare_select_fusion.8
  127.5 8.8 %gather_fusion.3 = bf16[24,4,128,512]{3,2,1,0:T(8,128)(2,1)} fusion(bf16[4,12,128,512]{3,2,1,0:T(8,128)(2,1)} %get-tuple-element.323, s32[1024]{0:T(1024)S(1)} %pad_clamp_fusion.8), kind=kCustom, calls=%fused_computation.1.clone.1 | custom fusion | bytes 25165920 | tf_op jit(solution)/shard_map/while/body/eval_jaxpr/jit(_take)/gather | solution.py:92
  136.3 0.7 compare_and_fusion.5
  137.0 8.2 %fusion.57 = f32[2,4,1,128,512]{4,3,1,2,0:T(8,128)S(1)} fusion(f32[2,4,1,128,512]{4,3,1,2,0:T(8,128)S(1)} %get-tuple-element.308, s32[]{:T(128)} %get-tuple-element.307, bf16[4,6,4,128,512]{4,3,2,1,0:T(8,128)(2,1)} %bitcast.139, pred[4,6]{1,0:T(4,128)(4,1)S(1)} %compare_and_fusion.5, f32[2,4,1,128,4,6,128]{6,3,5,4,1,2,0:T(8,128)} %get-tuple-element.320, ...), kind=kOutput, calls=%fused_computation.18.clone.1 | convolution fusion | flops 1621622784 | bytes 19927040 | tf_op jit(solution)/shard_map/while/body/eval_jaxpr/gqrfjn,fgjnv->gqrv/dot_general | solution.py:93
  145.2 1.8 copy-done.2
  146.9 1.2 fusion.58
  148.2 1.5 broadcast_multiply_fusion
  149.7 3.8 %psum.15 = f32[1024]{0:T(1024)S(1)} all-reduce(f32[1024]{0:T(1024)S(1)} %bitcast.152), channel_id=1, replica_groups=mesh['space'=16,'tm'=2] {'tm'}, use_global_device_ids=true, to_apply=%region_9.11 | all-reduce | flops 1024 | bytes 8192 | tf_op jit(solution)/shard_map/psum | solution.py:107
  153.5 62.5 %all-reduce.2.cloned.1.call-done = f32[1,1024,512]{2,1,0:T(8,128)} async-done(((f32[1,1024,512]{2,1,0:T(8,128)}), f32[1,1024,512]{2,1,0:T(8,128)}) %all-reduce.2.cloned.1.call-update) | async-done | bytes 2097168 | tf_op jit(solution)/shard_map/psum | solution.py:107
  216.0 2.8 %divide_convert_fusion = bf16[1,1024,512]{2,1,0:T(8,128)(2,1)} fusion(f32[1,1024,512]{2,1,0:T(8,128)} %all-reduce.2.cloned.1.call-done, f32[1024]{0:T(1024)S(1)} %psum.15), kind=kLoop, calls=%fused_computation.52 | loop fusion | flops 1048576 | bytes 3149824 | tf_op jit(solution)/shard_map/convert_element_type | solution.py:108
  (52 shorter events, 0.8 us)
Async XLA Ops:
  6.5 209.5 %all-reduce.2.cloned.1.call-start = ((), (), s32[]{:S(2)}) async-start(), calls=%async_computation | async-start | bytes 4194304 | tf_op jit(solution)/shard_map/psum | solution.py:107
  7.5 26.6 %collective-permute-start.2 = (bf16[4,256,64]{1,2,0:T(8,128)(2,1)S(1)}, bf16[4,256,64]{1,2,0:T(8,128)(2,1)S(1)}, u32[]{:S(2)}, u32[]{:S(2)}) collective-permute-start(bf16[4,256,64]{1,2,0:T(8,128)(2,1)S(1)} %get-tuple-element.150), channel_id=1, source_target_pairs={{0,2},{2,4},{4,6},{6,8},{8,10},{10,12},{12,14},{14,16},{16,18},{18... | collective-permute-start | bytes 393224 | tf_op jit(solution)/shard_map/ppermute | solution.py:19
  11.2 22.9 %collective-permute-start.3 = (bf16[4,256,64]{1,2,0:T(8,128)(2,1)S(1)}, bf16[4,256,64]{1,2,0:T(8,128)(2,1)S(1)}, u32[]{:S(2)}, u32[]{:S(2)}) collective-permute-start(bf16[4,256,64]{1,2,0:T(8,128)(2,1)S(1)} %get-tuple-element.151), channel_id=1, source_target_pairs={{2,0},{4,2},{6,4},{8,6},{10,8},{12,10},{14,12},{16,14},{18,16},{20... | collective-permute-start | bytes 393224 | tf_op jit(solution)/shard_map/ppermute | solution.py:20
  13.9 16.9 %collective-permute-start = (bf16[4,256]{1,0:T(4,128)(2,1)S(1)}, bf16[4,256]{1,0:T(4,128)(2,1)S(1)}, u32[]{:S(2)}, u32[]{:S(2)}) collective-permute-start(bf16[4,256]{1,0:T(4,128)(2,1)S(1)} %get-tuple-element.154), channel_id=1, source_target_pairs={{0,2},{2,4},{4,6},{6,8},{8,10},{10,12},{12,14},{14,16},{16,18},{18... | collective-permute-start | bytes 6152 | tf_op jit(solution)/shard_map/ppermute | solution.py:19
  17.5 15.9 %collective-permute-start.1 = (bf16[4,256]{1,0:T(4,128)(2,1)S(1)}, bf16[4,256]{1,0:T(4,128)(2,1)S(1)}, u32[]{:S(2)}, u32[]{:S(2)}) collective-permute-start(bf16[4,256]{1,0:T(4,128)(2,1)S(1)} %get-tuple-element.155), channel_id=1, source_target_pairs={{2,0},{4,2},{6,4},{8,6},{10,8},{12,10},{14,12},{16,14},{18,16},{20... | collective-permute-start | bytes 6152 | tf_op jit(solution)/shard_map/ppermute | solution.py:20
  22.4 76.7 %collective-permute-start.4 = (bf16[4,256,512]{2,1,0:T(8,128)(2,1)}, bf16[4,256,512]{2,1,0:T(8,128)(2,1)}, u32[]{:S(2)}, u32[]{:S(2)}) collective-permute-start(bf16[4,256,512]{2,1,0:T(8,128)(2,1)} %get-tuple-element.148), channel_id=1, source_target_pairs={{0,2},{2,4},{4,6},{6,8},{8,10},{10,12},{12,14},{14,16},{16,18},{18... | collective-permute-start | bytes 3145736 | tf_op jit(solution)/shard_map/ppermute | solution.py:19
  30.8 68.4 %collective-permute-start.5 = (bf16[4,256,512]{2,1,0:T(8,128)(2,1)}, bf16[4,256,512]{2,1,0:T(8,128)(2,1)}, u32[]{:S(2)}, u32[]{:S(2)}) collective-permute-start(bf16[4,256,512]{2,1,0:T(8,128)(2,1)} %get-tuple-element.149), channel_id=1, source_target_pairs={{2,0},{4,2},{6,4},{8,6},{10,8},{12,10},{14,12},{16,14},{18,16},{20... | collective-permute-start | bytes 3145736 | tf_op jit(solution)/shard_map/ppermute | solution.py:20
  37.7 1.2 copy-start
  38.9 10.1 %copy-start.4 = (s32[1024]{0:T(1024)}, s32[1024]{0:T(1024)S(1)}, u32[]{:S(2)}) copy-start(s32[1024]{0:T(1024)S(1)} %pad_clamp_fusion.6) | copy-start | bytes 12292 | tf_op jit(solution)/shard_map/while
  56.3 7.5 %copy-start.1 = (bf16[4,12,128,64]{3,2,1,0:T(8,128)(2,1)S(1)}, bf16[4,12,128,64]{3,2,1,0:T(8,128)(2,1)}, u32[]{:S(2)}) copy-start(bf16[4,12,128,64]{3,2,1,0:T(8,128)(2,1)} %copy-done) | copy-start | bytes 2359300 | tf_op jit(solution)/shard_map/while
  63.8 1.2 copy-start
  64.9 10.1 %copy-start.4 = (s32[1024]{0:T(1024)}, s32[1024]{0:T(1024)S(1)}, u32[]{:S(2)}) copy-start(s32[1024]{0:T(1024)S(1)} %pad_clamp_fusion.6) | copy-start | bytes 12292 | tf_op jit(solution)/shard_map/while
  82.3 7.5 %copy-start.1 = (bf16[4,12,128,64]{3,2,1,0:T(8,128)(2,1)S(1)}, bf16[4,12,128,64]{3,2,1,0:T(8,128)(2,1)}, u32[]{:S(2)}) copy-start(bf16[4,12,128,64]{3,2,1,0:T(8,128)(2,1)} %copy-done) | copy-start | bytes 2359300 | tf_op jit(solution)/shard_map/while
  99.1 6.0 %copy-start.3 = (f32[2,4,1,128,512]{4,3,1,2,0:T(8,128)S(1)}, f32[2,4,1,128,512]{4,3,1,2,0:T(8,128)}, u32[]{:S(2)}) copy-start(f32[2,4,1,128,512]{4,3,1,2,0:T(8,128)} %custom-call.9) | copy-start | bytes 6291460
  99.1 6.0 %copy-start.5 = (f32[2,4,1,128]{3,2,1,0:T(1,128)S(1)}, f32[2,4,1,128]{3,2,1,0:T(1,128)}, u32[]{:S(2)}) copy-start(f32[2,4,1,128]{3,2,1,0:T(1,128)} %custom-call.10) | copy-start | bytes 12292
  99.2 6.0 %copy-start.6 = (pred[2,4,1,1,1,6,1]{5,1,6,4,3,2,0:T(4,128)(4,1)S(1)}, pred[2,4,1,1,1,6,1]{5,1,6,4,3,2,0:T(4,128)(4,1)}, u32[]{:S(2)}) copy-start(pred[2,4,1,1,1,6,1]{5,1,6,4,3,2,0:T(4,128)(4,1)} %iota_compare_fusion.1) | copy-start | bytes 148
  115.5 10.0 %copy-start.2 = (f32[2,4,1,128,4,6,128]{6,3,5,4,1,2,0:T(8,128)S(1)}, f32[2,4,1,128,4,6,128]{6,3,5,4,1,2,0:T(8,128)}, u32[]{:S(2)}) copy-start(f32[2,4,1,128,4,6,128]{6,3,5,4,1,2,0:T(8,128)} %get-tuple-element.320) | copy-start | bytes 37748740 | tf_op jit(solution)/shard_map/while
  136.9 10.0 %copy-start.2 = (f32[2,4,1,128,4,6,128]{6,3,5,4,1,2,0:T(8,128)S(1)}, f32[2,4,1,128,4,6,128]{6,3,5,4,1,2,0:T(8,128)}, u32[]{:S(2)}) copy-start(f32[2,4,1,128,4,6,128]{6,3,5,4,1,2,0:T(8,128)} %get-tuple-element.320) | copy-start | bytes 37748740 | tf_op jit(solution)/shard_map/while
Sparse Core Ops, SparseCore 0:
  149.8 66.1 all-reduce.1
where the time goes:
time: 228 us; the launch traced here: 226 us
  waiting for transfers between devices  62.5 us (27%)
  local copies, waits for them, and re-layouts  52.8 us (23%)
  matrix products  41.4 us (18%)
  other arithmetic  30.2 us (13%)
  starting transfers between devices  17.4 us (8%)
  between operations  13.6 us (6%)
  blocking collectives  7.59 us (3%)
    psum x1, waiting for transfers between devices, shards(): lax.psum((summed * factor[..., None], row_total * factor), 'tm')  62.5 us
    gather x2, local copies, waits for them, and re-layouts, read_group(): values = jnp.take(value_blocks, listed, axis=1)  17.6 us
    dot_general x2, matrix products, read_group(): jnp.einsum('gqrfjn,fgjnv->gqrv', weights.astype(jnp.bfloat16), values, pr...  16.4 us
    dot_general x2, matrix products, score_group(): jnp.einsum('gqrc,fgjnc->gqrfjn', query_grp, key_rows, preferred_element_t...  14.9 us
    ppermute x3, starting transfers between devices, padded(): before = lax.ppermute(last, axis, up)  10.9 us
    gather x4, local copies, waits for them, and re-layouts, score_group(): key_rows = jnp.take(key_blocks, listed, axis=1)  10.2 us
    dot_general x2, matrix products, score_group(): jnp.einsum('gqrc,fgjnc->gqrfjn', select_grp, squares, preferred_element_t...  10.1 us
    gather x4, local copies, waits for them, and re-layouts, score_group(): squares = jnp.take(square_blocks, listed, axis=1)  9.99 us
  transfers between devices with their start and end apart: 7, of which 1 were waited for; matrix products, arithmetic and copies ran while one was open for 31% of the time, Pallas kernels for 0%

commit v1 on v0

v1 whole, which is shorter than its diff:
```python
import functools
import math

import jax
import jax.numpy as jnp
from jax import lax
from jax.experimental import pallas as pl
from jax.experimental.pallas import tpu as pltpu
from jax.sharding import PartitionSpec as P

BS = 128
W = 2
LANES = 128
EDGE = W * BS
NONE = -1e30
OWN_AT, HALO_AT, COUNT_AT = 0, 64, 128
F32, BF16 = jnp.float32, jnp.bfloat16

VMEM = pl.BlockSpec(memory_space=pltpu.VMEM)
SMEM = pl.BlockSpec(memory_space=pltpu.SMEM)
HBM = pl.BlockSpec(memory_space=pl.ANY)


def params(mib):
    return pltpu.CompilerParams(vmem_limit_bytes=mib * 1024 * 1024)


def nt_dot(a, b):
    return lax.dot_general(a, b, (((1,), (1,)), ((), ())), preferred_element_type=F32)


def lane_tiles(x):
    return [x[:, i * LANES : (i + 1) * LANES] for i in range(x.shape[1] // LANES)]


def wide(x, times):
    return jnp.concatenate([x] * times, axis=1)


def lists_and_edges(
    sizes, list_ref, count_ref, key_ref, shrink_ref, value_ref, pairs_ref, chip_ref, link_ref, key_sc, shr_sc, sems
):
    frames, pixels, n_blocks, n_listed, key_width, value_width = sizes
    odd = lax.rem(lax.axis_index("space"), 2)
    rows = frames * EDGE
    starts = [
        pl.multiple_of((1 - odd) * (pixels - EDGE), EDGE),
        pl.multiple_of(odd * (pixels - EDGE), EDGE),
    ]
    copies = []
    for e in range(W):
        for f in range(frames):
            at = (e * frames + f) * BS
            copies.append(
                pltpu.make_async_copy(
                    value_ref.at[f, pl.ds(starts[0] + e * BS, BS), :],
                    chip_ref.at[pl.ds(at, BS), :],
                    sems.at[0, e * frames + f],
                )
            )
            copies.append(
                pltpu.make_async_copy(
                    value_ref.at[f, pl.ds(starts[1] + e * BS, BS), pl.ds(0, LANES)],
                    link_ref.at[pl.ds(at, BS), :],
                    sems.at[1, e * frames + f],
                )
            )
    for copy in copies:
        copy.start()
    last = []
    for side in range(2):
        for f in range(frames):
            blocks = [key_ref[f, pl.ds(starts[side] + e * BS, BS), :] for e in range(W)]
            key_sc[side, f * BS : (f + 1) * BS, :] = jnp.concatenate(blocks, axis=1)
        edge = shrink_ref[:, pl.ds(starts[side], EDGE)].astype(F32)
        rows_e = [edge[:, e * BS : (e + 1) * BS] for e in range(W)]
        pad = jnp.zeros((16 - W * frames, LANES), F32)
        key_sc[side, frames * BS :, :] = jnp.concatenate(rows_e + [pad], axis=0).astype(BF16)
    key_rows = frames * BS + 16
    if True:
        copy = pltpu.make_async_copy(key_sc.at[1], link_ref.at[pl.ds(rows, key_rows), :], sems.at[1, W * frames])
        copy.start()
        last.append(copy)
        for i in range(4):
            part = key_rows // 4 // 16 * 16
            size = part if i < 3 else key_rows - 3 * part
            copy = pltpu.make_async_copy(
                key_sc.at[0, pl.ds(i * part, size), :],
                chip_ref.at[pl.ds(rows, size), pl.ds(i * LANES, LANES)],
                sems.at[0, W * frames + i],
            )
            copy.start()
            last.append(copy)

    def block(b, carry):
        live = count_ref[b]
        for j in range(n_listed):
            n_own, n_halo = carry
            l = list_ref[b, j]
            ok = j < live
            inside = (l >= W) & (l < W + n_blocks)
            right = jnp.where(l >= W + n_blocks, 1, 0)
            e = jnp.where(right == 1, l - (W + n_blocks), l)
            over_link = jnp.where(right == odd, 1, 0)
            pairs_ref[OWN_AT + n_own] = b * n_blocks + jnp.clip(l - W, 0, n_blocks - 1)
            pairs_ref[HALO_AT + n_halo] = b * 4 + over_link * W + jnp.clip(e, 0, W - 1)
            carry = (
                n_own + jnp.where(ok & inside, 1, 0),
                n_halo + jnp.where(ok & jnp.logical_not(inside), 1, 0),
            )
        return carry

    n_own, n_halo = lax.fori_loop(0, n_blocks, block, (0, 0))
    pairs_ref[OWN_AT + n_own] = n_blocks * n_blocks
    pairs_ref[HALO_AT + n_halo] = n_blocks * 4
    pairs_ref[COUNT_AT] = n_own
    pairs_ref[COUNT_AT + 1] = n_halo
    for copy in copies + last:
        copy.wait()


def edge_chunks(sizes, n_chunks, value_ref, *refs):
    frames, pixels = sizes[:2]
    outs, sems = refs[:-1], refs[-1]
    odd = lax.rem(lax.axis_index("space"), 2)
    start = pl.multiple_of(odd * (pixels - EDGE), EDGE)
    copies = []
    for c, out in enumerate(outs):
        for e in range(W):
            for f in range(frames):
                copies.append(
                    pltpu.make_async_copy(
                        value_ref.at[f, pl.ds(start + e * BS, BS), pl.ds((c + 1) * LANES, LANES)],
                        out.at[pl.ds((e * frames + f) * BS, BS), :],
                        sems.at[c, e * frames + f],
                    )
                )
    for copy in copies:
        copy.start()
    for copy in copies:
        copy.wait()


def paired(count, body):
    def step(i, carry):
        body(2 * i)
        body(2 * i + 1)
        return carry

    lax.fori_loop(0, (count + 1) // 2, step, 0)


def own_part(
    sizes, pairs_ref, query_ref, select_ref, key_ref, shrink_ref, value_ref,
    acc_ref, top_ref, total_ref, cat_ref, self_ref,
    keys_sc, shr_sc, score_sc, value_sc, sem,
):
    frames, pixels, n_blocks, n_listed, key_width, value_width = sizes
    cols = frames * BS
    bits = int(math.log2(n_blocks))
    values = pltpu.make_async_copy(value_ref, value_sc, sem)
    values.start()
    scale = -math.log2(math.e) / math.sqrt(key_width)
    for b in range(n_blocks):
        q = query_ref[b * BS : (b + 1) * BS, :].astype(F32)
        s = select_ref[b * BS : (b + 1) * BS, :]
        s_f = s.astype(F32)
        cat_ref[b] = jnp.concatenate([s, (-2.0 * q * s_f).astype(BF16)], axis=1)
        term = jnp.sum(s_f * q * q, axis=1, keepdims=True)
        self_ref[b] = jnp.broadcast_to(term, (BS, LANES))
    cat_ref[n_blocks] = jnp.zeros((BS, 2 * key_width), BF16)
    self_ref[n_blocks] = jnp.zeros((BS, LANES), F32)
    shrink = shrink_ref[...].astype(F32) * scale
    for l in range(n_blocks):
        for f in range(frames):
            k = key_ref[f, l * BS : (l + 1) * BS, :]
            k_f = k.astype(F32)
            keys_sc[l, f * BS : (f + 1) * BS, :] = jnp.concatenate([(k_f * k_f).astype(BF16), k], axis=1)
            shr_sc[l, :, f * BS : (f + 1) * BS] = shrink[f : f + 1, l * BS : (l + 1) * BS]
    top_ref[...] = jnp.full_like(top_ref, NONE)
    total_ref[...] = jnp.zeros_like(total_ref)
    acc_ref[...] = jnp.zeros_like(acc_ref)
    count = pairs_ref[COUNT_AT]

    def score(p):
        code = pairs_ref[OWN_AT + p]
        b, l = code >> bits, code & (n_blocks - 1)
        s = nt_dot(cat_ref[b], keys_sc[l])
        s = (s + wide(self_ref[b], frames)) * shr_sc[l]
        score_sc[p] = s
        top_ref[b] = functools.reduce(jnp.maximum, lane_tiles(s), top_ref[b])

    paired(count, score)
    for b in range(n_blocks):
        top_ref[b] = jnp.broadcast_to(jnp.max(top_ref[b], axis=1, keepdims=True), (BS, LANES))
    values.wait()

    def read(p):
        code = pairs_ref[OWN_AT + p]
        b, l = code >> bits, code & (n_blocks - 1)
        w = jnp.exp2(score_sc[p] - wide(top_ref[b], frames))
        total_ref[b] = functools.reduce(jnp.add, lane_tiles(w), total_ref[b])
        v = value_sc[:, pl.ds(pl.multiple_of(l * BS, BS), BS), :].reshape(cols, value_width)
        acc_ref[b] += jnp.dot(w.astype(BF16), v, preferred_element_type=F32)

    paired(count, read)


def halo_scores(
    sizes, pairs_ref, cat_ref, self_ref, chip_ref, link_ref, own_top_ref, own_total_ref,
    weight_ref, factor_ref, stats_ref,
    keys_sc, shr_sc, score_sc, top_sc, total_sc, weight_sc, sems,
):
    frames, pixels, n_blocks, n_listed, key_width, value_width = sizes
    rows = frames * EDGE
    key_rows = frames * BS + 16
    part = key_rows // 4 // 16 * 16
    scale = -math.log2(math.e) / math.sqrt(key_width)
    chip_parts = [
        chip_ref[: (part if i < 3 else key_rows - 3 * part), i * LANES : (i + 1) * LANES] for i in range(4)
    ]
    packs = [jnp.concatenate(chip_parts, axis=0), link_ref[...]]
    for side in range(2):
        shrink = packs[side][frames * BS :, :].astype(F32) * scale
        for f in range(frames):
            k2 = packs[side][f * BS : (f + 1) * BS, :]
            k2_f = k2.astype(F32)
            q2 = (k2_f * k2_f).astype(BF16)
            for e in range(W):
                lanes = slice(e * key_width, (e + 1) * key_width)
                keys_sc[side * W + e, f * BS : (f + 1) * BS, :] = jnp.concatenate([q2[:, lanes], k2[:, lanes]], axis=1)
                at = e * frames + f
                shr_sc[side * W + e, :, f * BS : (f + 1) * BS] = shrink[at : at + 1, :]
    top_sc[...] = jnp.full_like(top_sc, NONE)
    total_sc[...] = jnp.zeros_like(total_sc)
    count = pairs_ref[COUNT_AT + 1]

    def score(p):
        code = pairs_ref[HALO_AT + p]
        b, h = code >> 2, code & 3
        s = nt_dot(cat_ref[b], keys_sc[h])
        s = (s + wide(self_ref[b], frames)) * shr_sc[h]
        score_sc[p] = s
        top_sc[b] = functools.reduce(jnp.maximum, lane_tiles(s), top_sc[b])

    paired(count, score)
    for b in range(n_blocks):
        own = own_top_ref[b]
        top = jnp.maximum(own, jnp.broadcast_to(jnp.max(top_sc[b], axis=1, keepdims=True), (BS, LANES)))
        top_sc[b] = top
        factor_ref[b] = jnp.exp2(own - top)

    def weigh(p):
        code = pairs_ref[HALO_AT + p]
        b = code >> 2
        w = jnp.exp2(score_sc[p] - wide(top_sc[b], frames))
        total_sc[b] = functools.reduce(jnp.add, lane_tiles(w), total_sc[b])
        weight_sc[p] = w.astype(BF16)
        pltpu.make_async_copy(weight_sc.at[p], weight_ref.at[p], sems.at[p]).start()

    paired(count, weigh)
    for b in range(n_blocks):
        total = jnp.sum(total_sc[b] + own_total_ref[b] * factor_ref[b], axis=1, keepdims=True)
        stats_ref[b : b + 1, :] = jnp.transpose(top_sc[b])[:1, :]
        stats_ref[n_blocks + b : n_blocks + b + 1, :] = jnp.transpose(jnp.broadcast_to(total, (BS, LANES)))[:1, :]

    def drain(p):
        pltpu.make_async_copy(weight_sc.at[p], weight_ref.at[p], sems.at[p]).wait()

    paired(count, drain)


def chunk_sums(sizes, c, pairs_ref, weight_ref, acc_ref, factor_ref, stats_ref, chip_ref, link_ref, out_ref, weight_sc, sum_sc, sems):
    frames, pixels, n_blocks, n_listed, key_width, value_width = sizes
    cols = frames * BS
    count = pairs_ref[COUNT_AT + 1]

    def fetch(p):
        pltpu.make_async_copy(weight_ref.at[p], weight_sc.at[p], sems.at[p]).start()

    paired(count, fetch)
    for b in range(n_blocks):
        sum_sc[b] = acc_ref[b] * factor_ref[b]
    sum_sc[n_blocks] = jnp.zeros((BS, LANES), F32)

    def add(p):
        pltpu.make_async_copy(weight_ref.at[p], weight_sc.at[p], sems.at[p]).wait()
        code = pairs_ref[HALO_AT + p]
        b, h = code >> 2, code & 3
        at = pl.multiple_of((h & (W - 1)) * cols, cols)
        v = jnp.where(h >= W, link_ref[pl.ds(at, cols), :], chip_ref[pl.ds(at, cols), :])
        sum_sc[b] += jnp.dot(weight_sc[p], v, preferred_element_type=F32)

    paired(count, add)
    for b in range(n_blocks):
        out_ref[b * BS : (b + 1) * BS, :] = sum_sc[b].astype(BF16)
    if c == 0:
        rest = stats_ref[...]
        for i in range(3):
            piece = rest.astype(BF16)
            rest = rest - piece.astype(F32)
            out_ref[pixels + i * 2 * n_blocks : pixels + (i + 1) * 2 * n_blocks, :] = piece


def unpack_stats(x, n_blocks):
    n = 2 * n_blocks
    x = x.astype(F32)
    x = (x[:n] + x[n : 2 * n]) + x[2 * n :]
    return x[:n_blocks], x[n_blocks:]


def combine(sizes, n_chunks, *refs):
    frames, pixels, n_blocks = sizes[:3]
    mine, other, out_ref = refs[:n_chunks], refs[n_chunks : 2 * n_chunks], refs[-1]

    def run(first, second):
        top_a, total_a = unpack_stats(first[0][pixels:, :], n_blocks)
        top_b, total_b = unpack_stats(second[0][pixels:, :], n_blocks)
        top = jnp.maximum(top_a, top_b)
        a, b = jnp.exp2(top_a - top), jnp.exp2(top_b - top)
        total = total_a * a + total_b * b
        a, b = a / total, b / total
        for i in range(n_blocks):
            col_a = jnp.transpose(jnp.broadcast_to(a[i : i + 1, :], (BS, LANES)))
            col_b = jnp.transpose(jnp.broadcast_to(b[i : i + 1, :], (BS, LANES)))
            r = slice(i * BS, (i + 1) * BS)
            for c in range(n_chunks):
                x = first[c][r, :].astype(F32) * col_a + second[c][r, :].astype(F32) * col_b
                out_ref[r, c * LANES : (c + 1) * LANES] = x.astype(BF16)

    me = lax.axis_index("tm")

    @pl.when(me == 0)
    def _():
        run(mine, other)

    @pl.when(me != 0)
    def _():
        run(other, mine)


def shards(n_space, n_tm, query_key, selection, memory_key, shrinkage, memory_value, block_list, block_count):
    frames, pixels, key_width = memory_key.shape
    value_width = memory_value.shape[2]
    n_blocks, n_listed = block_list.shape
    sizes = (frames, pixels, n_blocks, n_listed, key_width, value_width)
    n_chunks = value_width // LANES
    rows = frames * EDGE
    key_rows = frames * BS + 16
    chip_key_rows = key_rows - 3 * (key_rows // 4 // 16 * 16)
    max_halo = n_blocks * min(n_listed, 2 * W) + 2
    max_own = n_blocks * n_listed + 2
    struct = jax.ShapeDtypeStruct
    query, select = query_key[0], selection[0]

    pairs, chip_edge, link_edge = pl.pallas_call(
        functools.partial(lists_and_edges, sizes),
        out_shape=(
            struct((256,), jnp.int32),
            struct((rows + chip_key_rows, value_width), BF16),
            struct((rows + key_rows, LANES), BF16),
        ),
        in_specs=[SMEM, SMEM, VMEM, VMEM, HBM],
        out_specs=(SMEM, HBM, HBM),
        scratch_shapes=[
            pltpu.VMEM((2, key_rows, LANES), BF16),
            pltpu.VMEM((8, LANES), F32),
            pltpu.SemaphoreType.DMA((2, W * frames + 4)),
        ],
        compiler_params=params(16),
        name="lists_and_edges",
    )(block_list, block_count, memory_key, shrinkage, memory_value)
    more_edges = pl.pallas_call(
        functools.partial(edge_chunks, sizes, n_chunks),
        out_shape=[struct((rows, LANES), BF16)] * (n_chunks - 1),
        in_specs=[HBM],
        out_specs=[HBM] * (n_chunks - 1),
        scratch_shapes=[pltpu.SemaphoreType.DMA((n_chunks - 1, W * frames))],
        compiler_params=params(16),
        name="edge_chunks",
    )(memory_value)

    on_chip = [(i ^ 1, i) for i in range(n_space)]
    over_link = []
    for i in range(1, n_space - 1, 2):
        over_link += [(i, i + 1), (i + 1, i)]
    link_halo = [lax.ppermute(link_edge, "space", over_link)]
    chip_halo = lax.ppermute(chip_edge, "space", on_chip)
    for edge in more_edges:
        link_halo.append(lax.ppermute(edge, "space", over_link))

    acc, own_top, own_total, cat, self_term = pl.pallas_call(
        functools.partial(own_part, sizes),
        out_shape=(
            struct((n_blocks + 1, BS, value_width), F32),
            struct((n_blocks + 1, BS, LANES), F32),
            struct((n_blocks + 1, BS, LANES), F32),
            struct((n_blocks + 1, BS, 2 * key_width), BF16),
            struct((n_blocks + 1, BS, LANES), F32),
        ),
        in_specs=[SMEM, VMEM, VMEM, VMEM, VMEM, HBM],
        out_specs=(VMEM,) * 5,
        scratch_shapes=[
            pltpu.VMEM((n_blocks, frames * BS, 2 * key_width), BF16),
            pltpu.VMEM((n_blocks, 1, frames * BS), F32),
            pltpu.VMEM((max_own, BS, frames * BS), F32),
            pltpu.VMEM(memory_value.shape, BF16),
            pltpu.SemaphoreType.DMA,
        ],
        compiler_params=params(44),
        name="own_part",
    )(pairs, query, select, memory_key, shrinkage, memory_value)

    weights, factor, stats = pl.pallas_call(
        functools.partial(halo_scores, sizes),
        out_shape=(
            struct((max_halo, BS, frames * BS), BF16),
            struct((n_blocks + 1, BS, LANES), F32),
            struct((2 * n_blocks, LANES), F32),
        ),
        grid=(1,),
        in_specs=[
            SMEM,
            VMEM,
            VMEM,
            pl.BlockSpec((chip_key_rows, value_width), lambda i: (rows // chip_key_rows, 0))
            if rows % chip_key_rows == 0
            else pl.BlockSpec((pl.Element(chip_key_rows), pl.Element(value_width)), lambda i: (rows, 0)),
            pl.BlockSpec((pl.Element(key_rows), pl.Element(LANES)), lambda i: (rows, 0)),
            VMEM,
            VMEM,
        ],
        out_specs=(HBM, VMEM, VMEM),
        scratch_shapes=[
            pltpu.VMEM((2 * W, frames * BS, 2 * key_width), BF16),
            pltpu.VMEM((2 * W, 1, frames * BS), F32),
            pltpu.VMEM((max_halo, BS, frames * BS), F32),
            pltpu.VMEM((n_blocks + 1, BS, LANES), F32),
            pltpu.VMEM((n_blocks + 1, BS, LANES), F32),
            pltpu.VMEM((max_halo, BS, frames * BS), BF16),
            pltpu.SemaphoreType.DMA((max_halo,)),
        ],
        compiler_params=params(44),
        name="halo_scores",
    )(pairs, cat, self_term, chip_halo, link_halo[0], own_top, own_total)

    mine, other = [], []
    swap = [(i ^ 1, i) for i in range(n_tm)]
    for c in range(n_chunks):
        out_rows = pixels + (6 * n_blocks if c == 0 else 0)
        x = pl.pallas_call(
            functools.partial(chunk_sums, sizes, c),
            out_shape=struct((out_rows, LANES), BF16),
            grid=(1,),
            in_specs=[
                SMEM,
                HBM,
                pl.BlockSpec((n_blocks, BS, LANES), lambda i, c=c: (0, 0, c)),
                VMEM,
                VMEM,
                pl.BlockSpec((rows, LANES), lambda i, c=c: (0, c)),
                pl.BlockSpec((rows, LANES), lambda i: (0, 0)),
            ],
            out_specs=pl.BlockSpec((out_rows, LANES), lambda i: (0, 0)),
            scratch_shapes=[
                pltpu.VMEM((max_halo, BS, frames * BS), BF16),
                pltpu.VMEM((n_blocks + 1, BS, LANES), F32),
                pltpu.SemaphoreType.DMA((max_halo,)),
            ],
            compiler_params=params(32),
            name=f"chunk_sums_{c}",
        )(pairs, weights, acc, factor, stats, chip_halo, link_halo[c])
        mine.append(x)
        other.append(lax.ppermute(x, "tm", swap) if n_tm == 2 else lax.all_gather(x, "tm"))

    if n_tm == 2:
        out = pl.pallas_call(
            functools.partial(combine, sizes, n_chunks),
            out_shape=struct((pixels, value_width), BF16),
            in_specs=[VMEM] * (2 * n_chunks),
            out_specs=VMEM,
            compiler_params=params(32),
            name="combine",
        )(*mine, *other)
    else:
        packed = other[0][:, pixels:, :]
        tops, totals = zip(*[unpack_stats(packed[i], n_blocks) for i in range(n_tm)])
        tops = jnp.stack(tops).reshape(n_tm, pixels, 1)
        totals = jnp.stack(totals).reshape(n_tm, pixels, 1)
        factors = jnp.exp2(tops - jnp.max(tops, axis=0, keepdims=True))
        total = jnp.sum(totals * factors, axis=0)
        sums = [jnp.sum(x[:, :pixels, :].astype(F32) * factors, axis=0) / total for x in other]
        out = jnp.concatenate(sums, axis=1).astype(BF16)
    return out[None]


def solution(mesh):
    in_specs = (
        P(None, "space", None),
        P(None, "space", None),
        P("tm", "space", None),
        P("tm", "space"),
        P("tm", "space", None),
        P("space", None),
        P("space"),
    )
    out_specs = P(None, "space", None)
    body = functools.partial(shards, mesh.shape["space"], mesh.shape["tm"])
    return jax.shard_map(body, mesh=mesh, in_specs=in_specs, out_specs=out_specs, check_vma=False)
```

time: 228 us -> 75.9 us (0.33)
  the two profiles are of different devices: /device:TPU:25 before, /device:TPU:3 now
where the time goes in v1:
time: 75.9 us; the launch traced here: 76.3 us
  Pallas kernels  44.9 us (59%)
  starting transfers between devices  17 us (22%)
  local copies, waits for them, and re-layouts  9.22 us (12%)
  waiting for transfers between devices  5.02 us (7%)
    pallas_call x4, Pallas kernels, shards(): pl.pallas_call(functools.partial(chunk_sums, sizes, c), out_shape=struct(...  25.1 us
    ppermute x3, starting transfers between devices, shards(): link_halo.append(lax.ppermute(edge, 'space', over_link))  9.96 us
    unnamed x19, local copies, waits for them, and re-layouts  9.22 us
    pallas_call x1, Pallas kernels, shards(): pl.pallas_call(functools.partial(own_part, sizes), out_shape=(struct((n_b...  8.07 us
    pallas_call x1, Pallas kernels, shards(): pl.pallas_call(functools.partial(halo_scores, sizes), out_shape=(struct((...  6.57 us
    ppermute x4, waiting for transfers between devices, shards(): lax.ppermute(x, 'tm', swap)  5 us
    ppermute x4, starting transfers between devices, shards(): lax.ppermute(x, 'tm', swap)  3.19 us
    ppermute x1, starting transfers between devices, shards(): link_halo = [lax.ppermute(link_edge, 'space', over_link)]  3.08 us
  transfers between devices with their start and end apart: 9, of which 1 were waited for; matrix products, arithmetic and copies ran while one was open for 2% of the time, Pallas kernels for 54%

profile of v1, /device:TPU:3, one launch (start us, length us, event | category | flops | bytes accessed | tf_op | source)
XLA Modules:
  0.0 76.3 jit_solution(16815766334603547229)
XLA Ops:
  0.0 1.5 %copy.8.key_ref = bf16[4,1024,64]{2,1,0:T(8,128)(2,1)S(1)} copy(bf16[4,1024,64]{1,2,0:T(8,128)(2,1)} %param.9) | data formatting | bytes 1048576 | tf_op args[2]
  1.5 0.0 copy-start
  1.5 2.2 %copy-done = bf16[4,1024,512]{2,1,0:T(8,128)(2,1)S(1)} copy-done((bf16[4,1024,512]{2,1,0:T(8,128)(2,1)S(1)}, bf16[4,1024,512]{2,1,0:T(8,128)(2,1)}, u32[]{:S(2)}) %copy-start) | copy-done | bytes 4194328
  3.7 0.0 copy-start.3
  3.7 0.7 copy-done.3
  4.4 0.0 copy-start.5
  4.4 0.7 copy-done.5
  5.1 0.0 copy-start.6
  5.1 0.7 copy-done.6
  5.8 0.0 copy-start.1
  5.8 2.6 %lists_and_edges.1 = (s32[256]{0:T(256)S(1)}, bf16[1168,512]{1,0:T(8,128)(2,1)}, bf16[1552,128]{1,0:T(8,128)(2,1)}) custom-call(s32[8,6]{1,0:T(8,128)S(1)} %copy-done.5, s32[8]{0:T(128)S(1)} %copy-done.6, bf16[4,1024,64]{2,1,0:T(8,128)(2,1)S(1)} %copy.8.key_ref, bf16[4,1024]{1,0:T(4,128)(2,1)S(1)} %copy-done.3, bf16[4,1024,512]{2,1,0:T(8,128)(2,1)S(1)} %copy-done), custom_call_target="tpu_custom_call" | custom-call | tf_op jit(solution)/shard_map/lists_and_edges/pallas_call | solution.py:356
  8.3 0.0 copy-start.7
  8.3 0.7 collective-permute-start
  9.1 0.0 copy-start.4
  9.1 3.1 %collective-permute-start.1 = (bf16[1552,128]{1,0:T(8,128)(2,1)}, bf16[1552,128]{1,0:T(8,128)(2,1)S(1)}, u32[]{:S(2)}, u32[]{:S(2)}) collective-permute-start(bf16[1552,128]{1,0:T(8,128)(2,1)} %get-tuple-element.23), channel_id=1, source_target_pairs={{2,4},{4,2},{6,8},{8,6},{10,12},{12,10},{14,16},{16,14},{18,20},{2... | collective-permute-start | bytes 1191944 | tf_op jit(solution)/shard_map/ppermute | solution.py:387
  12.2 0.0 copy-done.1
  12.2 1.1 %edge_chunks.1 = (bf16[1024,128]{1,0:T(8,128)(2,1)}, bf16[1024,128]{1,0:T(8,128)(2,1)}, bf16[1024,128]{1,0:T(8,128)(2,1)}) custom-call(bf16[4,1024,512]{2,1,0:T(8,128)(2,1)S(1)} %copy-done.1), custom_call_target="tpu_custom_call" | custom-call | tf_op jit(solution)/shard_map/edge_chunks/pallas_call | solution.py:373
  13.3 3.5 %collective-permute-start.4 = (bf16[1024,128]{1,0:T(8,128)(2,1)}, bf16[1024,128]{1,0:T(8,128)(2,1)}, u32[]{:S(2)}, u32[]{:S(2)}) collective-permute-start(bf16[1024,128]{1,0:T(8,128)(2,1)} %get-tuple-element.32), channel_id=1, source_target_pairs={{2,4},{4,2},{6,8},{8,6},{10,12},{12,10},{14,16},{16,14},{18,20},{2... | collective-permute-start | bytes 786440 | tf_op jit(solution)/shard_map/ppermute | solution.py:390
  16.8 3.0 %collective-permute-start.3 = (bf16[1024,128]{1,0:T(8,128)(2,1)}, bf16[1024,128]{1,0:T(8,128)(2,1)}, u32[]{:S(2)}, u32[]{:S(2)}) collective-permute-start(bf16[1024,128]{1,0:T(8,128)(2,1)} %get-tuple-element.31), channel_id=1, source_target_pairs={{2,4},{4,2},{6,8},{8,6},{10,12},{12,10},{14,16},{16,14},{18,20},{2... | collective-permute-start | bytes 786440 | tf_op jit(solution)/shard_map/ppermute | solution.py:390
  19.8 3.5 %collective-permute-start.2 = (bf16[1024,128]{1,0:T(8,128)(2,1)}, bf16[1024,128]{1,0:T(8,128)(2,1)S(1)}, u32[]{:S(2)}, u32[]{:S(2)}) collective-permute-start(bf16[1024,128]{1,0:T(8,128)(2,1)} %get-tuple-element.30), channel_id=1, source_target_pairs={{2,4},{4,2},{6,8},{8,6},{10,12},{12,10},{14,16},{16,14},{18,20},{2... | collective-permute-start | bytes 786440 | tf_op jit(solution)/shard_map/ppermute | solution.py:390
  23.3 0.0 copy-done.7
  23.3 0.2 copy.9
  23.5 1.1 %copy.10 = bf16[1,1024,64]{2,1,0:T(8,128)(2,1)S(1)} copy(bf16[1,1024,64]{1,2,0:T(8,128)(2,1)} %param.8) | data formatting | bytes 262144 | tf_op args[1]
  24.6 0.0 copy-done.4
  24.6 0.0 copy-start.2
  24.6 2.2 %copy-done.2 = bf16[4,1024,512]{2,1,0:T(8,128)(2,1)S(1)} copy-done((bf16[4,1024,512]{2,1,0:T(8,128)(2,1)S(1)}, bf16[4,1024,512]{2,1,0:T(8,128)(2,1)}, u32[]{:S(2)}) %copy-start.2) | copy-done | bytes 4194328
  26.8 8.1 %own_part.1 = (f32[9,128,512]{2,1,0:T(8,128)S(1)}, f32[9,128,128]{2,1,0:T(8,128)S(1)}, f32[9,128,128]{2,1,0:T(8,128)S(1)}, bf16[9,128,128]{2,1,0:T(8,128)(2,1)S(1)}, f32[9,128,128]{2,1,0:T(8,128)S(1)}) custom-call(s32[256]{0:T(256)S(1)} %get-tuple-element.19.pairs_ref, bf16[1024,64]{1,0:T(8,128)(2,1)S(1)} %bitcast.3, bf16[1024,64]{1,0:T(8,128)(2,1)S(1)} %bitcast.4, ...), custom_call_target="tpu_custom_call" | custom-call | tf_op jit(solution)/shard_map/own_part/pallas_call | solution.py:392
  34.9 0.0 collective-permute-done.1.link_ref
  34.9 0.0 collective-permute-done.chip_ref
  34.9 6.6 %halo_scores.1 = (bf16[34,128,512]{2,1,0:T(8,128)(2,1)S(1)}, f32[9,128,128]{2,1,0:T(8,128)S(1)}, f32[16,128]{1,0:T(8,128)S(1)}) custom-call(s32[256]{0:T(256)S(1)} %get-tuple-element.19.pairs_ref, bf16[9,128,128]{2,1,0:T(8,128)(2,1)S(1)} %get-tuple-element.20.cat_ref, f32[9,128,128]{2,1,0:T(8,128)S(1)} %get-tuple-element.21.self_ref, ...), custom_call_target="tpu_custom_call" | custom-call | tf_op jit(solution)/shard_map/halo_scores/pallas_call | solution.py:414
  41.5 6.0 %chunk_sums_0.1.refs_0_ = bf16[1072,128]{1,0:T(8,128)(2,1)S(1)} custom-call(s32[256]{0:T(256)S(1)} %get-tuple-element.19.pairs_ref, bf16[34,128,512]{2,1,0:T(8,128)(2,1)S(1)} %get-tuple-element.26.weight_ref, f32[9,128,512]{2,1,0:T(8,128)S(1)} %get-tuple-element.27.acc_ref, f32[9,128,128]{2,1,0:T(8,128)S(1)} %get-tuple-element.28.factor_ref, ...), custom_call_target="tpu_custom_call" | custom-call | tf_op jit(solution)/shard_map/chunk_sums_0/pallas_call | solution.py:451
  47.5 1.3 %collective-permute-start.5 = (bf16[1072,128]{1,0:T(8,128)(2,1)S(1)}, bf16[1072,128]{1,0:T(8,128)(2,1)S(1)}, u32[]{:S(2)}, u32[]{:S(2)}) collective-permute-start(bf16[1072,128]{1,0:T(8,128)(2,1)S(1)} %chunk_sums_0.1.refs_0_), channel_id=1, source_target_pairs={{1,0},{0,1},{3,2},{2,3},{5,4},{4,5},{7,6},{6,7},{9,8},{8,9},{11,10... | collective-permute-start | bytes 823304 | tf_op jit(solution)/shard_map/ppermute | solution.py:474
  48.8 0.0 collective-permute-done.4.link_ref
  48.8 6.5 %chunk_sums_3.1.refs_3_ = bf16[1024,128]{1,0:T(8,128)(2,1)S(1)} custom-call(s32[256]{0:T(256)S(1)} %get-tuple-element.19.pairs_ref, bf16[34,128,512]{2,1,0:T(8,128)(2,1)S(1)} %get-tuple-element.26.weight_ref, f32[9,128,512]{2,1,0:T(8,128)S(1)} %get-tuple-element.27.acc_ref, f32[9,128,128]{2,1,0:T(8,128)S(1)} %get-tuple-element.28.factor_ref, ...), custom_call_target="tpu_custom_call" | custom-call | tf_op jit(solution)/shard_map/chunk_sums_3/pallas_call | solution.py:451
  55.3 0.3 collective-permute-start.8
  55.6 0.0 collective-permute-done.3.link_ref
  55.6 6.5 %chunk_sums_2.1.refs_2_ = bf16[1024,128]{1,0:T(8,128)(2,1)S(1)} custom-call(s32[256]{0:T(256)S(1)} %get-tuple-element.19.pairs_ref, bf16[34,128,512]{2,1,0:T(8,128)(2,1)S(1)} %get-tuple-element.26.weight_ref, f32[9,128,512]{2,1,0:T(8,128)S(1)} %get-tuple-element.27.acc_ref, f32[9,128,128]{2,1,0:T(8,128)S(1)} %get-tuple-element.28.factor_ref, ...), custom_call_target="tpu_custom_call" | custom-call | tf_op jit(solution)/shard_map/chunk_sums_2/pallas_call | solution.py:451
  62.2 1.3 %collective-permute-start.7 = (bf16[1024,128]{1,0:T(8,128)(2,1)S(1)}, bf16[1024,128]{1,0:T(8,128)(2,1)S(1)}, u32[]{:S(2)}, u32[]{:S(2)}) collective-permute-start(bf16[1024,128]{1,0:T(8,128)(2,1)S(1)} %chunk_sums_2.1.refs_2_), channel_id=1, source_target_pairs={{1,0},{0,1},{3,2},{2,3},{5,4},{4,5},{7,6},{6,7},{9,8},{8,9},{11,10... | collective-permute-start | bytes 786440 | tf_op jit(solution)/shard_map/ppermute | solution.py:474
  63.5 0.0 collective-permute-done.2.link_ref
  63.5 6.1 %chunk_sums_1.1.refs_1_ = bf16[1024,128]{1,0:T(8,128)(2,1)S(1)} custom-call(s32[256]{0:T(256)S(1)} %get-tuple-element.19.pairs_ref, bf16[34,128,512]{2,1,0:T(8,128)(2,1)S(1)} %get-tuple-element.26.weight_ref, f32[9,128,512]{2,1,0:T(8,128)S(1)} %get-tuple-element.27.acc_ref, f32[9,128,128]{2,1,0:T(8,128)S(1)} %get-tuple-element.28.factor_ref, ...), custom_call_target="tpu_custom_call" | custom-call | tf_op jit(solution)/shard_map/chunk_sums_1/pallas_call | solution.py:451
  69.6 0.3 collective-permute-start.6
  69.8 0.0 collective-permute-done.8.refs_7_
  69.8 0.0 collective-permute-done.7.refs_6_
  69.9 5.0 %collective-permute-done.6.refs_5_ = bf16[1024,128]{1,0:T(8,128)(2,1)S(1)} collective-permute-done((bf16[1024,128]{1,0:T(8,128)(2,1)S(1)}, bf16[1024,128]{1,0:T(8,128)(2,1)S(1)}, u32[]{:S(2)}, u32[]{:S(2)}) %collective-permute-start.6) | collective-permute-done | bytes 262176 | tf_op jit(solution)/shard_map/ppermute | solution.py:474
  74.8 0.0 collective-permute-done.5.refs_4_
  74.9 1.5 %combine.1 = bf16[1024,512]{1,0:T(8,128)(2,1)} custom-call(bf16[1072,128]{1,0:T(8,128)(2,1)S(1)} %chunk_sums_0.1.refs_0_, bf16[1024,128]{1,0:T(8,128)(2,1)S(1)} %chunk_sums_1.1.refs_1_, bf16[1024,128]{1,0:T(8,128)(2,1)S(1)} %chunk_sums_2.1.refs_2_, bf16[1024,128]{1,0:T(8,128)(2,1)S(1)} %chunk_sums_3.1.refs_3_, ...), custom_call_target="tpu_custom_call" | custom-call | tf_op jit(solution)/shard_map/combine/pallas_call | solution.py:477
Async XLA Ops:
  1.5 2.2 %copy-start = (bf16[4,1024,512]{2,1,0:T(8,128)(2,1)S(1)}, bf16[4,1024,512]{2,1,0:T(8,128)(2,1)}, u32[]{:S(2)}) copy-start(bf16[4,1024,512]{2,1,0:T(8,128)(2,1)} %value_ref.5) | copy-start | bytes 12582916
  3.7 0.7 copy-start.3
  4.4 0.7 copy-start.5
  5.1 0.7 copy-start.6
  5.8 6.4 %copy-start.1 = (bf16[4,1024,512]{2,1,0:T(8,128)(2,1)S(1)}, bf16[4,1024,512]{2,1,0:T(8,128)(2,1)}, u32[]{:S(2)}) copy-start(bf16[4,1024,512]{2,1,0:T(8,128)(2,1)} %value_ref.5) | copy-start | bytes 12582916
  8.3 15.0 %copy-start.7 = (bf16[1,1024,64]{1,2,0:T(8,128)(2,1)S(1)}, bf16[1,1024,64]{1,2,0:T(8,128)(2,1)}, u32[]{:S(2)}) copy-start(bf16[1,1024,64]{1,2,0:T(8,128)(2,1)} %param.7) | copy-start | bytes 393220
  8.3 26.6 %collective-permute-start = (bf16[1168,512]{1,0:T(8,128)(2,1)}, bf16[1168,512]{1,0:T(8,128)(2,1)S(1)}, u32[]{:S(2)}, u32[]{:S(2)}) collective-permute-start(bf16[1168,512]{1,0:T(8,128)(2,1)} %get-tuple-element.22), channel_id=1, source_target_pairs={{2,0},{0,2},{6,4},{4,6},{10,8},{8,10},{14,12},{12,14},{18,16},{16,... | collective-permute-start | bytes 3588104 | tf_op jit(solution)/shard_map/ppermute | solution.py:388
  9.1 15.5 %copy-start.4 = (bf16[4,1024]{1,0:T(4,128)(2,1)S(1)}, bf16[4,1024]{1,0:T(4,128)(2,1)}, u32[]{:S(2)}) copy-start(bf16[4,1024]{1,0:T(4,128)(2,1)} %shrink_ref.3) | copy-start | bytes 24580
  9.1 25.8 %collective-permute-start.1 = (bf16[1552,128]{1,0:T(8,128)(2,1)}, bf16[1552,128]{1,0:T(8,128)(2,1)S(1)}, u32[]{:S(2)}, u32[]{:S(2)}) collective-permute-start(bf16[1552,128]{1,0:T(8,128)(2,1)} %get-tuple-element.23), channel_id=1, source_target_pairs={{2,4},{4,2},{6,8},{8,6},{10,12},{12,10},{14,16},{16,14},{18,20},{2... | collective-permute-start | bytes 1191944 | tf_op jit(solution)/shard_map/ppermute | solution.py:387
  13.3 35.5 %collective-permute-start.4 = (bf16[1024,128]{1,0:T(8,128)(2,1)}, bf16[1024,128]{1,0:T(8,128)(2,1)}, u32[]{:S(2)}, u32[]{:S(2)}) collective-permute-start(bf16[1024,128]{1,0:T(8,128)(2,1)} %get-tuple-element.32), channel_id=1, source_target_pairs={{2,4},{4,2},{6,8},{8,6},{10,12},{12,10},{14,16},{16,14},{18,20},{2... | collective-permute-start | bytes 786440 | tf_op jit(solution)/shard_map/ppermute | solution.py:390
  16.8 38.8 %collective-permute-start.3 = (bf16[1024,128]{1,0:T(8,128)(2,1)}, bf16[1024,128]{1,0:T(8,128)(2,1)}, u32[]{:S(2)}, u32[]{:S(2)}) collective-permute-start(bf16[1024,128]{1,0:T(8,128)(2,1)} %get-tuple-element.31), channel_id=1, source_target_pairs={{2,4},{4,2},{6,8},{8,6},{10,12},{12,10},{14,16},{16,14},{18,20},{2... | collective-permute-start | bytes 786440 | tf_op jit(solution)/shard_map/ppermute | solution.py:390
  19.8 43.7 %collective-permute-start.2 = (bf16[1024,128]{1,0:T(8,128)(2,1)}, bf16[1024,128]{1,0:T(8,128)(2,1)S(1)}, u32[]{:S(2)}, u32[]{:S(2)}) collective-permute-start(bf16[1024,128]{1,0:T(8,128)(2,1)} %get-tuple-element.30), channel_id=1, source_target_pairs={{2,4},{4,2},{6,8},{8,6},{10,12},{12,10},{14,16},{16,14},{18,20},{2... | collective-permute-start | bytes 786440 | tf_op jit(solution)/shard_map/ppermute | solution.py:390
  24.6 2.2 %copy-start.2 = (bf16[4,1024,512]{2,1,0:T(8,128)(2,1)S(1)}, bf16[4,1024,512]{2,1,0:T(8,128)(2,1)}, u32[]{:S(2)}) copy-start(bf16[4,1024,512]{2,1,0:T(8,128)(2,1)} %value_ref.5) | copy-start | bytes 12582916
  47.5 27.3 %collective-permute-start.5 = (bf16[1072,128]{1,0:T(8,128)(2,1)S(1)}, bf16[1072,128]{1,0:T(8,128)(2,1)S(1)}, u32[]{:S(2)}, u32[]{:S(2)}) collective-permute-start(bf16[1072,128]{1,0:T(8,128)(2,1)S(1)} %chunk_sums_0.1.refs_0_), channel_id=1, source_target_pairs={{1,0},{0,1},{3,2},{2,3},{5,4},{4,5},{7,6},{6,7},{9,8},{8,9},{11,10... | collective-permute-start | bytes 823304 | tf_op jit(solution)/shard_map/ppermute | solution.py:474
  55.3 14.5 %collective-permute-start.8 = (bf16[1024,128]{1,0:T(8,128)(2,1)S(1)}, bf16[1024,128]{1,0:T(8,128)(2,1)S(1)}, u32[]{:S(2)}, u32[]{:S(2)}) collective-permute-start(bf16[1024,128]{1,0:T(8,128)(2,1)S(1)} %chunk_sums_3.1.refs_3_), channel_id=1, source_target_pairs={{1,0},{0,1},{3,2},{2,3},{5,4},{4,5},{7,6},{6,7},{9,8},{8,9},{11,10... | collective-permute-start | bytes 786440 | tf_op jit(solution)/shard_map/ppermute | solution.py:474
  62.2 7.7 %collective-permute-start.7 = (bf16[1024,128]{1,0:T(8,128)(2,1)S(1)}, bf16[1024,128]{1,0:T(8,128)(2,1)S(1)}, u32[]{:S(2)}, u32[]{:S(2)}) collective-permute-start(bf16[1024,128]{1,0:T(8,128)(2,1)S(1)} %chunk_sums_2.1.refs_2_), channel_id=1, source_target_pairs={{1,0},{0,1},{3,2},{2,3},{5,4},{4,5},{7,6},{6,7},{9,8},{8,9},{11,10... | collective-permute-start | bytes 786440 | tf_op jit(solution)/shard_map/ppermute | solution.py:474
  69.6 5.3 %collective-permute-start.6 = (bf16[1024,128]{1,0:T(8,128)(2,1)S(1)}, bf16[1024,128]{1,0:T(8,128)(2,1)S(1)}, u32[]{:S(2)}, u32[]{:S(2)}) collective-permute-start(bf16[1024,128]{1,0:T(8,128)(2,1)S(1)} %chunk_sums_1.1.refs_1_), channel_id=1, source_target_pairs={{1,0},{0,1},{3,2},{2,3},{5,4},{4,5},{7,6},{6,7},{9,8},{8,9},{11,10... | collective-permute-start | bytes 786440 | tf_op jit(solution)/shard_map/ppermute | solution.py:474

commit v2 on v1

v2 whole, which is shorter than its diff:
```python
import functools
import math

import jax
import jax.numpy as jnp
from jax import lax
from jax.experimental import pallas as pl
from jax.experimental.pallas import tpu as pltpu
from jax.sharding import PartitionSpec as P

BS = 128
W = 2
LANES = 128
EDGE = W * BS
NONE = -1e30
OWN_AT, HALO_AT, COUNT_AT = 0, 64, 128
F32, BF16 = jnp.float32, jnp.bfloat16

VMEM = pl.BlockSpec(memory_space=pltpu.VMEM)
SMEM = pl.BlockSpec(memory_space=pltpu.SMEM)
HBM = pl.BlockSpec(memory_space=pltpu.HBM)


def params(mib):
    return pltpu.CompilerParams(vmem_limit_bytes=mib * 1024 * 1024)


def row_to_lanes(row):
    return jnp.transpose(jnp.broadcast_to(row, (row.shape[1], row.shape[1])))


def lane_tiles(x):
    return [x[:, i * LANES : (i + 1) * LANES] for i in range(x.shape[1] // LANES)]


def wide(x, times):
    return jnp.concatenate([x] * times, axis=1)


def run_all(copies):
    for copy in copies:
        copy.start()
    for copy in copies:
        copy.wait()


def value_copies(sizes, value_ref, out, start, lanes, sems):
    frames = sizes[0]
    return [
        pltpu.make_async_copy(
            value_ref.at[f, pl.ds(start + e * BS, BS), lanes],
            out.at[pl.ds((e * frames + f) * BS, BS), :],
            sems.at[e * frames + f],
        )
        for e in range(W)
        for f in range(frames)
    ]


def edge_start(pixels, over_link):
    odd = lax.rem(lax.axis_index("space"), 2)
    side = odd if over_link else 1 - odd
    return pl.multiple_of(side * (pixels - EDGE), EDGE)


def shrink_rows(sizes, shrink, start):
    frames = sizes[0]
    edge = shrink[:, pl.ds(start, EDGE)].astype(F32)
    rows = [edge[:, e * BS : (e + 1) * BS] for e in range(W)]
    pad = jnp.zeros((16 - W * frames, LANES), F32)
    return jnp.concatenate(rows + [pad], axis=0).astype(BF16)


def lists_and_edge(
    sizes, list_ref, count_ref, key_ref, shrink_ref, value_ref, pairs_ref, link_ref,
    list_sc, count_sc, shrink_sc, sems, key_sems, small_sems,
):
    frames, pixels, n_blocks, n_listed, key_width, value_width = sizes
    start = edge_start(pixels, True)
    small = [
        pltpu.make_async_copy(list_ref, list_sc, small_sems.at[0]),
        pltpu.make_async_copy(count_ref, count_sc, small_sems.at[1]),
        pltpu.make_async_copy(shrink_ref, shrink_sc, small_sems.at[2]),
    ]
    for copy in small:
        copy.start()
    copies = value_copies(sizes, value_ref, link_ref, start, pl.ds(0, LANES), sems)
    at = frames * EDGE
    for e in range(W):
        for f in range(frames):
            copies.append(
                pltpu.make_async_copy(
                    key_ref.at[f, :, pl.ds(start + e * BS, BS)],
                    link_ref.at[pl.ds(at, key_width), :],
                    key_sems.at[e * frames + f],
                )
            )
            at += key_width
    for copy in copies:
        copy.start()
    for copy in small:
        copy.wait()
    link_ref[at : at + 16, :] = shrink_rows(sizes, shrink_sc, start)
    odd = lax.rem(lax.axis_index("space"), 2)

    def block(b, carry):
        live = count_sc[b]
        for j in range(n_listed):
            n_own, n_halo = carry
            l = list_sc[b, j]
            ok = j < live
            inside = (l >= W) & (l < W + n_blocks)
            right = jnp.where(l >= W + n_blocks, 1, 0)
            e = jnp.where(right == 1, l - (W + n_blocks), l)
            over_link = jnp.where(right == odd, 1, 0)
            pairs_ref[OWN_AT + n_own] = b * n_blocks + jnp.clip(l - W, 0, n_blocks - 1)
            pairs_ref[HALO_AT + n_halo] = b * 4 + over_link * W + jnp.clip(e, 0, W - 1)
            carry = (
                n_own + jnp.where(ok & inside, 1, 0),
                n_halo + jnp.where(ok & jnp.logical_not(inside), 1, 0),
            )
        return carry

    n_own, n_halo = lax.fori_loop(0, n_blocks, block, (0, 0))
    pairs_ref[OWN_AT + n_own] = n_blocks * n_blocks
    pairs_ref[HALO_AT + n_halo] = n_blocks * 4
    pairs_ref[COUNT_AT] = n_own
    pairs_ref[COUNT_AT + 1] = n_halo
    for copy in copies:
        copy.wait()


def chip_edge_and_chunk(
    sizes, query_ref, select_ref, key_ref, shrink_ref, value_ref, after_ref,
    chip_ref, link_ref, query_out, select_out, key_out, shrink_out,
    sems, key_sems, small_sems,
):
    frames, pixels, n_blocks, n_listed, key_width, value_width = sizes
    start = edge_start(pixels, False)
    small = pltpu.make_async_copy(shrink_ref, shrink_out, small_sems.at[0])
    small.start()
    copies = value_copies(sizes, value_ref, chip_ref, start, slice(None), sems.at[0])
    at = frames * EDGE
    for e in range(W):
        for f in range(frames):
            copies.append(
                pltpu.make_async_copy(
                    key_ref.at[f, :, pl.ds(start + e * BS, BS)],
                    chip_ref.at[pl.ds(at, key_width), pl.ds(f * BS, BS)],
                    key_sems.at[e * frames + f],
                )
            )
        at += key_width
    copies += value_copies(sizes, value_ref, link_ref, edge_start(pixels, True), pl.ds(LANES, LANES), sems.at[1])
    copies += [
        pltpu.make_async_copy(query_ref, query_out, small_sems.at[1]),
        pltpu.make_async_copy(select_ref, select_out, small_sems.at[2]),
        pltpu.make_async_copy(key_ref, key_out, small_sems.at[3]),
    ]
    for copy in copies:
        copy.start()
    small.wait()
    chip_ref[at : at + 16, :LANES] = shrink_rows(sizes, shrink_out, start)
    for copy in copies:
        copy.wait()


def link_chunks(sizes, first, value_ref, after_ref, *refs):
    outs, sems = refs[:-1], refs[-1]
    start = edge_start(sizes[1], True)
    copies = []
    for i, out in enumerate(outs):
        copies += value_copies(sizes, value_ref, out, start, pl.ds((first + i) * LANES, LANES), sems.at[i])
    run_all(copies)


def paired(count, body):
    def step(i, carry):
        body(2 * i)
        body(2 * i + 1)
        return carry

    lax.fori_loop(0, (count + 1) // 2, step, 0)


def squares_over(k):
    k_f = k.astype(F32)
    return jnp.concatenate([(k_f * k_f).astype(BF16), k], axis=0)


def own_part(
    sizes, pairs_ref, query_ref, select_ref, key_ref, shrink_ref, value_ref,
    weight_ref, rest_ref, acc_ref, top_ref, total_ref, cat_ref, self_ref,
    keys_sc, shr_sc, score_sc, value_sc, sems,
):
    frames, pixels, n_blocks, n_listed, key_width, value_width = sizes
    cols = frames * BS
    half = value_width // 2
    bits = int(math.log2(n_blocks))
    values = [
        pltpu.make_async_copy(value_ref.at[:, :, pl.ds(0, half)], value_sc, sems.at[0]),
        pltpu.make_async_copy(value_ref.at[:, :, pl.ds(half, half)], rest_ref, sems.at[1]),
    ]
    for copy in values:
        copy.start()
    scale = -math.log2(math.e) / math.sqrt(key_width)
    for b in range(n_blocks):
        block = slice(b * BS, (b + 1) * BS)
        q = query_ref[:, block].astype(F32)
        s = select_ref[:, block].astype(F32)
        both = jnp.concatenate([s, -2.0 * q * s], axis=0)
        cat_ref[b] = jnp.transpose(both).astype(BF16)
        self_ref[b] = row_to_lanes(jnp.sum(s * q * q, axis=0, keepdims=True))
    cat_ref[n_blocks] = jnp.zeros((BS, 2 * key_width), BF16)
    self_ref[n_blocks] = jnp.zeros((BS, LANES), F32)
    shrink = shrink_ref[...].astype(F32) * scale
    for l in range(n_blocks):
        for f in range(frames):
            block = slice(l * BS, (l + 1) * BS)
            keys_sc[l, :, f * BS : (f + 1) * BS] = squares_over(key_ref[f, :, block])
            shr_sc[l, :, f * BS : (f + 1) * BS] = shrink[f : f + 1, block]
    top_ref[...] = jnp.full_like(top_ref, NONE)
    total_ref[...] = jnp.zeros_like(total_ref)
    acc_ref[...] = jnp.zeros_like(acc_ref)
    count = pairs_ref[COUNT_AT]

    def score(p):
        code = pairs_ref[OWN_AT + p]
        b, l = code >> bits, code & (n_blocks - 1)
        s = jnp.dot(cat_ref[b], keys_sc[l], preferred_element_type=F32)
        s = (s + wide(self_ref[b], frames)) * shr_sc[l]
        score_sc[p] = s
        top_ref[b] = functools.reduce(jnp.maximum, lane_tiles(s), top_ref[b])

    paired(count, score)
    for b in range(n_blocks):
        top_ref[b] = jnp.broadcast_to(jnp.max(top_ref[b], axis=1, keepdims=True), (BS, LANES))
    values[0].wait()

    def read(p):
        code = pairs_ref[OWN_AT + p]
        b, l = code >> bits, code & (n_blocks - 1)
        w = jnp.exp2(score_sc[p] - wide(top_ref[b], frames))
        total_ref[b] = functools.reduce(jnp.add, lane_tiles(w), total_ref[b])
        w = w.astype(BF16)
        weight_ref[p] = w
        v = value_sc[:, pl.ds(pl.multiple_of(l * BS, BS), BS), :].reshape(cols, half)
        acc_ref[b] += jnp.dot(w, v, preferred_element_type=F32)

    paired(count, read)
    values[1].wait()


def own_rest(sizes, pairs_ref, weight_ref, value_ref, after_ref, acc_ref):
    frames, pixels, n_blocks = sizes[:3]
    bits = int(math.log2(n_blocks))
    acc_ref[...] = jnp.zeros_like(acc_ref)

    def read(p):
        code = pairs_ref[OWN_AT + p]
        b, l = code >> bits, code & (n_blocks - 1)
        v = value_ref[:, pl.ds(pl.multiple_of(l * BS, BS), BS), :].reshape(frames * BS, value_ref.shape[2])
        acc_ref[b] += jnp.dot(weight_ref[p], v, preferred_element_type=F32)

    paired(pairs_ref[COUNT_AT], read)


def halo_scores(
    sizes, pairs_ref, cat_ref, self_ref, chip_ref, link_ref, own_top_ref, own_total_ref,
    weight_ref, factor_ref, stats_ref,
    keys_sc, shr_sc, score_sc, top_sc, total_sc,
):
    frames, pixels, n_blocks, n_listed, key_width, value_width = sizes
    rows = frames * EDGE
    scale = -math.log2(math.e) / math.sqrt(key_width)
    for e in range(W):
        at = rows + e * key_width
        keys_sc[e] = squares_over(chip_ref[at : at + key_width, :])
        for f in range(frames):
            at = rows + (e * frames + f) * key_width
            keys_sc[W + e, :, f * BS : (f + 1) * BS] = squares_over(link_ref[at : at + key_width, :])
    shrinks = [
        chip_ref[rows + W * key_width :, :LANES].astype(F32) * scale,
        link_ref[rows + W * frames * key_width :, :].astype(F32) * scale,
    ]
    for side in range(2):
        for e in range(W):
            for f in range(frames):
                at = e * frames + f
                shr_sc[side * W + e, :, f * BS : (f + 1) * BS] = shrinks[side][at : at + 1, :]
    top_sc[...] = jnp.full_like(top_sc, NONE)
    total_sc[...] = jnp.zeros_like(total_sc)
    count = pairs_ref[COUNT_AT + 1]

    def score(p):
        code = pairs_ref[HALO_AT + p]
        b, h = code >> 2, code & 3
        s = jnp.dot(cat_ref[b], keys_sc[h], preferred_element_type=F32)
        s = (s + wide(self_ref[b], frames)) * shr_sc[h]
        score_sc[p] = s
        top_sc[b] = functools.reduce(jnp.maximum, lane_tiles(s), top_sc[b])

    paired(count, score)
    for b in range(n_blocks):
        own = own_top_ref[b]
        top = jnp.maximum(own, jnp.broadcast_to(jnp.max(top_sc[b], axis=1, keepdims=True), (BS, LANES)))
        top_sc[b] = top
        factor_ref[b] = jnp.exp2(own - top)

    def weigh(p):
        code = pairs_ref[HALO_AT + p]
        b = code >> 2
        w = jnp.exp2(score_sc[p] - wide(top_sc[b], frames))
        total_sc[b] = functools.reduce(jnp.add, lane_tiles(w), total_sc[b])
        weight_ref[p] = w.astype(BF16)

    paired(count, weigh)
    for b in range(n_blocks):
        total = jnp.sum(total_sc[b] + own_total_ref[b] * factor_ref[b], axis=1, keepdims=True)
        stats_ref[b : b + 1, :] = jnp.transpose(top_sc[b])[:1, :]
        stats_ref[n_blocks + b : n_blocks + b + 1, :] = jnp.transpose(jnp.broadcast_to(total, (BS, LANES)))[:1, :]


def chunk_sums(sizes, c, pairs_ref, weight_ref, acc_ref, factor_ref, stats_ref, chip_ref, link_ref, out_ref, sum_sc):
    frames, pixels, n_blocks, n_listed, key_width, value_width = sizes
    cols = frames * BS
    per_half = acc_ref.shape[2] // LANES
    half_lanes = slice((c % per_half) * LANES, (c % per_half + 1) * LANES)
    for b in range(n_blocks):
        sum_sc[b] = acc_ref[b, :, half_lanes] * factor_ref[b]
    sum_sc[n_blocks] = jnp.zeros((BS, LANES), F32)

    def add(p):
        code = pairs_ref[HALO_AT + p]
        b, h = code >> 2, code & 3
        at = pl.multiple_of((h & (W - 1)) * cols, cols)
        chip = chip_ref[pl.ds(at, cols), c * LANES : (c + 1) * LANES]
        v = jnp.where(h >= W, link_ref[pl.ds(at, cols), :], chip)
        sum_sc[b] += jnp.dot(weight_ref[p], v, preferred_element_type=F32)

    paired(pairs_ref[COUNT_AT + 1], add)
    for b in range(n_blocks):
        out_ref[b * BS : (b + 1) * BS, :] = sum_sc[b].astype(BF16)
    if c == 0:
        rest = stats_ref[...]
        for i in range(3):
            piece = rest.astype(BF16)
            rest = rest - piece.astype(F32)
            out_ref[pixels + i * 2 * n_blocks : pixels + (i + 1) * 2 * n_blocks, :] = piece


def unpack_stats(x, n_blocks):
    n = 2 * n_blocks
    x = x.astype(F32)
    x = (x[:n] + x[n : 2 * n]) + x[2 * n :]
    return x[:n_blocks], x[n_blocks:]


def combine(sizes, n_chunks, *refs):
    frames, pixels, n_blocks = sizes[:3]
    mine, other, out_ref = refs[:n_chunks], refs[n_chunks : 2 * n_chunks], refs[-1]

    def run(first, second):
        top_a, total_a = unpack_stats(first[0][pixels:, :], n_blocks)
        top_b, total_b = unpack_stats(second[0][pixels:, :], n_blocks)
        top = jnp.maximum(top_a, top_b)
        a, b = jnp.exp2(top_a - top), jnp.exp2(top_b - top)
        total = total_a * a + total_b * b
        a, b = a / total, b / total
        for i in range(n_blocks):
            col_a = row_to_lanes(a[i : i + 1, :])
            col_b = row_to_lanes(b[i : i + 1, :])
            r = slice(i * BS, (i + 1) * BS)
            for c in range(n_chunks):
                x = first[c][r, :].astype(F32) * col_a + second[c][r, :].astype(F32) * col_b
                out_ref[r, c * LANES : (c + 1) * LANES] = x.astype(BF16)

    me = lax.axis_index("tm")

    @pl.when(me == 0)
    def _():
        run(mine, other)

    @pl.when(me != 0)
    def _():
        run(other, mine)


def shards(n_space, n_tm, query_key, selection, memory_key, shrinkage, memory_value, block_list, block_count):
    frames, pixels, key_width = memory_key.shape
    value_width = memory_value.shape[2]
    n_blocks, n_listed = block_list.shape
    sizes = (frames, pixels, n_blocks, n_listed, key_width, value_width)
    n_chunks = value_width // LANES
    half = value_width // 2
    cols = frames * BS
    rows = frames * EDGE
    link_rows = rows + W * frames * key_width + 16
    chip_rows = rows + W * key_width + 16
    max_halo = n_blocks * min(n_listed, 2 * W) + 2
    max_own = n_blocks * n_listed + 2
    struct = jax.ShapeDtypeStruct
    dma = pltpu.SemaphoreType.DMA
    query, select = jnp.swapaxes(query_key[0], 0, 1), jnp.swapaxes(selection[0], 0, 1)
    keys = jnp.swapaxes(memory_key, 1, 2)
    query, select, keys, shrinkage, memory_value, block_list, block_count = [
        pltpu.with_memory_space_constraint(x, pltpu.HBM)
        for x in (query, select, keys, shrinkage, memory_value, block_list, block_count)
    ]
    on_chip = [(i ^ 1, i) for i in range(n_space)]
    over_link = []
    for i in range(1, n_space - 1, 2):
        over_link += [(i, i + 1), (i + 1, i)]
    swap = [(i ^ 1, i) for i in range(n_tm)]

    pairs, link_edge = pl.pallas_call(
        functools.partial(lists_and_edge, sizes),
        out_shape=(struct((256,), jnp.int32), struct((link_rows, LANES), BF16)),
        in_specs=[HBM] * 5,
        out_specs=(SMEM, VMEM),
        scratch_shapes=[
            pltpu.SMEM(block_list.shape, jnp.int32),
            pltpu.SMEM(block_count.shape, jnp.int32),
            pltpu.VMEM(shrinkage.shape, BF16),
            dma((W * frames,)),
            dma((W * frames,)),
            dma((3,)),
        ],
        compiler_params=params(1),
        name="lists_and_edge",
    )(block_list, block_count, keys, shrinkage, memory_value)
    link_halo = [lax.ppermute(link_edge, "space", over_link)]
    chip_edge, link_edge, query, select, near_keys, near_shrink = pl.pallas_call(
        functools.partial(chip_edge_and_chunk, sizes),
        out_shape=(
            struct((chip_rows, value_width), BF16),
            struct((rows, LANES), BF16),
            struct(query.shape, BF16),
            struct(select.shape, BF16),
            struct(keys.shape, BF16),
            struct(shrinkage.shape, BF16),
        ),
        in_specs=[HBM] * 5 + [VMEM],
        out_specs=(VMEM,) * 6,
        scratch_shapes=[dma((2, W * frames)), dma((W * frames,)), dma((4,))],
        compiler_params=params(1),
        name="chip_edge_and_chunk",
    )(query, select, keys, shrinkage, memory_value, link_edge)
    chip_halo = lax.ppermute(chip_edge, "space", on_chip)
    link_halo.append(lax.ppermute(link_edge, "space", over_link))

    own_weights, rest, acc, own_top, own_total, cat, self_term = pl.pallas_call(
        functools.partial(own_part, sizes),
        out_shape=(
            struct((max_own, BS, cols), BF16),
            struct((frames, pixels, value_width - half), BF16),
            struct((n_blocks + 1, BS, half), F32),
            struct((n_blocks + 1, BS, LANES), F32),
            struct((n_blocks + 1, BS, LANES), F32),
            struct((n_blocks + 1, BS, 2 * key_width), BF16),
            struct((n_blocks + 1, BS, LANES), F32),
        ),
        in_specs=[SMEM, VMEM, VMEM, VMEM, VMEM, HBM],
        out_specs=(VMEM,) * 7,
        scratch_shapes=[
            pltpu.VMEM((n_blocks, 2 * key_width, cols), BF16),
            pltpu.VMEM((n_blocks, 1, cols), F32),
            pltpu.VMEM((max_own, BS, cols), F32),
            pltpu.VMEM((frames, pixels, half), BF16),
            dma((2,)),
        ],
        compiler_params=params(20),
        name="own_part",
    )(pairs, query, select, near_keys, near_shrink, memory_value)

    more_edges = pl.pallas_call(
        functools.partial(link_chunks, sizes, 2),
        out_shape=[struct((rows, LANES), BF16)] * (n_chunks - 2),
        in_specs=[HBM, VMEM],
        out_specs=[VMEM] * (n_chunks - 2),
        scratch_shapes=[dma((n_chunks - 2, W * frames))],
        compiler_params=params(1),
        name="link_chunks",
    )(memory_value, own_top)
    for edge in more_edges:
        link_halo.append(lax.ppermute(edge, "space", over_link))

    weights, factor, stats = pl.pallas_call(
        functools.partial(halo_scores, sizes),
        out_shape=(
            struct((max_halo, BS, cols), BF16),
            struct((n_blocks + 1, BS, LANES), F32),
            struct((2 * n_blocks, LANES), F32),
        ),
        in_specs=[SMEM] + [VMEM] * 6,
        out_specs=(VMEM,) * 3,
        scratch_shapes=[
            pltpu.VMEM((2 * W, 2 * key_width, cols), BF16),
            pltpu.VMEM((2 * W, 1, cols), F32),
            pltpu.VMEM((max_halo, BS, cols), F32),
            pltpu.VMEM((n_blocks + 1, BS, LANES), F32),
            pltpu.VMEM((n_blocks + 1, BS, LANES), F32),
        ],
        compiler_params=params(12),
        name="halo_scores",
    )(pairs, cat, self_term, chip_halo, link_halo[0], own_top, own_total)

    mine, other = [], []
    for c in range(n_chunks):
        if c * LANES == half:
            acc = pl.pallas_call(
                functools.partial(own_rest, sizes),
                out_shape=struct((n_blocks + 1, BS, value_width - half), F32),
                in_specs=[SMEM] + [VMEM] * 3,
                out_specs=VMEM,
                compiler_params=params(2),
                name="own_rest",
            )(pairs, own_weights, rest, mine[0])
        out_rows = pixels + (6 * n_blocks if c == 0 else 0)
        x = pl.pallas_call(
            functools.partial(chunk_sums, sizes, c),
            out_shape=struct((out_rows, LANES), BF16),
            in_specs=[SMEM] + [VMEM] * 6,
            out_specs=VMEM,
            scratch_shapes=[pltpu.VMEM((n_blocks + 1, BS, LANES), F32)],
            compiler_params=params(2),
            name=f"chunk_sums_{c}",
        )(pairs, weights, acc, factor, stats, chip_halo, link_halo[c])
        mine.append(x)
        other.append(lax.ppermute(x, "tm", swap) if n_tm == 2 else lax.all_gather(x, "tm"))

    if n_tm == 2:
        out = pl.pallas_call(
            functools.partial(combine, sizes, n_chunks),
            out_shape=struct((pixels, value_width), BF16),
            in_specs=[VMEM] * (2 * n_chunks),
            out_specs=VMEM,
            compiler_params=params(2),
            name="combine",
        )(*mine, *other)
    else:
        packed = other[0][:, pixels:, :]
        tops, totals = zip(*[unpack_stats(packed[i], n_blocks) for i in range(n_tm)])
        tops = jnp.stack(tops).reshape(n_tm, pixels, 1)
        totals = jnp.stack(totals).reshape(n_tm, pixels, 1)
        factors = jnp.exp2(tops - jnp.max(tops, axis=0, keepdims=True))
        total = jnp.sum(totals * factors, axis=0)
        sums = [jnp.sum(x[:, :pixels, :].astype(F32) * factors, axis=0) / total for x in other]
        out = jnp.concatenate(sums, axis=1).astype(BF16)
    return out[None]


def solution(mesh):
    in_specs = (
        P(None, "space", None),
        P(None, "space", None),
        P("tm", "space", None),
        P("tm", "space"),
        P("tm", "space", None),
        P("space", None),
        P("space"),
    )
    out_specs = P(None, "space", None)
    body = functools.partial(shards, mesh.shape["space"], mesh.shape["tm"])
    return jax.shard_map(body, mesh=mesh, in_specs=in_specs, out_specs=out_specs, check_vma=False)
```

time: 75.9 us -> 58.1 us (0.77)
  the two profiles are of different devices: /device:TPU:3 before, /device:TPU:8 now
where the time goes in v2:
time: 58.1 us; the launch traced here: 57 us
  Pallas kernels  29.2 us (50%)
  starting transfers between devices  17.8 us (31%)
  waiting for transfers between devices  9.92 us (17%)
    ppermute x4, waiting for transfers between devices, shards(): lax.ppermute(x, 'tm', swap)  9.9 us
    pallas_call x4, Pallas kernels, shards(): pl.pallas_call(functools.partial(chunk_sums, sizes, c), out_shape=struct(...  9.45 us
    ppermute x2, starting transfers between devices, shards(): link_halo.append(lax.ppermute(edge, 'space', over_link))  6.46 us
    pallas_call x1, Pallas kernels, shards(): pl.pallas_call(functools.partial(own_part, sizes), out_shape=(struct((max...  6.24 us
    ppermute x4, starting transfers between devices, shards(): lax.ppermute(x, 'tm', swap)  4.28 us
    ppermute x1, starting transfers between devices, shards(): link_halo.append(lax.ppermute(link_edge, 'space', over_link))  3.6 us
    pallas_call x1, Pallas kernels, shards(): pl.pallas_call(functools.partial(halo_scores, sizes), out_shape=(struct((...  3.57 us
    ppermute x1, starting transfers between devices, shards(): link_halo = [lax.ppermute(link_edge, 'space', over_link)]  3.37 us
  transfers between devices with their start and end apart: 9, of which 3 were waited for; matrix products, arithmetic and copies ran while one was open for 0% of the time, Pallas kernels for 41%

profile of v2, /device:TPU:8, one launch (start us, length us, event | category | flops | bytes accessed | tf_op | source)
XLA Modules:
  0.0 57.0 jit_solution(2397006258012844103)
XLA Ops:
  0.0 2.2 %lists_and_edge.1 = (s32[256]{0:T(256)S(1)}, bf16[1552,128]{1,0:T(8,128)(2,1)S(1)}) custom-call(s32[8,6]{1,0:T(8,128)} %list_ref.1, s32[8]{0:T(128)} %count_ref.1, bf16[4,64,1024]{2,1,0:T(8,128)(2,1)} %bitcast.8, bf16[4,1024]{1,0:T(4,128)(2,1)} %shrink_ref.3, bf16[4,1024,512]{2,1,0:T(8,128)(2,1)} %value_ref.7), custom_call_target="tpu_custom_call" | custom-call | tf_op jit(solution)/shard_map/lists_and_edge/pallas_call | solution.py:416
  2.2 1.9 %chip_edge_and_chunk.1 = (bf16[1168,512]{1,0:T(8,128)(2,1)S(1)}, bf16[1024,128]{1,0:T(8,128)(2,1)S(1)}, bf16[64,1024]{1,0:T(8,128)(2,1)S(1)}, bf16[64,1024]{1,0:...) custom-call(bf16[64,1024]{1,0:T(8,128)(2,1)} %bitcast.10, bf16[64,1024]{1,0:T(8,128)(2,1)} %bitcast.11, ...), custom_call_target="tpu_custom_call" | custom-call | tf_op jit(solution)/shard_map/chip_edge_and_chunk/pallas_call | solution.py:433
  4.2 0.1 collective-permute-start
  4.3 3.4 %collective-permute-start.1 = (bf16[1552,128]{1,0:T(8,128)(2,1)S(1)}, bf16[1552,128]{1,0:T(8,128)(2,1)S(1)}, u32[]{:S(2)}, u32[]{:S(2)}) collective-permute-start(bf16[1552,128]{1,0:T(8,128)(2,1)S(1)} %get-tuple-element.26.after_ref), channel_id=1, source_target_pairs={{2,4},{4,2},{6,8},{8,6},{10,12},{12,10},{14,16},{16,14},{18,20},{2... | collective-permute-start | bytes 1191944 | tf_op jit(solution)/shard_map/ppermute | solution.py:432
  7.6 6.2 %own_part.1 = (bf16[50,128,512]{2,1,0:T(8,128)(2,1)S(1)}, bf16[4,1024,256]{2,1,0:T(8,128)(2,1)S(1)}, f32[9,128,256]{2,1,0:T(8,128)S(1)}, f32[9,128,128]{2,1,0:T(...) custom-call(s32[256]{0:T(256)S(1)} %get-tuple-element.25.pairs_ref, ...), custom_call_target="tpu_custom_call" | custom-call | tf_op jit(solution)/shard_map/own_part/pallas_call | solution.py:452
  13.9 1.2 %link_chunks.1 = (bf16[1024,128]{1,0:T(8,128)(2,1)S(1)}, bf16[1024,128]{1,0:T(8,128)(2,1)S(1)}) custom-call(bf16[4,1024,512]{2,1,0:T(8,128)(2,1)} %value_ref.7, f32[9,128,128]{2,1,0:T(8,128)S(1)} %get-tuple-element.34.own_top_ref.after_ref), custom_call_target="tpu_custom_call" | custom-call | tf_op jit(solution)/shard_map/link_chunks/pallas_call | solution.py:476
  15.1 3.6 %collective-permute-start.4 = (bf16[1024,128]{1,0:T(8,128)(2,1)S(1)}, bf16[1024,128]{1,0:T(8,128)(2,1)S(1)}, u32[]{:S(2)}, u32[]{:S(2)}) collective-permute-start(bf16[1024,128]{1,0:T(8,128)(2,1)S(1)} %get-tuple-element.44), channel_id=1, source_target_pairs={{2,4},{4,2},{6,8},{8,6},{10,12},{12,10},{14,16},{16,14},{18,20},{2... | collective-permute-start | bytes 786440 | tf_op jit(solution)/shard_map/ppermute | solution.py:486
  18.7 2.9 %collective-permute-start.3 = (bf16[1024,128]{1,0:T(8,128)(2,1)S(1)}, bf16[1024,128]{1,0:T(8,128)(2,1)S(1)}, u32[]{:S(2)}, u32[]{:S(2)}) collective-permute-start(bf16[1024,128]{1,0:T(8,128)(2,1)S(1)} %get-tuple-element.43), channel_id=1, source_target_pairs={{2,4},{4,2},{6,8},{8,6},{10,12},{12,10},{14,16},{16,14},{18,20},{2... | collective-permute-start | bytes 786440 | tf_op jit(solution)/shard_map/ppermute | solution.py:486
  21.5 3.6 %collective-permute-start.2 = (bf16[1024,128]{1,0:T(8,128)(2,1)S(1)}, bf16[1024,128]{1,0:T(8,128)(2,1)S(1)}, u32[]{:S(2)}, u32[]{:S(2)}) collective-permute-start(bf16[1024,128]{1,0:T(8,128)(2,1)S(1)} %get-tuple-element.40), channel_id=1, source_target_pairs={{2,4},{4,2},{6,8},{8,6},{10,12},{12,10},{14,16},{16,14},{18,20},{2... | collective-permute-start | bytes 786440 | tf_op jit(solution)/shard_map/ppermute | solution.py:450
  25.2 0.0 collective-permute-done.1.link_ref
  25.2 0.0 collective-permute-done.chip_ref
  25.2 3.6 %halo_scores.1 = (bf16[34,128,512]{2,1,0:T(8,128)(2,1)S(1)}, f32[9,128,128]{2,1,0:T(8,128)S(1)}, f32[16,128]{1,0:T(8,128)S(1)}) custom-call(s32[256]{0:T(256)S(1)} %get-tuple-element.25.pairs_ref, bf16[9,128,128]{2,1,0:T(8,128)(2,1)S(1)} %get-tuple-element.31.cat_ref, f32[9,128,128]{2,1,0:T(8,128)S(1)} %get-tuple-element.32.self_ref, ...), custom_call_target="tpu_custom_call" | custom-call | tf_op jit(solution)/shard_map/halo_scores/pallas_call | solution.py:488
  28.8 2.3 %chunk_sums_0.1.after_ref.refs_0_ = bf16[1072,128]{1,0:T(8,128)(2,1)S(1)} custom-call(s32[256]{0:T(256)S(1)} %get-tuple-element.25.pairs_ref, bf16[34,128,512]{2,1,0:T(8,128)(2,1)S(1)} %get-tuple-element.36.weight_ref, f32[9,128,256]{2,1,0:T(8,128)S(1)} %get-tuple-element.37.acc_ref, f32[9,128,128]{2,1,0:T(8,128)S(1)} %get-tuple-element.38.factor_ref, ...), custom_call_target="tpu_custom_call" | custom-call | tf_op jit(solution)/shard_map/chunk_sums_0/pallas_call | solution.py:520
  31.1 1.6 %collective-permute-start.5 = (bf16[1072,128]{1,0:T(8,128)(2,1)S(1)}, bf16[1072,128]{1,0:T(8,128)(2,1)S(1)}, u32[]{:S(2)}, u32[]{:S(2)}) collective-permute-start(bf16[1072,128]{1,0:T(8,128)(2,1)S(1)} %chunk_sums_0.1.after_ref.refs_0_), channel_id=1, source_target_pairs={{1,0},{0,1},{3,2},{2,3},{5,4},{4,5},{7,6},{6,7},{9,8},{8,9},{11,10... | collective-permute-start | bytes 823304 | tf_op jit(solution)/shard_map/ppermute | solution.py:530
  32.6 3.1 %own_rest.1.acc_ref = f32[9,128,256]{2,1,0:T(8,128)S(1)} custom-call(s32[256]{0:T(256)S(1)} %get-tuple-element.25.pairs_ref, bf16[50,128,512]{2,1,0:T(8,128)(2,1)S(1)} %get-tuple-element.41.weight_ref, bf16[4,1024,256]{2,1,0:T(8,128)(2,1)S(1)} %get-tuple-element.42.value_ref, bf16[1072,128]{1,0:T(8,128)(2,1)S(1)} %chunk_sums_0.1.after_ref.refs_0_), custom_call_target="tpu_custom_call" | custom-call | tf_op jit(solution)/shard_map/own_rest/pallas_call | solution.py:511
  35.7 0.0 collective-permute-done.4.link_ref
  35.7 2.4 %chunk_sums_3.1.refs_3_ = bf16[1024,128]{1,0:T(8,128)(2,1)S(1)} custom-call(s32[256]{0:T(256)S(1)} %get-tuple-element.25.pairs_ref, bf16[34,128,512]{2,1,0:T(8,128)(2,1)S(1)} %get-tuple-element.36.weight_ref, f32[9,128,256]{2,1,0:T(8,128)S(1)} %own_rest.1.acc_ref, f32[9,128,128]{2,1,0:T(8,128)S(1)} %get-tuple-element.38.factor_ref, ...), custom_call_target="tpu_custom_call" | custom-call | tf_op jit(solution)/shard_map/chunk_sums_3/pallas_call | solution.py:520
  38.1 0.6 collective-permute-start.8
  38.7 0.0 collective-permute-done.3.link_ref
  38.7 2.4 %chunk_sums_2.1.refs_2_ = bf16[1024,128]{1,0:T(8,128)(2,1)S(1)} custom-call(s32[256]{0:T(256)S(1)} %get-tuple-element.25.pairs_ref, bf16[34,128,512]{2,1,0:T(8,128)(2,1)S(1)} %get-tuple-element.36.weight_ref, f32[9,128,256]{2,1,0:T(8,128)S(1)} %own_rest.1.acc_ref, f32[9,128,128]{2,1,0:T(8,128)S(1)} %get-tuple-element.38.factor_ref, ...), custom_call_target="tpu_custom_call" | custom-call | tf_op jit(solution)/shard_map/chunk_sums_2/pallas_call | solution.py:520
  41.1 1.6 %collective-permute-start.7 = (bf16[1024,128]{1,0:T(8,128)(2,1)S(1)}, bf16[1024,128]{1,0:T(8,128)(2,1)S(1)}, u32[]{:S(2)}, u32[]{:S(2)}) collective-permute-start(bf16[1024,128]{1,0:T(8,128)(2,1)S(1)} %chunk_sums_2.1.refs_2_), channel_id=1, source_target_pairs={{1,0},{0,1},{3,2},{2,3},{5,4},{4,5},{7,6},{6,7},{9,8},{8,9},{11,10... | collective-permute-start | bytes 786440 | tf_op jit(solution)/shard_map/ppermute | solution.py:530
  42.7 0.0 collective-permute-done.2.link_ref
  42.7 2.4 %chunk_sums_1.1.refs_1_ = bf16[1024,128]{1,0:T(8,128)(2,1)S(1)} custom-call(s32[256]{0:T(256)S(1)} %get-tuple-element.25.pairs_ref, bf16[34,128,512]{2,1,0:T(8,128)(2,1)S(1)} %get-tuple-element.36.weight_ref, f32[9,128,256]{2,1,0:T(8,128)S(1)} %get-tuple-element.37.acc_ref, f32[9,128,128]{2,1,0:T(8,128)S(1)} %get-tuple-element.38.factor_ref, ...), custom_call_target="tpu_custom_call" | custom-call | tf_op jit(solution)/shard_map/chunk_sums_1/pallas_call | solution.py:520
  45.1 0.6 collective-permute-start.6
  45.6 1.8 %collective-permute-done.8.refs_7_ = bf16[1024,128]{1,0:T(8,128)(2,1)S(1)} collective-permute-done((bf16[1024,128]{1,0:T(8,128)(2,1)S(1)}, bf16[1024,128]{1,0:T(8,128)(2,1)S(1)}, u32[]{:S(2)}, u32[]{:S(2)}) %collective-permute-start.8) | collective-permute-done | bytes 262176 | tf_op jit(solution)/shard_map/ppermute | solution.py:530
  47.4 5.3 %collective-permute-done.7.refs_6_ = bf16[1024,128]{1,0:T(8,128)(2,1)S(1)} collective-permute-done((bf16[1024,128]{1,0:T(8,128)(2,1)S(1)}, bf16[1024,128]{1,0:T(8,128)(2,1)S(1)}, u32[]{:S(2)}, u32[]{:S(2)}) %collective-permute-start.7) | collective-permute-done | bytes 262176 | tf_op jit(solution)/shard_map/ppermute | solution.py:530
  52.7 2.8 %collective-permute-done.6.refs_5_ = bf16[1024,128]{1,0:T(8,128)(2,1)S(1)} collective-permute-done((bf16[1024,128]{1,0:T(8,128)(2,1)S(1)}, bf16[1024,128]{1,0:T(8,128)(2,1)S(1)}, u32[]{:S(2)}, u32[]{:S(2)}) %collective-permute-start.6) | collective-permute-done | bytes 262176 | tf_op jit(solution)/shard_map/ppermute | solution.py:530
  55.5 0.0 collective-permute-done.5.refs_4_
  55.5 1.5 %combine.1 = bf16[1024,512]{1,0:T(8,128)(2,1)} custom-call(bf16[1072,128]{1,0:T(8,128)(2,1)S(1)} %chunk_sums_0.1.after_ref.refs_0_, bf16[1024,128]{1,0:T(8,128)(2,1)S(1)} %chunk_sums_1.1.refs_1_, bf16[1024,128]{1,0:T(8,128)(2,1)S(1)} %chunk_sums_2.1.refs_2_, bf16[1024,128]{1,0:T(8,128)(2,1)S(1)} %chunk_sums_3.1.refs_3_, ...), custom_call_target="tpu_custom_call" | custom-call | tf_op jit(solution)/shard_map/combine/pallas_call | solution.py:533
Async XLA Ops:
  4.2 21.0 %collective-permute-start = (bf16[1168,512]{1,0:T(8,128)(2,1)S(1)}, bf16[1168,512]{1,0:T(8,128)(2,1)S(1)}, u32[]{:S(2)}, u32[]{:S(2)}) collective-permute-start(bf16[1168,512]{1,0:T(8,128)(2,1)S(1)} %get-tuple-element.33), channel_id=1, source_target_pairs={{2,0},{0,2},{6,4},{4,6},{10,8},{8,10},{14,12},{12,14},{18,16},{16,... | collective-permute-start | bytes 3588104 | tf_op jit(solution)/shard_map/ppermute | solution.py:449
  4.3 20.9 %collective-permute-start.1 = (bf16[1552,128]{1,0:T(8,128)(2,1)S(1)}, bf16[1552,128]{1,0:T(8,128)(2,1)S(1)}, u32[]{:S(2)}, u32[]{:S(2)}) collective-permute-start(bf16[1552,128]{1,0:T(8,128)(2,1)S(1)} %get-tuple-element.26.after_ref), channel_id=1, source_target_pairs={{2,4},{4,2},{6,8},{8,6},{10,12},{12,10},{14,16},{16,14},{18,20},{2... | collective-permute-start | bytes 1191944 | tf_op jit(solution)/shard_map/ppermute | solution.py:432
  15.1 20.7 %collective-permute-start.4 = (bf16[1024,128]{1,0:T(8,128)(2,1)S(1)}, bf16[1024,128]{1,0:T(8,128)(2,1)S(1)}, u32[]{:S(2)}, u32[]{:S(2)}) collective-permute-start(bf16[1024,128]{1,0:T(8,128)(2,1)S(1)} %get-tuple-element.44), channel_id=1, source_target_pairs={{2,4},{4,2},{6,8},{8,6},{10,12},{12,10},{14,16},{16,14},{18,20},{2... | collective-permute-start | bytes 786440 | tf_op jit(solution)/shard_map/ppermute | solution.py:486
  18.7 20.0 %collective-permute-start.3 = (bf16[1024,128]{1,0:T(8,128)(2,1)S(1)}, bf16[1024,128]{1,0:T(8,128)(2,1)S(1)}, u32[]{:S(2)}, u32[]{:S(2)}) collective-permute-start(bf16[1024,128]{1,0:T(8,128)(2,1)S(1)} %get-tuple-element.43), channel_id=1, source_target_pairs={{2,4},{4,2},{6,8},{8,6},{10,12},{12,10},{14,16},{16,14},{18,20},{2... | collective-permute-start | bytes 786440 | tf_op jit(solution)/shard_map/ppermute | solution.py:486
  21.5 21.2 %collective-permute-start.2 = (bf16[1024,128]{1,0:T(8,128)(2,1)S(1)}, bf16[1024,128]{1,0:T(8,128)(2,1)S(1)}, u32[]{:S(2)}, u32[]{:S(2)}) collective-permute-start(bf16[1024,128]{1,0:T(8,128)(2,1)S(1)} %get-tuple-element.40), channel_id=1, source_target_pairs={{2,4},{4,2},{6,8},{8,6},{10,12},{12,10},{14,16},{16,14},{18,20},{2... | collective-permute-start | bytes 786440 | tf_op jit(solution)/shard_map/ppermute | solution.py:450
  31.1 24.5 %collective-permute-start.5 = (bf16[1072,128]{1,0:T(8,128)(2,1)S(1)}, bf16[1072,128]{1,0:T(8,128)(2,1)S(1)}, u32[]{:S(2)}, u32[]{:S(2)}) collective-permute-start(bf16[1072,128]{1,0:T(8,128)(2,1)S(1)} %chunk_sums_0.1.after_ref.refs_0_), channel_id=1, source_target_pairs={{1,0},{0,1},{3,2},{2,3},{5,4},{4,5},{7,6},{6,7},{9,8},{8,9},{11,10... | collective-permute-start | bytes 823304 | tf_op jit(solution)/shard_map/ppermute | solution.py:530
  38.1 9.3 %collective-permute-start.8 = (bf16[1024,128]{1,0:T(8,128)(2,1)S(1)}, bf16[1024,128]{1,0:T(8,128)(2,1)S(1)}, u32[]{:S(2)}, u32[]{:S(2)}) collective-permute-start(bf16[1024,128]{1,0:T(8,128)(2,1)S(1)} %chunk_sums_3.1.refs_3_), channel_id=1, source_target_pairs={{1,0},{0,1},{3,2},{2,3},{5,4},{4,5},{7,6},{6,7},{9,8},{8,9},{11,10... | collective-permute-start | bytes 786440 | tf_op jit(solution)/shard_map/ppermute | solution.py:530
  41.1 11.6 %collective-permute-start.7 = (bf16[1024,128]{1,0:T(8,128)(2,1)S(1)}, bf16[1024,128]{1,0:T(8,128)(2,1)S(1)}, u32[]{:S(2)}, u32[]{:S(2)}) collective-permute-start(bf16[1024,128]{1,0:T(8,128)(2,1)S(1)} %chunk_sums_2.1.refs_2_), channel_id=1, source_target_pairs={{1,0},{0,1},{3,2},{2,3},{5,4},{4,5},{7,6},{6,7},{9,8},{8,9},{11,10... | collective-permute-start | bytes 786440 | tf_op jit(solution)/shard_map/ppermute | solution.py:530
  45.1 10.5 %collective-permute-start.6 = (bf16[1024,128]{1,0:T(8,128)(2,1)S(1)}, bf16[1024,128]{1,0:T(8,128)(2,1)S(1)}, u32[]{:S(2)}, u32[]{:S(2)}) collective-permute-start(bf16[1024,128]{1,0:T(8,128)(2,1)S(1)} %chunk_sums_1.1.refs_1_), channel_id=1, source_target_pairs={{1,0},{0,1},{3,2},{2,3},{5,4},{4,5},{7,6},{6,7},{9,8},{8,9},{11,10... | collective-permute-start | bytes 786440 | tf_op jit(solution)/shard_map/ppermute | solution.py:530

commit v3 on v2

v3 whole, which is shorter than its diff:
```python
import functools
import math

import jax
import jax.numpy as jnp
from jax import lax
from jax.experimental import pallas as pl
from jax.experimental.pallas import tpu as pltpu
from jax.sharding import PartitionSpec as P

BS = 128
W = 2
LANES = 128
EDGE = W * BS
NONE = -1e30
WIDTH = 128
UNROLL = 4
OWN_AT, HALO_AT, COUNT_AT = 0, 64, 128
F32, BF16 = jnp.float32, jnp.bfloat16

VMEM = pl.BlockSpec(memory_space=pltpu.VMEM)
SMEM = pl.BlockSpec(memory_space=pltpu.SMEM)
HBM = pl.BlockSpec(memory_space=pltpu.HBM)


def params(mib):
    return pltpu.CompilerParams(vmem_limit_bytes=mib * 1024 * 1024)


def row_to_lanes(row):
    return jnp.transpose(jnp.broadcast_to(row, (row.shape[1], row.shape[1])))


def lane_tiles(x):
    return [x[:, i * LANES : (i + 1) * LANES] for i in range(x.shape[1] // LANES)]


def wide(x, times):
    return jnp.concatenate([x] * times, axis=1)


def value_copies(sizes, value_ref, out, start, lanes, sems):
    frames = sizes[0]
    return [
        pltpu.make_async_copy(
            value_ref.at[f, pl.ds(start + e * BS, BS), lanes],
            out.at[pl.ds((e * frames + f) * BS, BS), :],
            sems.at[e * frames + f],
        )
        for e in range(W)
        for f in range(frames)
    ]


def key_place(sizes, e, f):
    frames, key_width = sizes[0], sizes[4]
    per_row = WIDTH // LANES
    i = e * frames + f
    at, lane = frames * EDGE + i // per_row * key_width, i % per_row * LANES
    return slice(at, at + key_width), slice(lane, lane + LANES)


def edge_start(pixels, over_link):
    odd = lax.rem(lax.axis_index("space"), 2)
    side = odd if over_link else 1 - odd
    return pl.multiple_of(side * (pixels - EDGE), EDGE)


def shrink_rows(sizes, shrink, start):
    frames = sizes[0]
    edge = shrink[:, pl.ds(start, EDGE)].astype(F32)
    rows = [edge[:, e * BS : (e + 1) * BS] for e in range(W)]
    pad = jnp.zeros((16 - W * frames, LANES), F32)
    return jnp.concatenate(rows + [pad], axis=0).astype(BF16)


def lists_and_edge(
    sizes, list_ref, count_ref, query_ref, select_ref, key_ref, shrink_ref, value_ref,
    pairs_ref, link_ref, chip_ref, query_out, select_out, key_out, shrink_out,
    list_sc, count_sc, sems, key_sems, small_sems,
):
    frames, pixels, n_blocks, n_listed, key_width, value_width = sizes
    start = edge_start(pixels, True)
    small = [
        pltpu.make_async_copy(list_ref, list_sc, small_sems.at[0]),
        pltpu.make_async_copy(count_ref, count_sc, small_sems.at[1]),
        pltpu.make_async_copy(shrink_ref, shrink_out, small_sems.at[2]),
    ]
    for copy in small:
        copy.start()
    copies = value_copies(sizes, value_ref, link_ref, start, pl.ds(0, WIDTH), sems.at[0])
    for e in range(W):
        for f in range(frames):
            copies.append(
                pltpu.make_async_copy(
                    key_ref.at[f, :, pl.ds(start + e * BS, BS)],
                    link_ref.at[key_place(sizes, e, f)],
                    key_sems.at[e * frames + f],
                )
            )
    copies += [
        pltpu.make_async_copy(query_ref, query_out, small_sems.at[3]),
        pltpu.make_async_copy(select_ref, select_out, small_sems.at[4]),
        pltpu.make_async_copy(key_ref, key_out, small_sems.at[5]),
    ]
    chip_start = edge_start(pixels, False)
    copies += value_copies(sizes, value_ref, chip_ref, chip_start, slice(None), sems.at[1])
    chip_at = frames * EDGE
    for e in range(W):
        for f in range(frames):
            copies.append(
                pltpu.make_async_copy(
                    key_ref.at[f, :, pl.ds(chip_start + e * BS, BS)],
                    chip_ref.at[pl.ds(chip_at, key_width), pl.ds(f * BS, BS)],
                    key_sems.at[(W + e) * frames + f],
                )
            )
        chip_at += key_width
    for copy in copies:
        copy.start()
    for copy in small:
        copy.wait()
    link_ref[link_ref.shape[0] - 16 :, :LANES] = shrink_rows(sizes, shrink_out, start)
    chip_ref[chip_at : chip_at + 16, :LANES] = shrink_rows(sizes, shrink_out, chip_start)
    odd = lax.rem(lax.axis_index("space"), 2)

    left, right = W * (1 - odd), W * odd - (W + n_blocks)

    def block(b, carry):
        n_own, n_halo = carry
        live = count_sc[b]
        for j in range(n_listed):
            l = list_sc[b, j]
            inside = (l >= W) & (l < W + n_blocks)
            pairs_ref[OWN_AT + n_own] = b * n_blocks + (l - W)
            pairs_ref[HALO_AT + n_halo] = b * 4 + l + jnp.where(l >= W, right, left)
            n_own += jnp.where((j < live) & inside, 1, 0)
            n_halo += jnp.where((j < live) & jnp.logical_not(inside), 1, 0)
        return n_own, n_halo

    n_own, n_halo = lax.fori_loop(0, n_blocks, block, (0, 0))
    for i in range(UNROLL - 1):
        pairs_ref[OWN_AT + n_own + i] = n_blocks * n_blocks
        pairs_ref[HALO_AT + n_halo + i] = n_blocks * 4
    pairs_ref[COUNT_AT] = n_own
    pairs_ref[COUNT_AT + 1] = n_halo
    for copy in copies:
        copy.wait()


def unrolled(count, body):
    def step(i, carry):
        for k in range(UNROLL):
            body(UNROLL * i + k)
        return carry

    lax.fori_loop(0, (count + UNROLL - 1) // UNROLL, step, 0)


def squares_over(k):
    k_f = k.astype(F32)
    return jnp.concatenate([(k_f * k_f).astype(BF16), k], axis=0)


def own_part(
    sizes, pairs_ref, query_ref, select_ref, key_ref, shrink_ref, value_ref,
    acc_ref, top_ref, total_ref, cat_ref, self_ref, *refs,
):
    links, (keys_sc, shr_sc, score_sc, value_sc, sem, edge_sems) = refs[:-6], refs[-6:]
    frames, pixels, n_blocks, n_listed, key_width, value_width = sizes
    cols = frames * BS
    bits = int(math.log2(n_blocks))
    values = pltpu.make_async_copy(value_ref, value_sc, sem)
    values.start()
    edges = []
    for i, link in enumerate(links):
        lanes = pl.ds((i + 1) * WIDTH, WIDTH)
        edges += value_copies(sizes, value_ref, link, edge_start(pixels, True), lanes, edge_sems.at[i])
    for copy in edges:
        copy.start()
    scale = -math.log2(math.e) / math.sqrt(key_width)
    for b in range(n_blocks):
        block = slice(b * BS, (b + 1) * BS)
        q = query_ref[:, block].astype(F32)
        s = select_ref[:, block].astype(F32)
        both = jnp.concatenate([s, -2.0 * q * s], axis=0)
        cat_ref[b] = jnp.transpose(both).astype(BF16)
        self_ref[b] = row_to_lanes(jnp.sum(s * q * q, axis=0, keepdims=True))
    cat_ref[n_blocks] = jnp.zeros((BS, 2 * key_width), BF16)
    self_ref[n_blocks] = jnp.zeros((BS, LANES), F32)
    shrink = shrink_ref[...].astype(F32) * scale
    for l in range(n_blocks):
        for f in range(frames):
            block = slice(l * BS, (l + 1) * BS)
            keys_sc[l, :, f * BS : (f + 1) * BS] = squares_over(key_ref[f, :, block])
            shr_sc[l, :, f * BS : (f + 1) * BS] = shrink[f : f + 1, block]
    top_ref[...] = jnp.full_like(top_ref, NONE)
    total_ref[...] = jnp.zeros_like(total_ref)
    acc_ref[...] = jnp.zeros_like(acc_ref)
    count = pairs_ref[COUNT_AT]

    def score(p):
        code = pairs_ref[OWN_AT + p]
        b, l = code >> bits, code & (n_blocks - 1)
        s = jnp.dot(cat_ref[b], keys_sc[l], preferred_element_type=F32)
        s = (s + wide(self_ref[b], frames)) * shr_sc[l]
        score_sc[p] = s
        top_ref[b] = functools.reduce(jnp.maximum, lane_tiles(s), top_ref[b])

    unrolled(count, score)
    for b in range(n_blocks):
        top_ref[b] = jnp.broadcast_to(jnp.max(top_ref[b], axis=1, keepdims=True), (BS, LANES))
    values.wait()

    def read(p):
        code = pairs_ref[OWN_AT + p]
        b, l = code >> bits, code & (n_blocks - 1)
        w = jnp.exp2(score_sc[p] - wide(top_ref[b], frames))
        total_ref[b] = functools.reduce(jnp.add, lane_tiles(w), total_ref[b])
        v = value_sc[:, pl.ds(pl.multiple_of(l * BS, BS), BS), :].reshape(cols, value_width)
        acc_ref[b] += jnp.dot(w.astype(BF16), v, preferred_element_type=F32)

    unrolled(count, read)
    for copy in edges:
        copy.wait()


def gate(x_ref, *refs):
    pass

def halo_scores(
    sizes, pairs_ref, cat_ref, self_ref, chip_ref, link_ref, own_top_ref, own_total_ref,
    weight_ref, factor_ref, stats_ref,
    keys_sc, shr_sc, score_sc, top_sc, total_sc,
):
    frames, pixels, n_blocks, n_listed, key_width, value_width = sizes
    rows = frames * EDGE
    scale = -math.log2(math.e) / math.sqrt(key_width)
    for e in range(W):
        at = rows + e * key_width
        keys_sc[e] = squares_over(chip_ref[at : at + key_width, :])
        for f in range(frames):
            keys_sc[W + e, :, f * BS : (f + 1) * BS] = squares_over(link_ref[key_place(sizes, e, f)])
    shrinks = [
        chip_ref[rows + W * key_width :, :LANES].astype(F32) * scale,
        link_ref[link_ref.shape[0] - 16 :, :LANES].astype(F32) * scale,
    ]
    for side in range(2):
        for e in range(W):
            for f in range(frames):
                at = e * frames + f
                shr_sc[side * W + e, :, f * BS : (f + 1) * BS] = shrinks[side][at : at + 1, :]
    top_sc[...] = jnp.full_like(top_sc, NONE)
    total_sc[...] = jnp.zeros_like(total_sc)
    count = pairs_ref[COUNT_AT + 1]

    def score(p):
        code = pairs_ref[HALO_AT + p]
        b, h = code >> 2, code & 3
        s = jnp.dot(cat_ref[b], keys_sc[h], preferred_element_type=F32)
        s = (s + wide(self_ref[b], frames)) * shr_sc[h]
        score_sc[p] = s
        top_sc[b] = functools.reduce(jnp.maximum, lane_tiles(s), top_sc[b])

    unrolled(count, score)
    for b in range(n_blocks):
        own = own_top_ref[b]
        top = jnp.maximum(own, jnp.broadcast_to(jnp.max(top_sc[b], axis=1, keepdims=True), (BS, LANES)))
        top_sc[b] = top
        factor_ref[b] = jnp.exp2(own - top)

    def weigh(p):
        code = pairs_ref[HALO_AT + p]
        b = code >> 2
        w = jnp.exp2(score_sc[p] - wide(top_sc[b], frames))
        total_sc[b] = functools.reduce(jnp.add, lane_tiles(w), total_sc[b])
        weight_ref[p] = w.astype(BF16)

    unrolled(count, weigh)
    for b in range(n_blocks):
        total = jnp.sum(total_sc[b] + own_total_ref[b] * factor_ref[b], axis=1, keepdims=True)
        stats_ref[b : b + 1, :] = jnp.transpose(top_sc[b])[:1, :]
        stats_ref[n_blocks + b : n_blocks + b + 1, :] = jnp.transpose(jnp.broadcast_to(total, (BS, LANES)))[:1, :]


def chunk_sums(sizes, lanes, pairs_ref, weight_ref, acc_ref, factor_ref, stats_ref, chip_ref, link_ref, *refs):
    frames, pixels, n_blocks, n_listed, key_width, value_width = sizes
    cols = frames * BS
    out_ref, sum_sc = refs[-2:]
    width = lanes.stop - lanes.start
    for b in range(n_blocks):
        sum_sc[b] = acc_ref[b, :, lanes] * wide(factor_ref[b], width // LANES)
    sum_sc[n_blocks] = jnp.zeros((BS, width), F32)

    def add(p):
        code = pairs_ref[HALO_AT + p]
        b, h = code >> 2, code & 3
        at = pl.multiple_of((h & (W - 1)) * cols, cols)
        chip = chip_ref[pl.ds(at, cols), lanes]
        v = jnp.where(h >= W, link_ref[pl.ds(at, cols), :], chip)
        sum_sc[b] += jnp.dot(weight_ref[p], v, preferred_element_type=F32)

    unrolled(pairs_ref[COUNT_AT + 1], add)
    for b in range(n_blocks):
        out_ref[b * BS : (b + 1) * BS, :] = sum_sc[b].astype(BF16)
    if lanes.start == 0:
        rest = stats_ref[...]
        for i in range(3):
            piece = rest.astype(BF16)
            rest = rest - piece.astype(F32)
            out_ref[pixels + i * 2 * n_blocks : pixels + (i + 1) * 2 * n_blocks, :] = piece


def unpack_stats(x, n_blocks):
    n = 2 * n_blocks
    x = x.astype(F32)
    x = (x[:n] + x[n : 2 * n]) + x[2 * n :]
    return x[:n_blocks], x[n_blocks:]


def combine(sizes, *refs):
    frames, pixels, n_blocks = sizes[:3]
    n = len(refs) // 2
    mine, other, out_ref = refs[:n], refs[n : 2 * n], refs[-1]

    def run(first, second):
        top_a, total_a = unpack_stats(first[0][pixels:, :], n_blocks)
        top_b, total_b = unpack_stats(second[0][pixels:, :], n_blocks)
        top = jnp.maximum(top_a, top_b)
        a, b = jnp.exp2(top_a - top), jnp.exp2(top_b - top)
        total = total_a * a + total_b * b
        a, b = a / total, b / total
        for i in range(n_blocks):
            col_a = row_to_lanes(a[i : i + 1, :])
            col_b = row_to_lanes(b[i : i + 1, :])
            r = slice(i * BS, (i + 1) * BS)
            at = 0
            for one, two in zip(first, second):
                width = one.shape[1]
                times = width // LANES
                x = one[r, :].astype(F32) * wide(col_a, times) + two[r, :].astype(F32) * wide(col_b, times)
                out_ref[r, at : at + width] = x.astype(BF16)
                at += width

    me = lax.axis_index("tm")

    @pl.when(me == 0)
    def _():
        run(mine, other)

    @pl.when(me != 0)
    def _():
        run(other, mine)


def shards(n_space, n_tm, query_key, selection, memory_key, shrinkage, memory_value, block_list, block_count):
    frames, pixels, key_width = memory_key.shape
    value_width = memory_value.shape[2]
    n_blocks, n_listed = block_list.shape
    sizes = (frames, pixels, n_blocks, n_listed, key_width, value_width)
    cols = frames * BS
    rows = frames * EDGE
    n_chunks = value_width // WIDTH
    link_rows = rows + W * frames * key_width * LANES // WIDTH + 16
    chip_rows = rows + W * key_width + 16
    max_halo = n_blocks * min(n_listed, 2 * W) + UNROLL
    max_own = n_blocks * n_listed + UNROLL
    struct = jax.ShapeDtypeStruct
    dma = pltpu.SemaphoreType.DMA
    query, select = jnp.swapaxes(query_key[0], 0, 1), jnp.swapaxes(selection[0], 0, 1)
    keys = jnp.swapaxes(memory_key, 1, 2)
    query, select, keys, shrinkage, memory_value, block_list, block_count = [
        pltpu.with_memory_space_constraint(x, pltpu.HBM)
        for x in (query, select, keys, shrinkage, memory_value, block_list, block_count)
    ]
    on_chip = [(i ^ 1, i) for i in range(n_space)]
    over_link = []
    for i in range(n_space):
        for t in range(n_tm):
            j = i - 1 if i % 2 == 0 else i + 1
            source = j * n_tm + t if 0 <= j < n_space else i * n_tm + (t ^ 1)
            over_link.append((source, i * n_tm + t))
    round_link = [((i - 1 if i % 2 == 0 else i + 1) % n_space, i) for i in range(n_space)]
    swap = [(i ^ 1, i) for i in range(n_tm)]

    pairs, link_edge, chip_edge, query, select, keys, near_shrink = pl.pallas_call(
        functools.partial(lists_and_edge, sizes),
        out_shape=(
            struct((256,), jnp.int32),
            struct((link_rows, WIDTH), BF16),
            struct((chip_rows, value_width), BF16),
            struct(query.shape, BF16),
            struct(select.shape, BF16),
            struct(keys.shape, BF16),
            struct(shrinkage.shape, BF16),
        ),
        in_specs=[HBM] * 7,
        out_specs=(SMEM,) + (VMEM,) * 6,
        scratch_shapes=[
            pltpu.SMEM(block_list.shape, jnp.int32),
            pltpu.SMEM(block_count.shape, jnp.int32),
            dma((2, W * frames)),
            dma((2 * W * frames,)),
            dma((6,)),
        ],
        compiler_params=params(1),
        name="lists_and_edge",
    )(block_list, block_count, query, select, keys, shrinkage, memory_value)
    link_halo = [lax.ppermute(link_edge, ("space", "tm"), over_link)]
    chip_halo = lax.ppermute(chip_edge, "space", on_chip)

    acc, own_top, own_total, cat, self_term, *more_edges = pl.pallas_call(
        functools.partial(own_part, sizes),
        out_shape=(
            struct((n_blocks + 1, BS, value_width), F32),
            struct((n_blocks + 1, BS, LANES), F32),
            struct((n_blocks + 1, BS, LANES), F32),
            struct((n_blocks + 1, BS, 2 * key_width), BF16),
            struct((n_blocks + 1, BS, LANES), F32),
        )
        + (struct((rows, WIDTH), BF16),) * (n_chunks - 1),
        in_specs=[SMEM, VMEM, VMEM, VMEM, VMEM, HBM],
        out_specs=(VMEM,) * (4 + n_chunks),
        scratch_shapes=[
            pltpu.VMEM((n_blocks, 2 * key_width, cols), BF16),
            pltpu.VMEM((n_blocks, 1, cols), F32),
            pltpu.VMEM((max_own, BS, cols), F32),
            pltpu.VMEM(memory_value.shape, BF16),
            dma,
            dma((n_chunks - 1, W * frames)),
        ],
        compiler_params=params(24),
        name="own_part",
    )(pairs, query, select, keys, near_shrink, memory_value)
    def send_edge(edge, *after):
        edge = pl.pallas_call(
            gate,
            out_shape=struct(edge.shape, edge.dtype),
            in_specs=[VMEM] * (1 + len(after)),
            out_specs=VMEM,
            input_output_aliases={0: 0},
            compiler_params=params(1),
            name="gate",
        )(edge, *after)
        return lax.ppermute(edge, "space", round_link)

    link_halo.append(send_edge(more_edges[0], link_halo[0], own_top))

    weights, factor, stats = pl.pallas_call(
        functools.partial(halo_scores, sizes),
        out_shape=(
            struct((max_halo, BS, cols), BF16),
            struct((n_blocks + 1, BS, LANES), F32),
            struct((2 * n_blocks, LANES), F32),
        ),
        in_specs=[SMEM] + [VMEM] * 6,
        out_specs=(VMEM,) * 3,
        scratch_shapes=[
            pltpu.VMEM((2 * W, 2 * key_width, cols), BF16),
            pltpu.VMEM((2 * W, 1, cols), F32),
            pltpu.VMEM((max_halo, BS, cols), F32),
            pltpu.VMEM((n_blocks + 1, BS, LANES), F32),
            pltpu.VMEM((n_blocks + 1, BS, LANES), F32),
        ],
        compiler_params=params(12),
        name="halo_scores",
    )(pairs, cat, self_term, chip_halo, link_halo[0], own_top, own_total)

    mine, other = [], []
    for c in range(n_chunks):
        lanes = slice(c * WIDTH, (c + 1) * WIDTH)
        out_rows = pixels + (6 * n_blocks if c == 0 else 0)
        after = other[:1] if c == 2 else []
        x = pl.pallas_call(
            functools.partial(chunk_sums, sizes, lanes),
            out_shape=struct((out_rows, WIDTH), BF16),
            in_specs=[SMEM] + [VMEM] * (6 + len(after)),
            out_specs=VMEM,
            scratch_shapes=[pltpu.VMEM((n_blocks + 1, BS, WIDTH), F32)],
            compiler_params=params(4),
            name=f"chunk_sums_{c}",
        )(pairs, weights, acc, factor, stats, chip_halo, link_halo[c], *after)
        mine.append(x)
        if c + 2 < n_chunks:
            link_halo.append(send_edge(more_edges[c + 1], x))
        other.append(lax.ppermute(x, "tm", swap) if n_tm == 2 else lax.all_gather(x, "tm"))

    if n_tm == 2:
        out = pl.pallas_call(
            functools.partial(combine, sizes),
            out_shape=struct((pixels, value_width), BF16),
            in_specs=[VMEM] * len(mine + other),
            out_specs=VMEM,
            compiler_params=params(2),
            name="combine",
        )(*mine, *other)
    else:
        packed = other[0][:, pixels:, :]
        tops, totals = zip(*[unpack_stats(packed[i], n_blocks) for i in range(n_tm)])
        tops = jnp.stack(tops).reshape(n_tm, pixels, 1)
        totals = jnp.stack(totals).reshape(n_tm, pixels, 1)
        factors = jnp.exp2(tops - jnp.max(tops, axis=0, keepdims=True))
        total = jnp.sum(totals * factors, axis=0)
        sums = [jnp.sum(x[:, :pixels, :].astype(F32) * factors, axis=0) / total for x in other]
        out = jnp.concatenate(sums, axis=1).astype(BF16)
    return out[None]


def solution(mesh):
    in_specs = (
        P(None, "space", None),
        P(None, "space", None),
        P("tm", "space", None),
        P("tm", "space"),
        P("tm", "space", None),
        P("space", None),
        P("space"),
    )
    out_specs = P(None, "space", None)
    body = functools.partial(shards, mesh.shape["space"], mesh.shape["tm"])
    return jax.shard_map(body, mesh=mesh, in_specs=in_specs, out_specs=out_specs, check_vma=False)
```

time: 58.1 us -> 50.5 us (0.87)
  the two profiles are of different devices: /device:TPU:8 before, /device:TPU:1 now
where the time goes in v3:
time: 50.5 us; the launch traced here: 51.3 us
  Pallas kernels  21.7 us (43%)
  waiting for transfers between devices  18.8 us (37%)
  starting transfers between devices  10.7 us (21%)
    ppermute x3, waiting for transfers between devices, send_edge(): return lax.ppermute(edge, 'space', round_link)  9.57 us
    pallas_call x4, Pallas kernels, shards(): pl.pallas_call(functools.partial(chunk_sums, sizes, lanes), out_shape=str...  7.8 us
    ppermute x4, waiting for transfers between devices, shards(): lax.ppermute(x, 'tm', swap)  6.76 us
    pallas_call x1, Pallas kernels, shards(): pl.pallas_call(functools.partial(own_part, sizes), out_shape=(struct((n_b...  6.57 us
    ppermute x3, starting transfers between devices, send_edge(): return lax.ppermute(edge, 'space', round_link)  4.27 us
    ppermute x4, starting transfers between devices, shards(): lax.ppermute(x, 'tm', swap)  3.71 us
    pallas_call x1, Pallas kernels, shards(): pl.pallas_call(functools.partial(halo_scores, sizes), out_shape=(struct((...  3.17 us
    pallas_call x1, Pallas kernels, shards(): pl.pallas_call(functools.partial(lists_and_edge, sizes), out_shape=(struc...  2.69 us
  transfers between devices with their start and end apart: 9, of which 5 were waited for; matrix products, arithmetic and copies ran while one was open for 0% of the time, Pallas kernels for 34%

profile of v3, /device:TPU:1, one launch (start us, length us, event | category | flops | bytes accessed | tf_op | source)
XLA Modules:
  0.0 51.3 jit_solution(8170156187710858270)
XLA Ops:
  0.0 2.7 %lists_and_edge.1 = (s32[256]{0:T(256)S(1)}, bf16[1552,128]{1,0:T(8,128)(2,1)S(1)}, bf16[1168,512]{1,0:T(8,128)(2,1)S(1)}, bf16[64,1024]{1,0:T(8,128)(2,1)S(1)},...) custom-call(s32[8,6]{1,0:T(8,128)} %list_ref.1, s32[8]{0:T(128)} %count_ref.1, ...), custom_call_target="tpu_custom_call" | custom-call | tf_op jit(solution)/shard_map/lists_and_edge/pallas_call | solution.py:386
  2.7 0.1 collective-permute-start
  2.8 2.6 %collective-permute-start.1 = (bf16[1552,128]{1,0:T(8,128)(2,1)S(1)}, bf16[1552,128]{1,0:T(8,128)(2,1)S(1)}, u32[]{:S(2)}, u32[]{:S(2)}) collective-permute-start(bf16[1552,128]{1,0:T(8,128)(2,1)S(1)} %get-tuple-element.31), channel_id=1, source_target_pairs={{1,0},{0,1},{4,2},{5,3},{2,4},{3,5},{8,6},{9,7},{6,8},{7,9},{12,10... | collective-permute-start | bytes 1191944 | tf_op jit(solution)/shard_map/ppermute | solution.py:409
  5.4 6.6 %own_part.1 = (f32[9,128,512]{2,1,0:T(8,128)S(1)}, f32[9,128,128]{2,1,0:T(8,128)S(1)}, f32[9,128,128]{2,1,0:T(8,128)S(1)}, bf16[9,128,128]{2,1,0:T(8,128)(2,1)S(...) custom-call(s32[256]{0:T(256)S(1)} %get-tuple-element.23.pairs_ref, ...), custom_call_target="tpu_custom_call" | custom-call | tf_op jit(solution)/shard_map/own_part/pallas_call | solution.py:412
  12.0 2.4 %collective-permute-done.1.link_ref.refs_0_ = bf16[1552,128]{1,0:T(8,128)(2,1)S(1)} collective-permute-done((bf16[1552,128]{1,0:T(8,128)(2,1)S(1)}, bf16[1552,128]{1,0:T(8,128)(2,1)S(1)}, u32[]{:S(2)}, u32[]{:S(2)}) %collective-permute-start.1) | collective-permute-done | bytes 397344 | tf_op jit(solution)/shard_map/ppermute | solution.py:409
  14.5 2.5 %collective-permute-start.2 = (bf16[1024,128]{1,0:T(8,128)(2,1)S(1)}, bf16[1024,128]{1,0:T(8,128)(2,1)S(1)}, u32[]{:S(2)}, u32[]{:S(2)}) collective-permute-start(bf16[1024,128]{1,0:T(8,128)(2,1)S(1)} %gate.3), channel_id=1, source_target_pairs={{30,0},{4,2},{2,4},{8,6},{6,8},{12,10},{10,12},{16,14},{14,16},{20... | collective-permute-start | bytes 786440 | tf_op jit(solution)/shard_map/ppermute | solution.py:445
  16.9 0.0 collective-permute-done.chip_ref
  17.0 3.2 %halo_scores.1 = (bf16[36,128,512]{2,1,0:T(8,128)(2,1)S(1)}, f32[9,128,128]{2,1,0:T(8,128)S(1)}, f32[16,128]{1,0:T(8,128)S(1)}) custom-call(s32[256]{0:T(256)S(1)} %get-tuple-element.23.pairs_ref, bf16[9,128,128]{2,1,0:T(8,128)(2,1)S(1)} %get-tuple-element.28.cat_ref, f32[9,128,128]{2,1,0:T(8,128)S(1)} %get-tuple-element.29.self_ref, ...), custom_call_target="tpu_custom_call" | custom-call | tf_op jit(solution)/shard_map/halo_scores/pallas_call | solution.py:449
  20.1 2.0 %chunk_sums_0.1.refs_0_ = bf16[1072,128]{1,0:T(8,128)(2,1)S(1)} custom-call(s32[256]{0:T(256)S(1)} %get-tuple-element.23.pairs_ref, bf16[36,128,512]{2,1,0:T(8,128)(2,1)S(1)} %get-tuple-element.34.weight_ref, f32[9,128,512]{2,1,0:T(8,128)S(1)} %get-tuple-element.35.acc_ref, f32[9,128,128]{2,1,0:T(8,128)S(1)} %get-tuple-element.36.factor_ref, ...), custom_call_target="tpu_custom_call" | custom-call | tf_op jit(solution)/shard_map/chunk_sums_0/pallas_call | solution.py:474
  22.1 1.3 %collective-permute-start.4 = (bf16[1072,128]{1,0:T(8,128)(2,1)S(1)}, bf16[1072,128]{1,0:T(8,128)(2,1)S(1)}, u32[]{:S(2)}, u32[]{:S(2)}) collective-permute-start(bf16[1072,128]{1,0:T(8,128)(2,1)S(1)} %chunk_sums_0.1.refs_0_), channel_id=1, source_target_pairs={{1,0},{0,1},{3,2},{2,3},{5,4},{4,5},{7,6},{6,7},{9,8},{8,9},{11,10... | collective-permute-start | bytes 823304 | tf_op jit(solution)/shard_map/ppermute | solution.py:486
  23.4 0.4 collective-permute-done.2.link_ref
  23.8 1.9 %chunk_sums_1.1.refs_0_.refs_1_ = bf16[1024,128]{1,0:T(8,128)(2,1)S(1)} custom-call(s32[256]{0:T(256)S(1)} %get-tuple-element.23.pairs_ref, bf16[36,128,512]{2,1,0:T(8,128)(2,1)S(1)} %get-tuple-element.34.weight_ref, f32[9,128,512]{2,1,0:T(8,128)S(1)} %get-tuple-element.35.acc_ref, f32[9,128,128]{2,1,0:T(8,128)S(1)} %get-tuple-element.36.factor_ref, ...), custom_call_target="tpu_custom_call" | custom-call | tf_op jit(solution)/shard_map/chunk_sums_1/pallas_call | solution.py:474
  25.8 0.1 collective-permute-start.5
  25.8 1.7 %collective-permute-start.3 = (bf16[1024,128]{1,0:T(8,128)(2,1)S(1)}, bf16[1024,128]{1,0:T(8,128)(2,1)S(1)}, u32[]{:S(2)}, u32[]{:S(2)}) collective-permute-start(bf16[1024,128]{1,0:T(8,128)(2,1)S(1)} %gate.4), channel_id=1, source_target_pairs={{30,0},{4,2},{2,4},{8,6},{6,8},{12,10},{10,12},{16,14},{14,16},{20... | collective-permute-start | bytes 786440 | tf_op jit(solution)/shard_map/ppermute | solution.py:445
  27.6 0.8 %collective-permute-start.6 = (bf16[1024,128]{1,0:T(8,128)(2,1)S(1)}, bf16[1024,128]{1,0:T(8,128)(2,1)S(1)}, u32[]{:S(2)}, u32[]{:S(2)}) collective-permute-start(bf16[1024,128]{1,0:T(8,128)(2,1)S(1)} %chunk_sums_1.1.refs_0_.refs_1_), channel_id=1, source_target_pairs={{1,0},{0,1},{3,2},{2,3},{5,4},{4,5},{7,6},{6,7},{9,8},{8,9},{11,10... | collective-permute-start | bytes 786440 | tf_op jit(solution)/shard_map/ppermute | solution.py:486
  28.4 9.1 %collective-permute-done.5.link_ref = bf16[1024,128]{1,0:T(8,128)(2,1)S(1)} collective-permute-done((bf16[1024,128]{1,0:T(8,128)(2,1)S(1)}, bf16[1024,128]{1,0:T(8,128)(2,1)S(1)}, u32[]{:S(2)}, u32[]{:S(2)}) %collective-permute-start.5) | collective-permute-done | bytes 262176 | tf_op jit(solution)/shard_map/ppermute | solution.py:445
  37.5 1.9 %chunk_sums_3.1.refs_3_ = bf16[1024,128]{1,0:T(8,128)(2,1)S(1)} custom-call(s32[256]{0:T(256)S(1)} %get-tuple-element.23.pairs_ref, bf16[36,128,512]{2,1,0:T(8,128)(2,1)S(1)} %get-tuple-element.34.weight_ref, f32[9,128,512]{2,1,0:T(8,128)S(1)} %get-tuple-element.35.acc_ref, f32[9,128,128]{2,1,0:T(8,128)S(1)} %get-tuple-element.36.factor_ref, ...), custom_call_target="tpu_custom_call" | custom-call | tf_op jit(solution)/shard_map/chunk_sums_3/pallas_call | solution.py:474
  39.5 0.9 %collective-permute-start.8 = (bf16[1024,128]{1,0:T(8,128)(2,1)S(1)}, bf16[1024,128]{1,0:T(8,128)(2,1)S(1)}, u32[]{:S(2)}, u32[]{:S(2)}) collective-permute-start(bf16[1024,128]{1,0:T(8,128)(2,1)S(1)} %chunk_sums_3.1.refs_3_), channel_id=1, source_target_pairs={{1,0},{0,1},{3,2},{2,3},{5,4},{4,5},{7,6},{6,7},{9,8},{8,9},{11,10... | collective-permute-start | bytes 786440 | tf_op jit(solution)/shard_map/ppermute | solution.py:486
  40.4 0.0 collective-permute-done.3.link_ref
  40.4 0.0 collective-permute-done.4.refs_0_.refs_4_
  40.4 2.0 %chunk_sums_2.1.refs_2_ = bf16[1024,128]{1,0:T(8,128)(2,1)S(1)} custom-call(s32[256]{0:T(256)S(1)} %get-tuple-element.23.pairs_ref, bf16[36,128,512]{2,1,0:T(8,128)(2,1)S(1)} %get-tuple-element.34.weight_ref, f32[9,128,512]{2,1,0:T(8,128)S(1)} %get-tuple-element.35.acc_ref, f32[9,128,128]{2,1,0:T(8,128)S(1)} %get-tuple-element.36.factor_ref, ...), custom_call_target="tpu_custom_call" | custom-call | tf_op jit(solution)/shard_map/chunk_sums_2/pallas_call | solution.py:474
  42.4 0.7 %collective-permute-start.7 = (bf16[1024,128]{1,0:T(8,128)(2,1)S(1)}, bf16[1024,128]{1,0:T(8,128)(2,1)S(1)}, u32[]{:S(2)}, u32[]{:S(2)}) collective-permute-start(bf16[1024,128]{1,0:T(8,128)(2,1)S(1)} %chunk_sums_2.1.refs_2_), channel_id=1, source_target_pairs={{1,0},{0,1},{3,2},{2,3},{5,4},{4,5},{7,6},{6,7},{9,8},{8,9},{11,10... | collective-permute-start | bytes 786440 | tf_op jit(solution)/shard_map/ppermute | solution.py:486
  43.1 0.0 collective-permute-done.6.refs_5_
  43.1 3.9 %collective-permute-done.8.refs_7_ = bf16[1024,128]{1,0:T(8,128)(2,1)S(1)} collective-permute-done((bf16[1024,128]{1,0:T(8,128)(2,1)S(1)}, bf16[1024,128]{1,0:T(8,128)(2,1)S(1)}, u32[]{:S(2)}, u32[]{:S(2)}) %collective-permute-start.8) | collective-permute-done | bytes 262176 | tf_op jit(solution)/shard_map/ppermute | solution.py:486
  47.0 2.8 %collective-permute-done.7.refs_6_ = bf16[1024,128]{1,0:T(8,128)(2,1)S(1)} collective-permute-done((bf16[1024,128]{1,0:T(8,128)(2,1)S(1)}, bf16[1024,128]{1,0:T(8,128)(2,1)S(1)}, u32[]{:S(2)}, u32[]{:S(2)}) %collective-permute-start.7) | collective-permute-done | bytes 262176 | tf_op jit(solution)/shard_map/ppermute | solution.py:486
  49.8 1.5 %combine.1 = bf16[1024,512]{1,0:T(8,128)(2,1)} custom-call(bf16[1072,128]{1,0:T(8,128)(2,1)S(1)} %chunk_sums_0.1.refs_0_, bf16[1024,128]{1,0:T(8,128)(2,1)S(1)} %chunk_sums_1.1.refs_0_.refs_1_, bf16[1024,128]{1,0:T(8,128)(2,1)S(1)} %chunk_sums_2.1.refs_2_, bf16[1024,128]{1,0:T(8,128)(2,1)S(1)} %chunk_sums_3.1.refs_3_, ...), custom_call_target="tpu_custom_call" | custom-call | tf_op jit(solution)/shard_map/combine/pallas_call | solution.py:489
  (3 shorter events, 0.0 us)
Async XLA Ops:
  2.7 14.3 %collective-permute-start = (bf16[1168,512]{1,0:T(8,128)(2,1)S(1)}, bf16[1168,512]{1,0:T(8,128)(2,1)S(1)}, u32[]{:S(2)}, u32[]{:S(2)}) collective-permute-start(bf16[1168,512]{1,0:T(8,128)(2,1)S(1)} %get-tuple-element.30), channel_id=1, source_target_pairs={{2,0},{0,2},{6,4},{4,6},{10,8},{8,10},{14,12},{12,14},{18,16},{16,... | collective-permute-start | bytes 3588104 | tf_op jit(solution)/shard_map/ppermute | solution.py:410
  2.8 11.6 %collective-permute-start.1 = (bf16[1552,128]{1,0:T(8,128)(2,1)S(1)}, bf16[1552,128]{1,0:T(8,128)(2,1)S(1)}, u32[]{:S(2)}, u32[]{:S(2)}) collective-permute-start(bf16[1552,128]{1,0:T(8,128)(2,1)S(1)} %get-tuple-element.31), channel_id=1, source_target_pairs={{1,0},{0,1},{4,2},{5,3},{2,4},{3,5},{8,6},{9,7},{6,8},{7,9},{12,10... | collective-permute-start | bytes 1191944 | tf_op jit(solution)/shard_map/ppermute | solution.py:409
  14.5 9.3 %collective-permute-start.2 = (bf16[1024,128]{1,0:T(8,128)(2,1)S(1)}, bf16[1024,128]{1,0:T(8,128)(2,1)S(1)}, u32[]{:S(2)}, u32[]{:S(2)}) collective-permute-start(bf16[1024,128]{1,0:T(8,128)(2,1)S(1)} %gate.3), channel_id=1, source_target_pairs={{30,0},{4,2},{2,4},{8,6},{6,8},{12,10},{10,12},{16,14},{14,16},{20... | collective-permute-start | bytes 786440 | tf_op jit(solution)/shard_map/ppermute | solution.py:445
  22.1 18.3 %collective-permute-start.4 = (bf16[1072,128]{1,0:T(8,128)(2,1)S(1)}, bf16[1072,128]{1,0:T(8,128)(2,1)S(1)}, u32[]{:S(2)}, u32[]{:S(2)}) collective-permute-start(bf16[1072,128]{1,0:T(8,128)(2,1)S(1)} %chunk_sums_0.1.refs_0_), channel_id=1, source_target_pairs={{1,0},{0,1},{3,2},{2,3},{5,4},{4,5},{7,6},{6,7},{9,8},{8,9},{11,10... | collective-permute-start | bytes 823304 | tf_op jit(solution)/shard_map/ppermute | solution.py:486
  25.8 11.8 %collective-permute-start.5 = (bf16[1024,128]{1,0:T(8,128)(2,1)S(1)}, bf16[1024,128]{1,0:T(8,128)(2,1)S(1)}, u32[]{:S(2)}, u32[]{:S(2)}) collective-permute-start(bf16[1024,128]{1,0:T(8,128)(2,1)S(1)} %gate.5), channel_id=1, source_target_pairs={{30,0},{4,2},{2,4},{8,6},{6,8},{12,10},{10,12},{16,14},{14,16},{20... | collective-permute-start | bytes 786440 | tf_op jit(solution)/shard_map/ppermute | solution.py:445
  25.8 14.5 %collective-permute-start.3 = (bf16[1024,128]{1,0:T(8,128)(2,1)S(1)}, bf16[1024,128]{1,0:T(8,128)(2,1)S(1)}, u32[]{:S(2)}, u32[]{:S(2)}) collective-permute-start(bf16[1024,128]{1,0:T(8,128)(2,1)S(1)} %gate.4), channel_id=1, source_target_pairs={{30,0},{4,2},{2,4},{8,6},{6,8},{12,10},{10,12},{16,14},{14,16},{20... | collective-permute-start | bytes 786440 | tf_op jit(solution)/shard_map/ppermute | solution.py:445
  27.6 15.5 %collective-permute-start.6 = (bf16[1024,128]{1,0:T(8,128)(2,1)S(1)}, bf16[1024,128]{1,0:T(8,128)(2,1)S(1)}, u32[]{:S(2)}, u32[]{:S(2)}) collective-permute-start(bf16[1024,128]{1,0:T(8,128)(2,1)S(1)} %chunk_sums_1.1.refs_0_.refs_1_), channel_id=1, source_target_pairs={{1,0},{0,1},{3,2},{2,3},{5,4},{4,5},{7,6},{6,7},{9,8},{8,9},{11,10... | collective-permute-start | bytes 786440 | tf_op jit(solution)/shard_map/ppermute | solution.py:486
  39.5 7.5 %collective-permute-start.8 = (bf16[1024,128]{1,0:T(8,128)(2,1)S(1)}, bf16[1024,128]{1,0:T(8,128)(2,1)S(1)}, u32[]{:S(2)}, u32[]{:S(2)}) collective-permute-start(bf16[1024,128]{1,0:T(8,128)(2,1)S(1)} %chunk_sums_3.1.refs_3_), channel_id=1, source_target_pairs={{1,0},{0,1},{3,2},{2,3},{5,4},{4,5},{7,6},{6,7},{9,8},{8,9},{11,10... | collective-permute-start | bytes 786440 | tf_op jit(solution)/shard_map/ppermute | solution.py:486
  42.4 7.5 %collective-permute-start.7 = (bf16[1024,128]{1,0:T(8,128)(2,1)S(1)}, bf16[1024,128]{1,0:T(8,128)(2,1)S(1)}, u32[]{:S(2)}, u32[]{:S(2)}) collective-permute-start(bf16[1024,128]{1,0:T(8,128)(2,1)S(1)} %chunk_sums_2.1.refs_2_), channel_id=1, source_target_pairs={{1,0},{0,1},{3,2},{2,3},{5,4},{4,5},{7,6},{6,7},{9,8},{8,9},{11,10... | collective-permute-start | bytes 786440 | tf_op jit(solution)/shard_map/ppermute | solution.py:486

commit v4 on v3

--- a/solution.py
+++ b/solution.py
@@ -14,7 +14,7 @@
 EDGE = W * BS
 NONE = -1e30
 WIDTH = 128
-UNROLL = 4
+UNROLL = 8
 OWN_AT, HALO_AT, COUNT_AT = 0, 64, 128
 F32, BF16 = jnp.float32, jnp.bfloat16
 
@@ -39,25 +39,8 @@
     return jnp.concatenate([x] * times, axis=1)
 
 
-def value_copies(sizes, value_ref, out, start, lanes, sems):
-    frames = sizes[0]
-    return [
-        pltpu.make_async_copy(
-            value_ref.at[f, pl.ds(start + e * BS, BS), lanes],
-            out.at[pl.ds((e * frames + f) * BS, BS), :],
-            sems.at[e * frames + f],
-        )
-        for e in range(W)
-        for f in range(frames)
-    ]
-
-
-def key_place(sizes, e, f):
-    frames, key_width = sizes[0], sizes[4]
-    per_row = WIDTH // LANES
-    i = e * frames + f
-    at, lane = frames * EDGE + i // per_row * key_width, i % per_row * LANES
-    return slice(at, at + key_width), slice(lane, lane + LANES)
+def value_copy(value_ref, out, start, lanes, sem):
+    return pltpu.make_async_copy(value_ref.at[:, pl.ds(start, EDGE), lanes], out.at[:, pl.ds(0, EDGE), :], sem)
 
 
 def edge_start(pixels, over_link):
@@ -77,7 +60,7 @@
 def lists_and_edge(
     sizes, list_ref, count_ref, query_ref, select_ref, key_ref, shrink_ref, value_ref,
     pairs_ref, link_ref, chip_ref, query_out, select_out, key_out, shrink_out,
-    list_sc, count_sc, sems, key_sems, small_sems,
+    list_sc, count_sc, small_sems, sems,
 ):
     frames, pixels, n_blocks, n_listed, key_width, value_width = sizes
     start = edge_start(pixels, True)
@@ -88,40 +71,33 @@
     ]
     for copy in small:
         copy.start()
-    copies = value_copies(sizes, value_ref, link_ref, start, pl.ds(0, WIDTH), sems.at[0])
+    chip_start = edge_start(pixels, False)
+    copies = [value_copy(value_ref, link_ref, start, pl.ds(0, WIDTH), sems.at[0])]
     for e in range(W):
-        for f in range(frames):
-            copies.append(
-                pltpu.make_async_copy(
-                    key_ref.at[f, :, pl.ds(start + e * BS, BS)],
-                    link_ref.at[key_place(sizes, e, f)],
-                    key_sems.at[e * frames + f],
-                )
+        copies.append(
+            pltpu.make_async_copy(
+                key_ref.at[:, :, pl.ds(start + e * BS, BS)],
+                link_ref.at[:, pl.ds(EDGE + e * key_width, key_width), :],
+                sems.at[1 + e],
             )
+        )
     copies += [
-        pltpu.make_async_copy(query_ref, query_out, small_sems.at[3]),
-        pltpu.make_async_copy(select_ref, select_out, small_sems.at[4]),
-        pltpu.make_async_copy(key_ref, key_out, small_sems.at[5]),
+        pltpu.make_async_copy(query_ref, query_out, sems.at[W + 1]),
+        pltpu.make_async_copy(select_ref, select_out, sems.at[W + 2]),
+        pltpu.make_async_copy(key_ref, key_out, sems.at[W + 3]),
+        value_copy(value_ref, chip_ref, chip_start, slice(None), sems.at[W + 4]),
+        pltpu.make_async_copy(
+            key_ref.at[:, :, pl.ds(chip_start, EDGE)],
+            chip_ref.at[:, pl.ds(EDGE, key_width), pl.ds(0, EDGE)],
+            sems.at[W + 5],
+        ),
     ]
-    chip_start = edge_start(pixels, False)
-    copies += value_copies(sizes, value_ref, chip_ref, chip_start, slice(None), sems.at[1])
-    chip_at = frames * EDGE
-    for e in range(W):
-        for f in range(frames):
-            copies.append(
-                pltpu.make_async_copy(
-                    key_ref.at[f, :, pl.ds(chip_start + e * BS, BS)],
-                    chip_ref.at[pl.ds(chip_at, key_width), pl.ds(f * BS, BS)],
-                    key_sems.at[(W + e) * frames + f],
-                )
-            )
-        chip_at += key_width
     for copy in copies:
         copy.start()
     for copy in small:
         copy.wait()
-    link_ref[link_ref.shape[0] - 16 :, :LANES] = shrink_rows(sizes, shrink_out, start)
-    chip_ref[chip_at : chip_at + 16, :LANES] = shrink_rows(sizes, shrink_out, chip_start)
+    link_ref[0, EDGE + W * key_width :, :] = shrink_rows(sizes, shrink_out, start)
+    chip_ref[0, EDGE + key_width :, :LANES] = shrink_rows(sizes, shrink_out, chip_start)
     odd = lax.rem(lax.axis_index("space"), 2)
 
     left, right = W * (1 - odd), W * odd - (W + n_blocks)
@@ -173,9 +149,11 @@
     values = pltpu.make_async_copy(value_ref, value_sc, sem)
     values.start()
     edges = []
+    at = WIDTH
     for i, link in enumerate(links):
-        lanes = pl.ds((i + 1) * WIDTH, WIDTH)
-        edges += value_copies(sizes, value_ref, link, edge_start(pixels, True), lanes, edge_sems.at[i])
+        lanes = pl.ds(at, link.shape[2])
+        edges.append(value_copy(value_ref, link, edge_start(pixels, True), lanes, edge_sems.at[i]))
+        at += link.shape[2]
     for copy in edges:
         copy.start()
     scale = -math.log2(math.e) / math.sqrt(key_width)
@@ -234,16 +212,16 @@
     keys_sc, shr_sc, score_sc, top_sc, total_sc,
 ):
     frames, pixels, n_blocks, n_listed, key_width, value_width = sizes
-    rows = frames * EDGE
     scale = -math.log2(math.e) / math.sqrt(key_width)
     for e in range(W):
-        at = rows + e * key_width
-        keys_sc[e] = squares_over(chip_ref[at : at + key_width, :])
+        at = EDGE + e * key_width
         for f in range(frames):
-            keys_sc[W + e, :, f * BS : (f + 1) * BS] = squares_over(link_ref[key_place(sizes, e, f)])
+            place = slice(f * BS, (f + 1) * BS)
+            keys_sc[e, :, place] = squares_over(chip_ref[f, EDGE : EDGE + key_width, e * BS : (e + 1) * BS])
+            keys_sc[W + e, :, place] = squares_over(link_ref[f, at : at + key_width, :])
     shrinks = [
-        chip_ref[rows + W * key_width :, :LANES].astype(F32) * scale,
-        link_ref[link_ref.shape[0] - 16 :, :LANES].astype(F32) * scale,
+        chip_ref[0, EDGE + key_width :, :LANES].astype(F32) * scale,
+        link_ref[0, EDGE + W * key_width :, :].astype(F32) * scale,
     ]
     for side in range(2):
         for e in range(W):
@@ -283,7 +261,7 @@
         stats_ref[n_blocks + b : n_blocks + b + 1, :] = jnp.transpose(jnp.broadcast_to(total, (BS, LANES)))[:1, :]
 
 
-def chunk_sums(sizes, lanes, pairs_ref, weight_ref, acc_ref, factor_ref, stats_ref, chip_ref, link_ref, *refs):
+def chunk_sums(sizes, lanes, begin, pairs_ref, weight_ref, acc_ref, factor_ref, stats_ref, chip_ref, link_ref, *refs):
     frames, pixels, n_blocks, n_listed, key_width, value_width = sizes
     cols = frames * BS
     out_ref, sum_sc = refs[-2:]
@@ -295,9 +273,9 @@
     def add(p):
         code = pairs_ref[HALO_AT + p]
         b, h = code >> 2, code & 3
-        at = pl.multiple_of((h & (W - 1)) * cols, cols)
-        chip = chip_ref[pl.ds(at, cols), lanes]
-        v = jnp.where(h >= W, link_ref[pl.ds(at, cols), :], chip)
+        rows = pl.ds(pl.multiple_of((h & (W - 1)) * BS, BS), BS)
+        link = link_ref[:, rows, lanes.start - begin : lanes.stop - begin]
+        v = jnp.where(h >= W, link, chip_ref[:, rows, lanes]).reshape(cols, width)
         sum_sc[b] += jnp.dot(weight_ref[p], v, preferred_element_type=F32)
 
     unrolled(pairs_ref[COUNT_AT + 1], add)
@@ -318,29 +296,31 @@
     return x[:n_blocks], x[n_blocks:]
 
 
-def combine(sizes, *refs):
-    frames, pixels, n_blocks = sizes[:3]
-    n = len(refs) // 2
-    mine, other, out_ref = refs[:n], refs[n : 2 * n], refs[-1]
-
-    def run(first, second):
-        top_a, total_a = unpack_stats(first[0][pixels:, :], n_blocks)
-        top_b, total_b = unpack_stats(second[0][pixels:, :], n_blocks)
-        top = jnp.maximum(top_a, top_b)
-        a, b = jnp.exp2(top_a - top), jnp.exp2(top_b - top)
-        total = total_a * a + total_b * b
-        a, b = a / total, b / total
+def combine(sizes, first_lane, count, *refs):
+    frames, pixels, n_blocks, n_listed, key_width, value_width = sizes
+    begin = first_lane == 0
+    mine, other, refs = refs[:count], refs[count : 2 * count], refs[2 * count :]
+    if begin:
+        out_ref, cols_ref, out_sc, sem = refs
+    else:
+        cols_ref, before_ref, out_ref, out_sc, sem = refs
+
+    def run(one, two):
+        if begin:
+            top_a, total_a = unpack_stats(one[0][pixels:, :], n_blocks)
+            top_b, total_b = unpack_stats(two[0][pixels:, :], n_blocks)
+            top = jnp.maximum(top_a, top_b)
+            a, b = jnp.exp2(top_a - top), jnp.exp2(top_b - top)
+            total = total_a * a + total_b * b
+            a, b = a / total, b / total
         for i in range(n_blocks):
-            col_a = row_to_lanes(a[i : i + 1, :])
-            col_b = row_to_lanes(b[i : i + 1, :])
             r = slice(i * BS, (i + 1) * BS)
-            at = 0
-            for one, two in zip(first, second):
-                width = one.shape[1]
-                times = width // LANES
-                x = one[r, :].astype(F32) * wide(col_a, times) + two[r, :].astype(F32) * wide(col_b, times)
-                out_ref[r, at : at + width] = x.astype(BF16)
-                at += width
+            if begin:
+                cols_ref[0, r, :] = row_to_lanes(a[i : i + 1, :])
+                cols_ref[1, r, :] = row_to_lanes(b[i : i + 1, :])
+            for c in range(count):
+                x = one[c][r, :].astype(F32) * cols_ref[0, r, :] + two[c][r, :].astype(F32) * cols_ref[1, r, :]
+                out_sc[r, c * WIDTH : (c + 1) * WIDTH] = x.astype(BF16)
 
     me = lax.axis_index("tm")
 
@@ -351,6 +331,10 @@
     @pl.when(me != 0)
     def _():
         run(other, mine)
+
+    copy = pltpu.make_async_copy(out_sc, out_ref.at[:, pl.ds(first_lane, count * WIDTH)], sem)
+    copy.start()
+    copy.wait()
 
 
 def shards(n_space, n_tm, query_key, selection, memory_key, shrinkage, memory_value, block_list, block_count):
@@ -359,10 +343,9 @@
     n_blocks, n_listed = block_list.shape
     sizes = (frames, pixels, n_blocks, n_listed, key_width, value_width)
     cols = frames * BS
-    rows = frames * EDGE
     n_chunks = value_width // WIDTH
-    link_rows = rows + W * frames * key_width * LANES // WIDTH + 16
-    chip_rows = rows + W * key_width + 16
+    link_rows = EDGE + W * key_width + 16
+    chip_rows = EDGE + key_width + 16
     max_halo = n_blocks * min(n_listed, 2 * W) + UNROLL
     max_own = n_blocks * n_listed + UNROLL
     struct = jax.ShapeDtypeStruct
@@ -387,8 +370,8 @@
         functools.partial(lists_and_edge, sizes),
         out_shape=(
             struct((256,), jnp.int32),
-            struct((link_rows, WIDTH), BF16),
-            struct((chip_rows, value_width), BF16),
+            struct((frames, link_rows, WIDTH), BF16),
+            struct((frames, chip_rows, value_width), BF16),
             struct(query.shape, BF16),
             struct(select.shape, BF16),
             struct(keys.shape, BF16),
@@ -399,9 +382,8 @@
         scratch_shapes=[
             pltpu.SMEM(block_list.shape, jnp.int32),
             pltpu.SMEM(block_count.shape, jnp.int32),
-            dma((2, W * frames)),
-            dma((2 * W * frames,)),
-            dma((6,)),
+            dma((3,)),
+            dma((W + 6,)),
         ],
         compiler_params=params(1),
         name="lists_and_edge",
@@ -418,21 +400,21 @@
             struct((n_blocks + 1, BS, 2 * key_width), BF16),
             struct((n_blocks + 1, BS, LANES), F32),
         )
-        + (struct((rows, WIDTH), BF16),) * (n_chunks - 1),
+        + (struct((frames, EDGE, value_width - 2 * WIDTH), BF16), struct((frames, EDGE, WIDTH), BF16)),
         in_specs=[SMEM, VMEM, VMEM, VMEM, VMEM, HBM],
-        out_specs=(VMEM,) * (4 + n_chunks),
+        out_specs=(VMEM,) * 7,
         scratch_shapes=[
             pltpu.VMEM((n_blocks, 2 * key_width, cols), BF16),
             pltpu.VMEM((n_blocks, 1, cols), F32),
             pltpu.VMEM((max_own, BS, cols), F32),
             pltpu.VMEM(memory_value.shape, BF16),
             dma,
-            dma((n_chunks - 1, W * frames)),
+            dma((2,)),
         ],
         compiler_params=params(24),
         name="own_part",
     )(pairs, query, select, keys, near_shrink, memory_value)
-    def send_edge(edge, *after):
+    def send_edge(axes, pairs, edge, *after):
         edge = pl.pallas_call(
             gate,
             out_shape=struct(edge.shape, edge.dtype),
@@ -442,9 +424,9 @@
             compiler_params=params(1),
             name="gate",
         )(edge, *after)
-        return lax.ppermute(edge, "space", round_link)
-
-    link_halo.append(send_edge(more_edges[0], link_halo[0], own_top))
+        return lax.ppermute(edge, axes, pairs)
+
+    link_halo.append(send_edge(("space", "tm"), over_link, more_edges[0], link_halo[0], own_top))
 
     weights, factor, stats = pl.pallas_call(
         functools.partial(halo_scores, sizes),
@@ -470,30 +452,43 @@
     for c in range(n_chunks):
         lanes = slice(c * WIDTH, (c + 1) * WIDTH)
         out_rows = pixels + (6 * n_blocks if c == 0 else 0)
-        after = other[:1] if c == 2 else []
+        after = other[:1] if c == n_chunks - 1 else []
+        part, begin = (0, 0) if c == 0 else (2, lanes.start) if c == n_chunks - 1 else (1, WIDTH)
         x = pl.pallas_call(
-            functools.partial(chunk_sums, sizes, lanes),
+            functools.partial(chunk_sums, sizes, lanes, begin),
             out_shape=struct((out_rows, WIDTH), BF16),
             in_specs=[SMEM] + [VMEM] * (6 + len(after)),
             out_specs=VMEM,
             scratch_shapes=[pltpu.VMEM((n_blocks + 1, BS, WIDTH), F32)],
             compiler_params=params(4),
             name=f"chunk_sums_{c}",
-        )(pairs, weights, acc, factor, stats, chip_halo, link_halo[c], *after)
+        )(pairs, weights, acc, factor, stats, chip_halo, link_halo[part], *after)
         mine.append(x)
-        if c + 2 < n_chunks:
-            link_halo.append(send_edge(more_edges[c + 1], x))
+        if c == 0:
+            link_halo.append(send_edge("space", round_link, more_edges[1], x))
         other.append(lax.ppermute(x, "tm", swap) if n_tm == 2 else lax.all_gather(x, "tm"))
 
     if n_tm == 2:
+        n = n_chunks - 1
+        out, cols = pl.pallas_call(
+            functools.partial(combine, sizes, 0, n),
+            out_shape=(pltpu.HBM((pixels, value_width), BF16), struct((2, pixels, LANES), F32)),
+            in_specs=[VMEM] * (2 * n),
+            out_specs=(HBM, VMEM),
+            scratch_shapes=[pltpu.VMEM((pixels, n * WIDTH), BF16), dma],
+            compiler_params=params(2),
+            name="combine_first",
+        )(*mine[:n], *other[:n])
         out = pl.pallas_call(
-            functools.partial(combine, sizes),
-            out_shape=struct((pixels, value_width), BF16),
-            in_specs=[VMEM] * len(mine + other),
-            out_specs=VMEM,
+            functools.partial(combine, sizes, n * WIDTH, 1),
+            out_shape=pltpu.HBM((pixels, value_width), BF16),
+            in_specs=[VMEM] * 3 + [HBM],
+            out_specs=HBM,
+            input_output_aliases={3: 0},
+            scratch_shapes=[pltpu.VMEM((pixels, WIDTH), BF16), dma],
             compiler_params=params(2),
-            name="combine",
-        )(*mine, *other)
+            name="combine_last",
+        )(mine[n], other[n], cols, out)
     else:
         packed = other[0][:, pixels:, :]
         tops, totals = zip(*[unpack_stats(packed[i], n_blocks) for i in range(n_tm)])

time: 50.5 us -> 46.5 us (0.921)
  the two profiles are of different devices: /device:TPU:1 before, /device:TPU:25 now
where the time goes in v4:
time: 46.5 us; the launch traced here: 46.4 us
  waiting for transfers between devices  21.1 us (45%)
  Pallas kernels  19.3 us (42%)
  starting transfers between devices  5.95 us (13%)
    ppermute x1, waiting for transfers between devices, shards(): link_halo = [lax.ppermute(link_edge, ('space', 'tm'), over_link)]  11.1 us
    ppermute x4, waiting for transfers between devices, shards(): lax.ppermute(x, 'tm', swap)  6.46 us
    pallas_call x4, Pallas kernels, shards(): pl.pallas_call(functools.partial(chunk_sums, sizes, lanes, begin), out_sh...  6.45 us
    pallas_call x1, Pallas kernels, shards(): pl.pallas_call(functools.partial(own_part, sizes), out_shape=(struct((n_b...  5.43 us
    ppermute x2, waiting for transfers between devices, send_edge(): return lax.ppermute(edge, axes, pairs)  3.57 us
    ppermute x4, starting transfers between devices, shards(): lax.ppermute(x, 'tm', swap)  3.19 us
    pallas_call x1, Pallas kernels, shards(): pl.pallas_call(functools.partial(halo_scores, sizes), out_shape=(struct((...  2.85 us
    pallas_call x1, Pallas kernels, shards(): pl.pallas_call(functools.partial(lists_and_edge, sizes), out_shape=(struc...  2.36 us
  transfers between devices with their start and end apart: 8, of which 5 were waited for; matrix products, arithmetic and copies ran while one was open for 0% of the time, Pallas kernels for 35%

profile of v4, /device:TPU:25, one launch (start us, length us, event | category | flops | bytes accessed | tf_op | source)
XLA Modules:
  0.0 46.4 jit_solution(13114427203121091297)
XLA Ops:
  0.0 2.4 %lists_and_edge.1 = (s32[256]{0:T(256)S(1)}, bf16[4,400,128]{2,1,0:T(8,128)(2,1)S(1)}, bf16[4,336,512]{2,1,0:T(8,128)(2,1)S(1)}, bf16[64,1024]{1,0:T(8,128)(2,1)...) custom-call(s32[8,6]{1,0:T(8,128)} %list_ref.1, s32[8]{0:T(128)} %count_ref.1, ...), custom_call_target="tpu_custom_call" | custom-call | tf_op jit(solution)/shard_map/lists_and_edge/pallas_call | solution.py:369
  2.4 0.7 %collective-permute-start = (bf16[4,336,512]{2,1,0:T(8,128)(2,1)S(1)}, bf16[4,336,512]{2,1,0:T(8,128)(2,1)S(1)}, u32[]{:S(2)}, u32[]{:S(2)}) collective-permute-start(bf16[4,336,512]{2,1,0:T(8,128)(2,1)S(1)} %get-tuple-element.31), channel_id=1, source_target_pairs={{2,0},{0,2},{6,4},{4,6},{10,8},{8,10},{14,12},{12,14},{18,16},{16,... | collective-permute-start | bytes 4128776 | tf_op jit(solution)/shard_map/ppermute | solution.py:392
  3.1 1.2 %collective-permute-start.1 = (bf16[4,400,128]{2,1,0:T(8,128)(2,1)S(1)}, bf16[4,400,128]{2,1,0:T(8,128)(2,1)S(1)}, u32[]{:S(2)}, u32[]{:S(2)}) collective-permute-start(bf16[4,400,128]{2,1,0:T(8,128)(2,1)S(1)} %get-tuple-element.32), channel_id=1, source_target_pairs={{1,0},{0,1},{4,2},{5,3},{2,4},{3,5},{8,6},{9,7},{6,8},{7,9},{12,10... | collective-permute-start | bytes 1228808 | tf_op jit(solution)/shard_map/ppermute | solution.py:391
  4.3 5.4 %own_part.1 = (f32[9,128,512]{2,1,0:T(8,128)S(1)}, f32[9,128,128]{2,1,0:T(8,128)S(1)}, f32[9,128,128]{2,1,0:T(8,128)S(1)}, bf16[9,128,128]{2,1,0:T(8,128)(2,1)S(...) custom-call(s32[256]{0:T(256)S(1)} %get-tuple-element.24.pairs_ref, ...), custom_call_target="tpu_custom_call" | custom-call | tf_op jit(solution)/shard_map/own_part/pallas_call | solution.py:394
  9.7 11.1 %collective-permute-done.1.link_ref.refs_0_ = bf16[4,400,128]{2,1,0:T(8,128)(2,1)S(1)} collective-permute-done((bf16[4,400,128]{2,1,0:T(8,128)(2,1)S(1)}, bf16[4,400,128]{2,1,0:T(8,128)(2,1)S(1)}, u32[]{:S(2)}, u32[]{:S(2)}) %collective-permute-start.1) | collective-permute-done | bytes 409632 | tf_op jit(solution)/shard_map/ppermute | solution.py:391
  20.8 0.0 collective-permute-start.5
  20.8 0.0 collective-permute-done.chip_ref
  20.8 2.9 %halo_scores.1 = (bf16[40,128,512]{2,1,0:T(8,128)(2,1)S(1)}, f32[9,128,128]{2,1,0:T(8,128)S(1)}, f32[16,128]{1,0:T(8,128)S(1)}) custom-call(s32[256]{0:T(256)S(1)} %get-tuple-element.24.pairs_ref, bf16[9,128,128]{2,1,0:T(8,128)(2,1)S(1)} %get-tuple-element.29.cat_ref, f32[9,128,128]{2,1,0:T(8,128)S(1)} %get-tuple-element.30.self_ref, ...), custom_call_target="tpu_custom_call" | custom-call | tf_op jit(solution)/shard_map/halo_scores/pallas_call | solution.py:431
  23.6 1.6 %chunk_sums_0.1.refs_0_ = bf16[1072,128]{1,0:T(8,128)(2,1)S(1)} custom-call(s32[256]{0:T(256)S(1)} %get-tuple-element.24.pairs_ref, bf16[40,128,512]{2,1,0:T(8,128)(2,1)S(1)} %get-tuple-element.35.weight_ref, f32[9,128,512]{2,1,0:T(8,128)S(1)} %get-tuple-element.36.acc_ref, f32[9,128,128]{2,1,0:T(8,128)S(1)} %get-tuple-element.37.factor_ref, ...), custom_call_target="tpu_custom_call" | custom-call | tf_op jit(solution)/shard_map/chunk_sums_0/pallas_call | solution.py:457
  25.3 1.3 %collective-permute-start.3 = (bf16[1072,128]{1,0:T(8,128)(2,1)S(1)}, bf16[1072,128]{1,0:T(8,128)(2,1)S(1)}, u32[]{:S(2)}, u32[]{:S(2)}) collective-permute-start(bf16[1072,128]{1,0:T(8,128)(2,1)S(1)} %chunk_sums_0.1.refs_0_), channel_id=1, source_target_pairs={{1,0},{0,1},{3,2},{2,3},{5,4},{4,5},{7,6},{6,7},{9,8},{8,9},{11,10... | collective-permute-start | bytes 823304 | tf_op jit(solution)/shard_map/ppermute | solution.py:469
  26.6 0.8 %collective-permute-start.2 = (bf16[4,256,128]{2,1,0:T(8,128)(2,1)S(1)}, bf16[4,256,128]{2,1,0:T(8,128)(2,1)S(1)}, u32[]{:S(2)}, u32[]{:S(2)}) collective-permute-start(bf16[4,256,128]{2,1,0:T(8,128)(2,1)S(1)} %gate.2), channel_id=1, source_target_pairs={{30,0},{4,2},{2,4},{8,6},{6,8},{12,10},{10,12},{16,14},{14,16},{20... | collective-permute-start | bytes 786440 | tf_op jit(solution)/shard_map/ppermute | solution.py:427
  27.4 3.6 %collective-permute-done.5.link_ref = bf16[4,256,256]{2,1,0:T(8,128)(2,1)S(1)} collective-permute-done((bf16[4,256,256]{2,1,0:T(8,128)(2,1)S(1)}, bf16[4,256,256]{2,1,0:T(8,128)(2,1)S(1)}, u32[]{:S(2)}, u32[]{:S(2)}) %collective-permute-start.5) | collective-permute-done | bytes 524320 | tf_op jit(solution)/shard_map/ppermute | solution.py:427
  31.0 1.6 %chunk_sums_1.1.refs_1_ = bf16[1024,128]{1,0:T(8,128)(2,1)S(1)} custom-call(s32[256]{0:T(256)S(1)} %get-tuple-element.24.pairs_ref, bf16[40,128,512]{2,1,0:T(8,128)(2,1)S(1)} %get-tuple-element.35.weight_ref, f32[9,128,512]{2,1,0:T(8,128)S(1)} %get-tuple-element.36.acc_ref, f32[9,128,128]{2,1,0:T(8,128)S(1)} %get-tuple-element.37.factor_ref, ...), custom_call_target="tpu_custom_call" | custom-call | tf_op jit(solution)/shard_map/chunk_sums_1/pallas_call | solution.py:457
  32.6 0.3 collective-permute-start.6
  32.9 1.6 %chunk_sums_2.1.refs_2_ = bf16[1024,128]{1,0:T(8,128)(2,1)S(1)} custom-call(s32[256]{0:T(256)S(1)} %get-tuple-element.24.pairs_ref, bf16[40,128,512]{2,1,0:T(8,128)(2,1)S(1)} %get-tuple-element.35.weight_ref, f32[9,128,512]{2,1,0:T(8,128)S(1)} %get-tuple-element.36.acc_ref, f32[9,128,128]{2,1,0:T(8,128)S(1)} %get-tuple-element.37.factor_ref, ...), custom_call_target="tpu_custom_call" | custom-call | tf_op jit(solution)/shard_map/chunk_sums_2/pallas_call | solution.py:457
  34.5 1.3 %collective-permute-start.7 = (bf16[1024,128]{1,0:T(8,128)(2,1)S(1)}, bf16[1024,128]{1,0:T(8,128)(2,1)S(1)}, u32[]{:S(2)}, u32[]{:S(2)}) collective-permute-start(bf16[1024,128]{1,0:T(8,128)(2,1)S(1)} %chunk_sums_2.1.refs_2_), channel_id=1, source_target_pairs={{1,0},{0,1},{3,2},{2,3},{5,4},{4,5},{7,6},{6,7},{9,8},{8,9},{11,10... | collective-permute-start | bytes 786440 | tf_op jit(solution)/shard_map/ppermute | solution.py:469
  35.8 0.0 collective-permute-done.2.link_ref
  35.8 0.0 collective-permute-done.3.refs_0_.refs_3_
  35.8 1.7 %chunk_sums_3.1.refs_0_ = bf16[1024,128]{1,0:T(8,128)(2,1)S(1)} custom-call(s32[256]{0:T(256)S(1)} %get-tuple-element.24.pairs_ref, bf16[40,128,512]{2,1,0:T(8,128)(2,1)S(1)} %get-tuple-element.35.weight_ref, f32[9,128,512]{2,1,0:T(8,128)S(1)} %get-tuple-element.36.acc_ref, f32[9,128,128]{2,1,0:T(8,128)S(1)} %get-tuple-element.37.factor_ref, ...), custom_call_target="tpu_custom_call" | custom-call | tf_op jit(solution)/shard_map/chunk_sums_3/pallas_call | solution.py:457
  37.4 0.3 collective-permute-start.4
  37.7 2.2 %collective-permute-done.6.refs_4_ = bf16[1024,128]{1,0:T(8,128)(2,1)S(1)} collective-permute-done((bf16[1024,128]{1,0:T(8,128)(2,1)S(1)}, bf16[1024,128]{1,0:T(8,128)(2,1)S(1)}, u32[]{:S(2)}, u32[]{:S(2)}) %collective-permute-start.6) | collective-permute-done | bytes 262176 | tf_op jit(solution)/shard_map/ppermute | solution.py:469
  39.9 2.8 %collective-permute-done.7.refs_5_ = bf16[1024,128]{1,0:T(8,128)(2,1)S(1)} collective-permute-done((bf16[1024,128]{1,0:T(8,128)(2,1)S(1)}, bf16[1024,128]{1,0:T(8,128)(2,1)S(1)}, u32[]{:S(2)}, u32[]{:S(2)}) %collective-permute-start.7) | collective-permute-done | bytes 262176 | tf_op jit(solution)/shard_map/ppermute | solution.py:469
  42.7 1.3 %combine_first.1 = (bf16[1024,512]{1,0:T(8,128)(2,1)}, f32[2,1024,128]{2,1,0:T(8,128)S(1)}) custom-call(bf16[1072,128]{1,0:T(8,128)(2,1)S(1)} %chunk_sums_0.1.refs_0_, bf16[1024,128]{1,0:T(8,128)(2,1)S(1)} %chunk_sums_1.1.refs_1_, bf16[1024,128]{1,0:T(8,128)(2,1)S(1)} %chunk_sums_2.1.refs_2_, bf16[1072,128]{1,0:T(8,128)(2,1)S(1)} %collective-permute-done.3.refs_0_.refs_3_, ...), custom_call_target="tpu_custom_call" | custom-call | tf_op jit(solution)/shard_map/combine_first/pallas_call | solution.py:473
  44.0 1.5 %collective-permute-done.4.refs_1_ = bf16[1024,128]{1,0:T(8,128)(2,1)S(1)} collective-permute-done((bf16[1024,128]{1,0:T(8,128)(2,1)S(1)}, bf16[1024,128]{1,0:T(8,128)(2,1)S(1)}, u32[]{:S(2)}, u32[]{:S(2)}) %collective-permute-start.4) | collective-permute-done | bytes 262176 | tf_op jit(solution)/shard_map/ppermute | solution.py:469
  45.5 0.8 %combine_last.1 = bf16[1024,512]{1,0:T(8,128)(2,1)} custom-call(bf16[1024,128]{1,0:T(8,128)(2,1)S(1)} %chunk_sums_3.1.refs_0_, bf16[1024,128]{1,0:T(8,128)(2,1)S(1)} %collective-permute-done.4.refs_1_, f32[2,1024,128]{2,1,0:T(8,128)S(1)} %get-tuple-element.41.refs_2_, bf16[1024,512]{1,0:T(8,128)(2,1)} %get-tuple-element.42.refs_3_), custom_call_target="tpu_custom_call", output_to_operand_aliasing={{}: (3, {})} | custom-call | tf_op jit(solution)/shard_map/combine_last/pallas_call | solution.py:482
  (2 shorter events, 0.0 us)
Async XLA Ops:
  2.4 18.4 %collective-permute-start = (bf16[4,336,512]{2,1,0:T(8,128)(2,1)S(1)}, bf16[4,336,512]{2,1,0:T(8,128)(2,1)S(1)}, u32[]{:S(2)}, u32[]{:S(2)}) collective-permute-start(bf16[4,336,512]{2,1,0:T(8,128)(2,1)S(1)} %get-tuple-element.31), channel_id=1, source_target_pairs={{2,0},{0,2},{6,4},{4,6},{10,8},{8,10},{14,12},{12,14},{18,16},{16,... | collective-permute-start | bytes 4128776 | tf_op jit(solution)/shard_map/ppermute | solution.py:392
  3.1 17.7 %collective-permute-start.1 = (bf16[4,400,128]{2,1,0:T(8,128)(2,1)S(1)}, bf16[4,400,128]{2,1,0:T(8,128)(2,1)S(1)}, u32[]{:S(2)}, u32[]{:S(2)}) collective-permute-start(bf16[4,400,128]{2,1,0:T(8,128)(2,1)S(1)} %get-tuple-element.32), channel_id=1, source_target_pairs={{1,0},{0,1},{4,2},{5,3},{2,4},{3,5},{8,6},{9,7},{6,8},{7,9},{12,10... | collective-permute-start | bytes 1228808 | tf_op jit(solution)/shard_map/ppermute | solution.py:391
  20.8 10.2 %collective-permute-start.5 = (bf16[4,256,256]{2,1,0:T(8,128)(2,1)S(1)}, bf16[4,256,256]{2,1,0:T(8,128)(2,1)S(1)}, u32[]{:S(2)}, u32[]{:S(2)}) collective-permute-start(bf16[4,256,256]{2,1,0:T(8,128)(2,1)S(1)} %gate.3), channel_id=1, source_target_pairs={{1,0},{0,1},{4,2},{5,3},{2,4},{3,5},{8,6},{9,7},{6,8},{7,9},{12,10... | collective-permute-start | bytes 1572872 | tf_op jit(solution)/shard_map/ppermute | solution.py:427
  25.3 10.5 %collective-permute-start.3 = (bf16[1072,128]{1,0:T(8,128)(2,1)S(1)}, bf16[1072,128]{1,0:T(8,128)(2,1)S(1)}, u32[]{:S(2)}, u32[]{:S(2)}) collective-permute-start(bf16[1072,128]{1,0:T(8,128)(2,1)S(1)} %chunk_sums_0.1.refs_0_), channel_id=1, source_target_pairs={{1,0},{0,1},{3,2},{2,3},{5,4},{4,5},{7,6},{6,7},{9,8},{8,9},{11,10... | collective-permute-start | bytes 823304 | tf_op jit(solution)/shard_map/ppermute | solution.py:469
  26.6 9.2 %collective-permute-start.2 = (bf16[4,256,128]{2,1,0:T(8,128)(2,1)S(1)}, bf16[4,256,128]{2,1,0:T(8,128)(2,1)S(1)}, u32[]{:S(2)}, u32[]{:S(2)}) collective-permute-start(bf16[4,256,128]{2,1,0:T(8,128)(2,1)S(1)} %gate.2), channel_id=1, source_target_pairs={{30,0},{4,2},{2,4},{8,6},{6,8},{12,10},{10,12},{16,14},{14,16},{20... | collective-permute-start | bytes 786440 | tf_op jit(solution)/shard_map/ppermute | solution.py:427
  32.6 7.3 %collective-permute-start.6 = (bf16[1024,128]{1,0:T(8,128)(2,1)S(1)}, bf16[1024,128]{1,0:T(8,128)(2,1)S(1)}, u32[]{:S(2)}, u32[]{:S(2)}) collective-permute-start(bf16[1024,128]{1,0:T(8,128)(2,1)S(1)} %chunk_sums_1.1.refs_1_), channel_id=1, source_target_pairs={{1,0},{0,1},{3,2},{2,3},{5,4},{4,5},{7,6},{6,7},{9,8},{8,9},{11,10... | collective-permute-start | bytes 786440 | tf_op jit(solution)/shard_map/ppermute | solution.py:469
  34.5 8.3 %collective-permute-start.7 = (bf16[1024,128]{1,0:T(8,128)(2,1)S(1)}, bf16[1024,128]{1,0:T(8,128)(2,1)S(1)}, u32[]{:S(2)}, u32[]{:S(2)}) collective-permute-start(bf16[1024,128]{1,0:T(8,128)(2,1)S(1)} %chunk_sums_2.1.refs_2_), channel_id=1, source_target_pairs={{1,0},{0,1},{3,2},{2,3},{5,4},{4,5},{7,6},{6,7},{9,8},{8,9},{11,10... | collective-permute-start | bytes 786440 | tf_op jit(solution)/shard_map/ppermute | solution.py:469
  37.4 8.1 %collective-permute-start.4 = (bf16[1024,128]{1,0:T(8,128)(2,1)S(1)}, bf16[1024,128]{1,0:T(8,128)(2,1)S(1)}, u32[]{:S(2)}, u32[]{:S(2)}) collective-permute-start(bf16[1024,128]{1,0:T(8,128)(2,1)S(1)} %chunk_sums_3.1.refs_0_), channel_id=1, source_target_pairs={{1,0},{0,1},{3,2},{2,3},{5,4},{4,5},{7,6},{6,7},{9,8},{8,9},{11,10... | collective-permute-start | bytes 786440 | tf_op jit(solution)/shard_map/ppermute | solution.py:469

commit v5 on v4

--- a/solution.py
+++ b/solution.py
@@ -59,8 +59,8 @@
 
 def lists_and_edge(
     sizes, list_ref, count_ref, query_ref, select_ref, key_ref, shrink_ref, value_ref,
-    pairs_ref, link_ref, chip_ref, query_out, select_out, key_out, shrink_out,
-    list_sc, count_sc, small_sems, sems,
+    pairs_ref, link_ref, chip_ref, cat_ref, self_ref, keys_ref, shr_ref,
+    list_sc, count_sc, query_out, select_out, key_out, shrink_out, small_sems, sems,
 ):
     frames, pixels, n_blocks, n_listed, key_width, value_width = sizes
     start = edge_start(pixels, True)
@@ -81,10 +81,12 @@
                 sems.at[1 + e],
             )
         )
-    copies += [
+    operands = [
         pltpu.make_async_copy(query_ref, query_out, sems.at[W + 1]),
         pltpu.make_async_copy(select_ref, select_out, sems.at[W + 2]),
         pltpu.make_async_copy(key_ref, key_out, sems.at[W + 3]),
+    ]
+    copies += [
         value_copy(value_ref, chip_ref, chip_start, slice(None), sems.at[W + 4]),
         pltpu.make_async_copy(
             key_ref.at[:, :, pl.ds(chip_start, EDGE)],
@@ -92,7 +94,7 @@
             sems.at[W + 5],
         ),
     ]
-    for copy in copies:
+    for copy in operands + copies:
         copy.start()
     for copy in small:
         copy.wait()
@@ -120,6 +122,24 @@
         pairs_ref[HALO_AT + n_halo + i] = n_blocks * 4
     pairs_ref[COUNT_AT] = n_own
     pairs_ref[COUNT_AT + 1] = n_halo
+    for copy in operands:
+        copy.wait()
+    scale = -math.log2(math.e) / math.sqrt(key_width)
+    for b in range(n_blocks):
+        block = slice(b * BS, (b + 1) * BS)
+        q = query_out[:, block].astype(F32)
+        s = select_out[:, block].astype(F32)
+        both = jnp.concatenate([s, -2.0 * q * s], axis=0)
+        cat_ref[b] = jnp.transpose(both).astype(BF16)
+        self_ref[b] = row_to_lanes(jnp.sum(s * q * q, axis=0, keepdims=True))
+    cat_ref[n_blocks] = jnp.zeros((BS, 2 * key_width), BF16)
+    self_ref[n_blocks] = jnp.zeros((BS, LANES), F32)
+    shrink = shrink_out[...].astype(F32) * scale
+    for l in range(n_blocks):
+        for f in range(frames):
+            block = slice(l * BS, (l + 1) * BS)
+            keys_ref[l, :, f * BS : (f + 1) * BS] = squares_over(key_out[f, :, block])
+            shr_ref[l, :, f * BS : (f + 1) * BS] = shrink[f : f + 1, block]
     for copy in copies:
         copy.wait()
 
@@ -139,10 +159,9 @@
 
 
 def own_part(
-    sizes, pairs_ref, query_ref, select_ref, key_ref, shrink_ref, value_ref,
-    acc_ref, top_ref, total_ref, cat_ref, self_ref, *refs,
+    sizes, pairs_ref, cat_ref, self_ref, keys_ref, shr_ref, value_ref, acc_ref, top_ref, total_ref, *refs
 ):
-    links, (keys_sc, shr_sc, score_sc, value_sc, sem, edge_sems) = refs[:-6], refs[-6:]
+    links, (score_sc, value_sc, sem, edge_sems) = refs[:-4], refs[-4:]
     frames, pixels, n_blocks, n_listed, key_width, value_width = sizes
     cols = frames * BS
     bits = int(math.log2(n_blocks))
@@ -154,24 +173,6 @@
         lanes = pl.ds(at, link.shape[2])
         edges.append(value_copy(value_ref, link, edge_start(pixels, True), lanes, edge_sems.at[i]))
         at += link.shape[2]
-    for copy in edges:
-        copy.start()
-    scale = -math.log2(math.e) / math.sqrt(key_width)
-    for b in range(n_blocks):
-        block = slice(b * BS, (b + 1) * BS)
-        q = query_ref[:, block].astype(F32)
-        s = select_ref[:, block].astype(F32)
-        both = jnp.concatenate([s, -2.0 * q * s], axis=0)
-        cat_ref[b] = jnp.transpose(both).astype(BF16)
-        self_ref[b] = row_to_lanes(jnp.sum(s * q * q, axis=0, keepdims=True))
-    cat_ref[n_blocks] = jnp.zeros((BS, 2 * key_width), BF16)
-    self_ref[n_blocks] = jnp.zeros((BS, LANES), F32)
-    shrink = shrink_ref[...].astype(F32) * scale
-    for l in range(n_blocks):
-        for f in range(frames):
-            block = slice(l * BS, (l + 1) * BS)
-            keys_sc[l, :, f * BS : (f + 1) * BS] = squares_over(key_ref[f, :, block])
-            shr_sc[l, :, f * BS : (f + 1) * BS] = shrink[f : f + 1, block]
     top_ref[...] = jnp.full_like(top_ref, NONE)
     total_ref[...] = jnp.zeros_like(total_ref)
     acc_ref[...] = jnp.zeros_like(acc_ref)
@@ -180,8 +181,8 @@
     def score(p):
         code = pairs_ref[OWN_AT + p]
         b, l = code >> bits, code & (n_blocks - 1)
-        s = jnp.dot(cat_ref[b], keys_sc[l], preferred_element_type=F32)
-        s = (s + wide(self_ref[b], frames)) * shr_sc[l]
+        s = jnp.dot(cat_ref[b], keys_ref[l], preferred_element_type=F32)
+        s = (s + wide(self_ref[b], frames)) * shr_ref[l]
         score_sc[p] = s
         top_ref[b] = functools.reduce(jnp.maximum, lane_tiles(s), top_ref[b])
 
@@ -189,6 +190,8 @@
     for b in range(n_blocks):
         top_ref[b] = jnp.broadcast_to(jnp.max(top_ref[b], axis=1, keepdims=True), (BS, LANES))
     values.wait()
+    for copy in edges:
+        copy.start()
 
     def read(p):
         code = pairs_ref[OWN_AT + p]
@@ -366,46 +369,46 @@
     round_link = [((i - 1 if i % 2 == 0 else i + 1) % n_space, i) for i in range(n_space)]
     swap = [(i ^ 1, i) for i in range(n_tm)]
 
-    pairs, link_edge, chip_edge, query, select, keys, near_shrink = pl.pallas_call(
+    pairs, link_edge, chip_edge, cat, self_term, near_keys, near_shrink = pl.pallas_call(
         functools.partial(lists_and_edge, sizes),
         out_shape=(
             struct((256,), jnp.int32),
             struct((frames, link_rows, WIDTH), BF16),
             struct((frames, chip_rows, value_width), BF16),
-            struct(query.shape, BF16),
-            struct(select.shape, BF16),
-            struct(keys.shape, BF16),
-            struct(shrinkage.shape, BF16),
+            struct((n_blocks + 1, BS, 2 * key_width), BF16),
+            struct((n_blocks + 1, BS, LANES), F32),
+            struct((n_blocks, 2 * key_width, cols), BF16),
+            struct((n_blocks, 1, cols), F32),
         ),
         in_specs=[HBM] * 7,
         out_specs=(SMEM,) + (VMEM,) * 6,
         scratch_shapes=[
             pltpu.SMEM(block_list.shape, jnp.int32),
             pltpu.SMEM(block_count.shape, jnp.int32),
+            pltpu.VMEM(query.shape, BF16),
+            pltpu.VMEM(select.shape, BF16),
+            pltpu.VMEM(keys.shape, BF16),
+            pltpu.VMEM(shrinkage.shape, BF16),
             dma((3,)),
             dma((W + 6,)),
         ],
-        compiler_params=params(1),
+        compiler_params=params(4),
         name="lists_and_edge",
     )(block_list, block_count, query, select, keys, shrinkage, memory_value)
     link_halo = [lax.ppermute(link_edge, ("space", "tm"), over_link)]
     chip_halo = lax.ppermute(chip_edge, "space", on_chip)
 
-    acc, own_top, own_total, cat, self_term, *more_edges = pl.pallas_call(
+    acc, own_top, own_total, *more_edges = pl.pallas_call(
         functools.partial(own_part, sizes),
         out_shape=(
             struct((n_blocks + 1, BS, value_width), F32),
             struct((n_blocks + 1, BS, LANES), F32),
             struct((n_blocks + 1, BS, LANES), F32),
-            struct((n_blocks + 1, BS, 2 * key_width), BF16),
-            struct((n_blocks + 1, BS, LANES), F32),
         )
         + (struct((frames, EDGE, value_width - 2 * WIDTH), BF16), struct((frames, EDGE, WIDTH), BF16)),
         in_specs=[SMEM, VMEM, VMEM, VMEM, VMEM, HBM],
-        out_specs=(VMEM,) * 7,
+        out_specs=(VMEM,) * 5,
         scratch_shapes=[
-            pltpu.VMEM((n_blocks, 2 * key_width, cols), BF16),
-            pltpu.VMEM((n_blocks, 1, cols), F32),
             pltpu.VMEM((max_own, BS, cols), F32),
             pltpu.VMEM(memory_value.shape, BF16),
             dma,
@@ -413,7 +416,7 @@
         ],
         compiler_params=params(24),
         name="own_part",
-    )(pairs, query, select, keys, near_shrink, memory_value)
+    )(pairs, cat, self_term, near_keys, near_shrink, memory_value)
     def send_edge(axes, pairs, edge, *after):
         edge = pl.pallas_call(
             gate,

time: 46.5 us -> 46.6 us (level)
  starting transfers between devices: 5.95 us -> 7.14 us
  waiting for transfers between devices: 21.1 us -> 20 us
    ppermute x2, waiting for transfers between devices: 3.57 us -> 2.38 us  [send_edge(): return lax.ppermute(edge, axes, pairs)]
    ppermute x2, starting transfers between devices: 0.85 us -> 2.03 us  [send_edge(): return lax.ppermute(edge, axes, pairs)]
  transfers between devices with their start and end apart: 8 -> 8, of which waited for: 5 -> 5; matrix products, arithmetic and copies ran while one was open for 0% -> 0% of each run, Pallas kernels for 35% -> 34%
where the time goes in v5:
time: 46.6 us; the launch traced here: 46.4 us
  waiting for transfers between devices  20 us (43%)
  Pallas kernels  19.2 us (41%)
  starting transfers between devices  7.14 us (15%)
    ppermute x1, waiting for transfers between devices, shards(): link_halo = [lax.ppermute(link_edge, ('space', 'tm'), over_link)]  11.1 us
    ppermute x4, waiting for transfers between devices, shards(): lax.ppermute(x, 'tm', swap)  6.55 us
    pallas_call x4, Pallas kernels, shards(): pl.pallas_call(functools.partial(chunk_sums, sizes, lanes, begin), out_sh...  6.36 us
    pallas_call x1, Pallas kernels, shards(): pl.pallas_call(functools.partial(own_part, sizes), out_shape=(struct((n_b...  5.42 us
    ppermute x4, starting transfers between devices, shards(): lax.ppermute(x, 'tm', swap)  3.19 us
    pallas_call x1, Pallas kernels, shards(): pl.pallas_call(functools.partial(halo_scores, sizes), out_shape=(struct((...  2.85 us
    pallas_call x1, Pallas kernels, shards(): pl.pallas_call(functools.partial(lists_and_edge, sizes), out_shape=(struc...  2.39 us
    ppermute x2, waiting for transfers between devices, send_edge(): return lax.ppermute(edge, axes, pairs)  2.38 us
  transfers between devices with their start and end apart: 8, of which 5 were waited for; matrix products, arithmetic and copies ran while one was open for 0% of the time, Pallas kernels for 34%

profile of v5, /device:TPU:25, one launch (start us, length us, event | category | flops | bytes accessed | tf_op | source)
XLA Modules:
  0.0 46.4 jit_solution(8235687880209201115)
XLA Ops:
  0.0 2.4 %lists_and_edge.1 = (s32[256]{0:T(256)S(1)}, bf16[4,400,128]{2,1,0:T(8,128)(2,1)S(1)}, bf16[4,336,512]{2,1,0:T(8,128)(2,1)S(1)}, bf16[9,128,128]{2,1,0:T(8,128)(...) custom-call(s32[8,6]{1,0:T(8,128)} %list_ref.1, s32[8]{0:T(128)} %count_ref.1, ...), custom_call_target="tpu_custom_call" | custom-call | tf_op jit(solution)/shard_map/lists_and_edge/pallas_call | solution.py:372
  2.4 0.7 %collective-permute-start = (bf16[4,336,512]{2,1,0:T(8,128)(2,1)S(1)}, bf16[4,336,512]{2,1,0:T(8,128)(2,1)S(1)}, u32[]{:S(2)}, u32[]{:S(2)}) collective-permute-start(bf16[4,336,512]{2,1,0:T(8,128)(2,1)S(1)} %get-tuple-element.25), channel_id=1, source_target_pairs={{2,0},{0,2},{6,4},{4,6},{10,8},{8,10},{14,12},{12,14},{18,16},{16,... | collective-permute-start | bytes 4128776 | tf_op jit(solution)/shard_map/ppermute | solution.py:399
  3.1 1.2 %collective-permute-start.1 = (bf16[4,400,128]{2,1,0:T(8,128)(2,1)S(1)}, bf16[4,400,128]{2,1,0:T(8,128)(2,1)S(1)}, u32[]{:S(2)}, u32[]{:S(2)}) collective-permute-start(bf16[4,400,128]{2,1,0:T(8,128)(2,1)S(1)} %get-tuple-element.26), channel_id=1, source_target_pairs={{1,0},{0,1},{4,2},{5,3},{2,4},{3,5},{8,6},{9,7},{6,8},{7,9},{12,10... | collective-permute-start | bytes 1228808 | tf_op jit(solution)/shard_map/ppermute | solution.py:398
  4.3 5.4 %own_part.1 = (f32[9,128,512]{2,1,0:T(8,128)S(1)}, f32[9,128,128]{2,1,0:T(8,128)S(1)}, f32[9,128,128]{2,1,0:T(8,128)S(1)}, bf16[4,256,256]{2,1,0:T(8,128)(2,1)S(1)}, bf16[4,256,128]{2,1,0:T(8,128)(2,1)S(1)}) custom-call(s32[256]{0:T(256)S(1)} %get-tuple-element.22.pairs_ref, bf16[9,128,128]{2,1,0:T(8,128)(2,1)S(1)} %get-tuple-element.23.cat_ref, ...), custom_call_target="tpu_custom_call" | custom-call | tf_op jit(solution)/shard_map/own_part/pallas_call | solution.py:401
  9.7 11.1 %collective-permute-done.1.link_ref.refs_0_ = bf16[4,400,128]{2,1,0:T(8,128)(2,1)S(1)} collective-permute-done((bf16[4,400,128]{2,1,0:T(8,128)(2,1)S(1)}, bf16[4,400,128]{2,1,0:T(8,128)(2,1)S(1)}, u32[]{:S(2)}, u32[]{:S(2)}) %collective-permute-start.1) | collective-permute-done | bytes 409632 | tf_op jit(solution)/shard_map/ppermute | solution.py:398
  20.8 0.0 collective-permute-start.5
  20.8 0.0 collective-permute-done.chip_ref
  20.8 2.8 %halo_scores.1 = (bf16[40,128,512]{2,1,0:T(8,128)(2,1)S(1)}, f32[9,128,128]{2,1,0:T(8,128)S(1)}, f32[16,128]{1,0:T(8,128)S(1)}) custom-call(s32[256]{0:T(256)S(1)} %get-tuple-element.22.pairs_ref, bf16[9,128,128]{2,1,0:T(8,128)(2,1)S(1)} %get-tuple-element.23.cat_ref, f32[9,128,128]{2,1,0:T(8,128)S(1)} %get-tuple-element.24.self_ref, ...), custom_call_target="tpu_custom_call" | custom-call | tf_op jit(solution)/shard_map/halo_scores/pallas_call | solution.py:434
  23.7 1.6 %chunk_sums_0.1.refs_0_ = bf16[1072,128]{1,0:T(8,128)(2,1)S(1)} custom-call(s32[256]{0:T(256)S(1)} %get-tuple-element.22.pairs_ref, bf16[40,128,512]{2,1,0:T(8,128)(2,1)S(1)} %get-tuple-element.31.weight_ref, f32[9,128,512]{2,1,0:T(8,128)S(1)} %get-tuple-element.32.acc_ref, f32[9,128,128]{2,1,0:T(8,128)S(1)} %get-tuple-element.33.factor_ref, ...), custom_call_target="tpu_custom_call" | custom-call | tf_op jit(solution)/shard_map/chunk_sums_0/pallas_call | solution.py:460
  25.3 1.3 %collective-permute-start.3 = (bf16[1072,128]{1,0:T(8,128)(2,1)S(1)}, bf16[1072,128]{1,0:T(8,128)(2,1)S(1)}, u32[]{:S(2)}, u32[]{:S(2)}) collective-permute-start(bf16[1072,128]{1,0:T(8,128)(2,1)S(1)} %chunk_sums_0.1.refs_0_), channel_id=1, source_target_pairs={{1,0},{0,1},{3,2},{2,3},{5,4},{4,5},{7,6},{6,7},{9,8},{8,9},{11,10... | collective-permute-start | bytes 823304 | tf_op jit(solution)/shard_map/ppermute | solution.py:472
  26.6 2.0 %collective-permute-start.2 = (bf16[4,256,128]{2,1,0:T(8,128)(2,1)S(1)}, bf16[4,256,128]{2,1,0:T(8,128)(2,1)S(1)}, u32[]{:S(2)}, u32[]{:S(2)}) collective-permute-start(bf16[4,256,128]{2,1,0:T(8,128)(2,1)S(1)} %gate.2), channel_id=1, source_target_pairs={{30,0},{4,2},{2,4},{8,6},{6,8},{12,10},{10,12},{16,14},{14,16},{20... | collective-permute-start | bytes 786440 | tf_op jit(solution)/shard_map/ppermute | solution.py:430
  28.6 2.4 %collective-permute-done.5.link_ref = bf16[4,256,256]{2,1,0:T(8,128)(2,1)S(1)} collective-permute-done((bf16[4,256,256]{2,1,0:T(8,128)(2,1)S(1)}, bf16[4,256,256]{2,1,0:T(8,128)(2,1)S(1)}, u32[]{:S(2)}, u32[]{:S(2)}) %collective-permute-start.5) | collective-permute-done | bytes 524320 | tf_op jit(solution)/shard_map/ppermute | solution.py:430
  31.0 1.6 %chunk_sums_1.1.refs_1_ = bf16[1024,128]{1,0:T(8,128)(2,1)S(1)} custom-call(s32[256]{0:T(256)S(1)} %get-tuple-element.22.pairs_ref, bf16[40,128,512]{2,1,0:T(8,128)(2,1)S(1)} %get-tuple-element.31.weight_ref, f32[9,128,512]{2,1,0:T(8,128)S(1)} %get-tuple-element.32.acc_ref, f32[9,128,128]{2,1,0:T(8,128)S(1)} %get-tuple-element.33.factor_ref, ...), custom_call_target="tpu_custom_call" | custom-call | tf_op jit(solution)/shard_map/chunk_sums_1/pallas_call | solution.py:460
  32.6 0.3 collective-permute-start.6
  32.9 1.6 %chunk_sums_2.1.refs_2_ = bf16[1024,128]{1,0:T(8,128)(2,1)S(1)} custom-call(s32[256]{0:T(256)S(1)} %get-tuple-element.22.pairs_ref, bf16[40,128,512]{2,1,0:T(8,128)(2,1)S(1)} %get-tuple-element.31.weight_ref, f32[9,128,512]{2,1,0:T(8,128)S(1)} %get-tuple-element.32.acc_ref, f32[9,128,128]{2,1,0:T(8,128)S(1)} %get-tuple-element.33.factor_ref, ...), custom_call_target="tpu_custom_call" | custom-call | tf_op jit(solution)/shard_map/chunk_sums_2/pallas_call | solution.py:460
  34.5 1.3 %collective-permute-start.7 = (bf16[1024,128]{1,0:T(8,128)(2,1)S(1)}, bf16[1024,128]{1,0:T(8,128)(2,1)S(1)}, u32[]{:S(2)}, u32[]{:S(2)}) collective-permute-start(bf16[1024,128]{1,0:T(8,128)(2,1)S(1)} %chunk_sums_2.1.refs_2_), channel_id=1, source_target_pairs={{1,0},{0,1},{3,2},{2,3},{5,4},{4,5},{7,6},{6,7},{9,8},{8,9},{11,10... | collective-permute-start | bytes 786440 | tf_op jit(solution)/shard_map/ppermute | solution.py:472
  35.8 0.0 collective-permute-done.2.link_ref
  35.8 0.0 collective-permute-done.3.refs_0_.refs_3_
  35.8 1.6 %chunk_sums_3.1.refs_0_ = bf16[1024,128]{1,0:T(8,128)(2,1)S(1)} custom-call(s32[256]{0:T(256)S(1)} %get-tuple-element.22.pairs_ref, bf16[40,128,512]{2,1,0:T(8,128)(2,1)S(1)} %get-tuple-element.31.weight_ref, f32[9,128,512]{2,1,0:T(8,128)S(1)} %get-tuple-element.32.acc_ref, f32[9,128,128]{2,1,0:T(8,128)S(1)} %get-tuple-element.33.factor_ref, ...), custom_call_target="tpu_custom_call" | custom-call | tf_op jit(solution)/shard_map/chunk_sums_3/pallas_call | solution.py:460
  37.4 0.3 collective-permute-start.4
  37.7 2.3 %collective-permute-done.6.refs_4_ = bf16[1024,128]{1,0:T(8,128)(2,1)S(1)} collective-permute-done((bf16[1024,128]{1,0:T(8,128)(2,1)S(1)}, bf16[1024,128]{1,0:T(8,128)(2,1)S(1)}, u32[]{:S(2)}, u32[]{:S(2)}) %collective-permute-start.6) | collective-permute-done | bytes 262176 | tf_op jit(solution)/shard_map/ppermute | solution.py:472
  39.9 2.8 %collective-permute-done.7.refs_5_ = bf16[1024,128]{1,0:T(8,128)(2,1)S(1)} collective-permute-done((bf16[1024,128]{1,0:T(8,128)(2,1)S(1)}, bf16[1024,128]{1,0:T(8,128)(2,1)S(1)}, u32[]{:S(2)}, u32[]{:S(2)}) %collective-permute-start.7) | collective-permute-done | bytes 262176 | tf_op jit(solution)/shard_map/ppermute | solution.py:472
  42.7 1.3 %combine_first.1 = (bf16[1024,512]{1,0:T(8,128)(2,1)}, f32[2,1024,128]{2,1,0:T(8,128)S(1)}) custom-call(bf16[1072,128]{1,0:T(8,128)(2,1)S(1)} %chunk_sums_0.1.refs_0_, bf16[1024,128]{1,0:T(8,128)(2,1)S(1)} %chunk_sums_1.1.refs_1_, bf16[1024,128]{1,0:T(8,128)(2,1)S(1)} %chunk_sums_2.1.refs_2_, bf16[1072,128]{1,0:T(8,128)(2,1)S(1)} %collective-permute-done.3.refs_0_.refs_3_, ...), custom_call_target="tpu_custom_call" | custom-call | tf_op jit(solution)/shard_map/combine_first/pallas_call | solution.py:476
  44.1 1.5 %collective-permute-done.4.refs_1_ = bf16[1024,128]{1,0:T(8,128)(2,1)S(1)} collective-permute-done((bf16[1024,128]{1,0:T(8,128)(2,1)S(1)}, bf16[1024,128]{1,0:T(8,128)(2,1)S(1)}, u32[]{:S(2)}, u32[]{:S(2)}) %collective-permute-start.4) | collective-permute-done | bytes 262176 | tf_op jit(solution)/shard_map/ppermute | solution.py:472
  45.5 0.9 %combine_last.1 = bf16[1024,512]{1,0:T(8,128)(2,1)} custom-call(bf16[1024,128]{1,0:T(8,128)(2,1)S(1)} %chunk_sums_3.1.refs_0_, bf16[1024,128]{1,0:T(8,128)(2,1)S(1)} %collective-permute-done.4.refs_1_, f32[2,1024,128]{2,1,0:T(8,128)S(1)} %get-tuple-element.37.refs_2_, bf16[1024,512]{1,0:T(8,128)(2,1)} %get-tuple-element.38.refs_3_), custom_call_target="tpu_custom_call", output_to_operand_aliasing={{}: (3, {})} | custom-call | tf_op jit(solution)/shard_map/combine_last/pallas_call | solution.py:485
  (2 shorter events, 0.0 us)
Async XLA Ops:
  2.4 18.4 %collective-permute-start = (bf16[4,336,512]{2,1,0:T(8,128)(2,1)S(1)}, bf16[4,336,512]{2,1,0:T(8,128)(2,1)S(1)}, u32[]{:S(2)}, u32[]{:S(2)}) collective-permute-start(bf16[4,336,512]{2,1,0:T(8,128)(2,1)S(1)} %get-tuple-element.25), channel_id=1, source_target_pairs={{2,0},{0,2},{6,4},{4,6},{10,8},{8,10},{14,12},{12,14},{18,16},{16,... | collective-permute-start | bytes 4128776 | tf_op jit(solution)/shard_map/ppermute | solution.py:399
  3.1 17.7 %collective-permute-start.1 = (bf16[4,400,128]{2,1,0:T(8,128)(2,1)S(1)}, bf16[4,400,128]{2,1,0:T(8,128)(2,1)S(1)}, u32[]{:S(2)}, u32[]{:S(2)}) collective-permute-start(bf16[4,400,128]{2,1,0:T(8,128)(2,1)S(1)} %get-tuple-element.26), channel_id=1, source_target_pairs={{1,0},{0,1},{4,2},{5,3},{2,4},{3,5},{8,6},{9,7},{6,8},{7,9},{12,10... | collective-permute-start | bytes 1228808 | tf_op jit(solution)/shard_map/ppermute | solution.py:398
  20.8 10.2 %collective-permute-start.5 = (bf16[4,256,256]{2,1,0:T(8,128)(2,1)S(1)}, bf16[4,256,256]{2,1,0:T(8,128)(2,1)S(1)}, u32[]{:S(2)}, u32[]{:S(2)}) collective-permute-start(bf16[4,256,256]{2,1,0:T(8,128)(2,1)S(1)} %gate.3), channel_id=1, source_target_pairs={{1,0},{0,1},{4,2},{5,3},{2,4},{3,5},{8,6},{9,7},{6,8},{7,9},{12,10... | collective-permute-start | bytes 1572872 | tf_op jit(solution)/shard_map/ppermute | solution.py:430
  25.3 10.5 %collective-permute-start.3 = (bf16[1072,128]{1,0:T(8,128)(2,1)S(1)}, bf16[1072,128]{1,0:T(8,128)(2,1)S(1)}, u32[]{:S(2)}, u32[]{:S(2)}) collective-permute-start(bf16[1072,128]{1,0:T(8,128)(2,1)S(1)} %chunk_sums_0.1.refs_0_), channel_id=1, source_target_pairs={{1,0},{0,1},{3,2},{2,3},{5,4},{4,5},{7,6},{6,7},{9,8},{8,9},{11,10... | collective-permute-start | bytes 823304 | tf_op jit(solution)/shard_map/ppermute | solution.py:472
  26.6 9.2 %collective-permute-start.2 = (bf16[4,256,128]{2,1,0:T(8,128)(2,1)S(1)}, bf16[4,256,128]{2,1,0:T(8,128)(2,1)S(1)}, u32[]{:S(2)}, u32[]{:S(2)}) collective-permute-start(bf16[4,256,128]{2,1,0:T(8,128)(2,1)S(1)} %gate.2), channel_id=1, source_target_pairs={{30,0},{4,2},{2,4},{8,6},{6,8},{12,10},{10,12},{16,14},{14,16},{20... | collective-permute-start | bytes 786440 | tf_op jit(solution)/shard_map/ppermute | solution.py:430
  32.6 7.3 %collective-permute-start.6 = (bf16[1024,128]{1,0:T(8,128)(2,1)S(1)}, bf16[1024,128]{1,0:T(8,128)(2,1)S(1)}, u32[]{:S(2)}, u32[]{:S(2)}) collective-permute-start(bf16[1024,128]{1,0:T(8,128)(2,1)S(1)} %chunk_sums_1.1.refs_1_), channel_id=1, source_target_pairs={{1,0},{0,1},{3,2},{2,3},{5,4},{4,5},{7,6},{6,7},{9,8},{8,9},{11,10... | collective-permute-start | bytes 786440 | tf_op jit(solution)/shard_map/ppermute | solution.py:472
  34.5 8.3 %collective-permute-start.7 = (bf16[1024,128]{1,0:T(8,128)(2,1)S(1)}, bf16[1024,128]{1,0:T(8,128)(2,1)S(1)}, u32[]{:S(2)}, u32[]{:S(2)}) collective-permute-start(bf16[1024,128]{1,0:T(8,128)(2,1)S(1)} %chunk_sums_2.1.refs_2_), channel_id=1, source_target_pairs={{1,0},{0,1},{3,2},{2,3},{5,4},{4,5},{7,6},{6,7},{9,8},{8,9},{11,10... | collective-permute-start | bytes 786440 | tf_op jit(solution)/shard_map/ppermute | solution.py:472
  37.4 8.2 %collective-permute-start.4 = (bf16[1024,128]{1,0:T(8,128)(2,1)S(1)}, bf16[1024,128]{1,0:T(8,128)(2,1)S(1)}, u32[]{:S(2)}, u32[]{:S(2)}) collective-permute-start(bf16[1024,128]{1,0:T(8,128)(2,1)S(1)} %chunk_sums_3.1.refs_0_), channel_id=1, source_target_pairs={{1,0},{0,1},{3,2},{2,3},{5,4},{4,5},{7,6},{6,7},{9,8},{8,9},{11,10... | collective-permute-start | bytes 786440 | tf_op jit(solution)/shard_map/ppermute | solution.py:472

commit v6 on v5

--- a/solution.py
+++ b/solution.py
@@ -405,7 +405,7 @@
             struct((n_blocks + 1, BS, LANES), F32),
             struct((n_blocks + 1, BS, LANES), F32),
         )
-        + (struct((frames, EDGE, value_width - 2 * WIDTH), BF16), struct((frames, EDGE, WIDTH), BF16)),
+        + (struct((frames, EDGE, WIDTH), BF16), struct((frames, EDGE, value_width - 2 * WIDTH), BF16)),
         in_specs=[SMEM, VMEM, VMEM, VMEM, VMEM, HBM],
         out_specs=(VMEM,) * 5,
         scratch_shapes=[
@@ -429,7 +429,7 @@
         )(edge, *after)
         return lax.ppermute(edge, axes, pairs)
 
-    link_halo.append(send_edge(("space", "tm"), over_link, more_edges[0], link_halo[0], own_top))
+    link_halo.append(send_edge(("space", "tm"), over_link, more_edges[0], own_top))
 
     weights, factor, stats = pl.pallas_call(
         functools.partial(halo_scores, sizes),
@@ -448,15 +448,18 @@
             pltpu.VMEM((n_blocks + 1, BS, LANES), F32),
         ],
         compiler_params=params(12),
+        cost_estimate=pl.CostEstimate(flops=30 * 10**9, bytes_accessed=2**20, transcendentals=0),
         name="halo_scores",
     )(pairs, cat, self_term, chip_halo, link_halo[0], own_top, own_total)
 
+    cost = pl.CostEstimate(flops=30 * 10**9, bytes_accessed=2**20, transcendentals=0)
     mine, other = [], []
     for c in range(n_chunks):
         lanes = slice(c * WIDTH, (c + 1) * WIDTH)
         out_rows = pixels + (6 * n_blocks if c == 0 else 0)
-        after = other[:1] if c == n_chunks - 1 else []
-        part, begin = (0, 0) if c == 0 else (2, lanes.start) if c == n_chunks - 1 else (1, WIDTH)
+        after = other[:1] if c >= 2 else []
+        part = min(c, 2)
+        begin = part * WIDTH
         x = pl.pallas_call(
             functools.partial(chunk_sums, sizes, lanes, begin),
             out_shape=struct((out_rows, WIDTH), BF16),
@@ -464,6 +467,7 @@
             out_specs=VMEM,
             scratch_shapes=[pltpu.VMEM((n_blocks + 1, BS, WIDTH), F32)],
             compiler_params=params(4),
+            cost_estimate=cost if c == 1 else None,
             name=f"chunk_sums_{c}",
         )(pairs, weights, acc, factor, stats, chip_halo, link_halo[part], *after)
         mine.append(x)

time: 46.6 us -> 45.3 us (0.972)
  waiting for transfers between devices: 20 us -> 15.8 us
  starting transfers between devices: 7.14 us -> 9.41 us
    ppermute x1, waiting for transfers between devices: 11.1 us -> 7.33 us  [shards(): link_halo = [lax.ppermute(link_edge, ('space', 'tm'), over_link)]]
    ppermute x4, starting transfers between devices: 3.19 us -> 6.85 us  [shards(): lax.ppermute(x, 'tm', swap)]
    ppermute x2, starting transfers between devices: 2.03 us -> 0.64 us  [send_edge(): return lax.ppermute(edge, axes, pairs)]
    ppermute x4, waiting for transfers between devices: 6.55 us -> 5.25 us  [shards(): lax.ppermute(x, 'tm', swap)]
    ppermute x2, waiting for transfers between devices: 2.38 us -> 3.25 us  [send_edge(): return lax.ppermute(edge, axes, pairs)]
  transfers between devices with their start and end apart: 8 -> 8, of which waited for: 5 -> 4; matrix products, arithmetic and copies ran while one was open for 0% -> 0% of each run, Pallas kernels for 34% -> 37%
where the time goes in v6:
time: 45.3 us; the launch traced here: 44.9 us
  Pallas kernels  19.6 us (43%)
  waiting for transfers between devices  15.8 us (35%)
  starting transfers between devices  9.41 us (21%)
    ppermute x1, waiting for transfers between devices, shards(): link_halo = [lax.ppermute(link_edge, ('space', 'tm'), over_link)]  7.33 us
    ppermute x4, starting transfers between devices, shards(): lax.ppermute(x, 'tm', swap)  6.85 us
    pallas_call x4, Pallas kernels, shards(): pl.pallas_call(functools.partial(chunk_sums, sizes, lanes, begin), out_sh...  6.8 us
    pallas_call x1, Pallas kernels, shards(): pl.pallas_call(functools.partial(own_part, sizes), out_shape=(struct((n_b...  5.42 us
    ppermute x4, waiting for transfers between devices, shards(): lax.ppermute(x, 'tm', swap)  5.25 us
    ppermute x2, waiting for transfers between devices, send_edge(): return lax.ppermute(edge, axes, pairs)  3.25 us
    pallas_call x1, Pallas kernels, shards(): pl.pallas_call(functools.partial(halo_scores, sizes), out_shape=(struct((...  2.85 us
    pallas_call x1, Pallas kernels, shards(): pl.pallas_call(functools.partial(lists_and_edge, sizes), out_shape=(struc...  2.39 us
  transfers between devices with their start and end apart: 8, of which 4 were waited for; matrix products, arithmetic and copies ran while one was open for 0% of the time, Pallas kernels for 37%

profile of v6, /device:TPU:25, one launch (start us, length us, event | category | flops | bytes accessed | tf_op | source)
XLA Modules:
  0.0 44.9 jit_solution(11196768561353341267)
XLA Ops:
  0.0 2.4 %lists_and_edge.1 = (s32[256]{0:T(256)S(1)}, bf16[4,400,128]{2,1,0:T(8,128)(2,1)S(1)}, bf16[4,336,512]{2,1,0:T(8,128)(2,1)S(1)}, bf16[9,128,128]{2,1,0:T(8,128)(...) custom-call(s32[8,6]{1,0:T(8,128)} %list_ref.1, s32[8]{0:T(128)} %count_ref.1, ...), custom_call_target="tpu_custom_call" | custom-call | tf_op jit(solution)/shard_map/lists_and_edge/pallas_call | solution.py:372
  2.4 0.7 %collective-permute-start = (bf16[4,336,512]{2,1,0:T(8,128)(2,1)S(1)}, bf16[4,336,512]{2,1,0:T(8,128)(2,1)S(1)}, u32[]{:S(2)}, u32[]{:S(2)}) collective-permute-start(bf16[4,336,512]{2,1,0:T(8,128)(2,1)S(1)} %get-tuple-element.25), channel_id=1, source_target_pairs={{2,0},{0,2},{6,4},{4,6},{10,8},{8,10},{14,12},{12,14},{18,16},{16,... | collective-permute-start | bytes 4128776 | tf_op jit(solution)/shard_map/ppermute | solution.py:399
  3.1 1.2 %collective-permute-start.1 = (bf16[4,400,128]{2,1,0:T(8,128)(2,1)S(1)}, bf16[4,400,128]{2,1,0:T(8,128)(2,1)S(1)}, u32[]{:S(2)}, u32[]{:S(2)}) collective-permute-start(bf16[4,400,128]{2,1,0:T(8,128)(2,1)S(1)} %get-tuple-element.26), channel_id=1, source_target_pairs={{1,0},{0,1},{4,2},{5,3},{2,4},{3,5},{8,6},{9,7},{6,8},{7,9},{12,10... | collective-permute-start | bytes 1228808 | tf_op jit(solution)/shard_map/ppermute | solution.py:398
  4.3 5.4 %own_part.1 = (f32[9,128,512]{2,1,0:T(8,128)S(1)}, f32[9,128,128]{2,1,0:T(8,128)S(1)}, f32[9,128,128]{2,1,0:T(8,128)S(1)}, bf16[4,256,128]{2,1,0:T(8,128)(2,1)S(1)}, bf16[4,256,256]{2,1,0:T(8,128)(2,1)S(1)}) custom-call(s32[256]{0:T(256)S(1)} %get-tuple-element.22.pairs_ref, bf16[9,128,128]{2,1,0:T(8,128)(2,1)S(1)} %get-tuple-element.23.cat_ref, ...), custom_call_target="tpu_custom_call" | custom-call | tf_op jit(solution)/shard_map/own_part/pallas_call | solution.py:401
  9.8 0.6 %collective-permute-start.5 = (bf16[4,256,128]{2,1,0:T(8,128)(2,1)S(1)}, bf16[4,256,128]{2,1,0:T(8,128)(2,1)S(1)}, u32[]{:S(2)}, u32[]{:S(2)}) collective-permute-start(bf16[4,256,128]{2,1,0:T(8,128)(2,1)S(1)} %gate.3), channel_id=1, source_target_pairs={{1,0},{0,1},{4,2},{5,3},{2,4},{3,5},{8,6},{9,7},{6,8},{7,9},{12,10... | collective-permute-start | bytes 786440 | tf_op jit(solution)/shard_map/ppermute | solution.py:430
  10.4 7.3 %collective-permute-done.1.link_ref = bf16[4,400,128]{2,1,0:T(8,128)(2,1)S(1)} collective-permute-done((bf16[4,400,128]{2,1,0:T(8,128)(2,1)S(1)}, bf16[4,400,128]{2,1,0:T(8,128)(2,1)S(1)}, u32[]{:S(2)}, u32[]{:S(2)}) %collective-permute-start.1) | collective-permute-done | bytes 409632 | tf_op jit(solution)/shard_map/ppermute | solution.py:398
  17.7 0.0 collective-permute-done.chip_ref
  17.7 2.8 %halo_scores.1 = (bf16[40,128,512]{2,1,0:T(8,128)(2,1)S(1)}, f32[9,128,128]{2,1,0:T(8,128)S(1)}, f32[16,128]{1,0:T(8,128)S(1)}) custom-call(s32[256]{0:T(256)S(1)} %get-tuple-element.22.pairs_ref, bf16[9,128,128]{2,1,0:T(8,128)(2,1)S(1)} %get-tuple-element.23.cat_ref, f32[9,128,128]{2,1,0:T(8,128)S(1)} %get-tuple-element.24.self_ref, ...), custom_call_target="tpu_custom_call" | custom-call | flops 30000001024 | bytes 1048576 | tf_op jit(solution)/shard_map/halo_scores/pallas_call | solution.py:434
  20.6 1.6 %chunk_sums_0.1.refs_0_ = bf16[1072,128]{1,0:T(8,128)(2,1)S(1)} custom-call(s32[256]{0:T(256)S(1)} %get-tuple-element.22.pairs_ref, bf16[40,128,512]{2,1,0:T(8,128)(2,1)S(1)} %get-tuple-element.31.weight_ref, f32[9,128,512]{2,1,0:T(8,128)S(1)} %get-tuple-element.32.acc_ref, f32[9,128,128]{2,1,0:T(8,128)S(1)} %get-tuple-element.33.factor_ref, ...), custom_call_target="tpu_custom_call" | custom-call | tf_op jit(solution)/shard_map/chunk_sums_0/pallas_call | solution.py:463
  22.2 1.3 %collective-permute-start.3 = (bf16[1072,128]{1,0:T(8,128)(2,1)S(1)}, bf16[1072,128]{1,0:T(8,128)(2,1)S(1)}, u32[]{:S(2)}, u32[]{:S(2)}) collective-permute-start(bf16[1072,128]{1,0:T(8,128)(2,1)S(1)} %chunk_sums_0.1.refs_0_), channel_id=1, source_target_pairs={{1,0},{0,1},{3,2},{2,3},{5,4},{4,5},{7,6},{6,7},{9,8},{8,9},{11,10... | collective-permute-start | bytes 823304 | tf_op jit(solution)/shard_map/ppermute | solution.py:476
  23.5 0.0 collective-permute-start.2
  23.5 0.0 collective-permute-done.5.link_ref
  23.5 1.7 %chunk_sums_1.1.refs_1_ = bf16[1024,128]{1,0:T(8,128)(2,1)S(1)} custom-call(s32[256]{0:T(256)S(1)} %get-tuple-element.22.pairs_ref, bf16[40,128,512]{2,1,0:T(8,128)(2,1)S(1)} %get-tuple-element.31.weight_ref, f32[9,128,512]{2,1,0:T(8,128)S(1)} %get-tuple-element.32.acc_ref, f32[9,128,128]{2,1,0:T(8,128)S(1)} %get-tuple-element.33.factor_ref, ...), custom_call_target="tpu_custom_call" | custom-call | flops 30000001024 | bytes 1048576 | tf_op jit(solution)/shard_map/chunk_sums_1/pallas_call | solution.py:463
  25.2 4.0 %collective-permute-start.6 = (bf16[1024,128]{1,0:T(8,128)(2,1)S(1)}, bf16[1024,128]{1,0:T(8,128)(2,1)S(1)}, u32[]{:S(2)}, u32[]{:S(2)}) collective-permute-start(bf16[1024,128]{1,0:T(8,128)(2,1)S(1)} %chunk_sums_1.1.refs_1_), channel_id=1, source_target_pairs={{1,0},{0,1},{3,2},{2,3},{5,4},{4,5},{7,6},{6,7},{9,8},{8,9},{11,10... | collective-permute-start | bytes 786440 | tf_op jit(solution)/shard_map/ppermute | solution.py:476
  29.1 0.0 collective-permute-done.3.refs_0_.refs_3_
  29.1 3.2 %collective-permute-done.2.link_ref = bf16[4,256,256]{2,1,0:T(8,128)(2,1)S(1)} collective-permute-done((bf16[4,256,256]{2,1,0:T(8,128)(2,1)S(1)}, bf16[4,256,256]{2,1,0:T(8,128)(2,1)S(1)}, u32[]{:S(2)}, u32[]{:S(2)}) %collective-permute-start.2) | collective-permute-done | bytes 524320 | tf_op jit(solution)/shard_map/ppermute | solution.py:430
  32.4 1.8 %chunk_sums_2.1.refs_2_ = bf16[1024,128]{1,0:T(8,128)(2,1)S(1)} custom-call(s32[256]{0:T(256)S(1)} %get-tuple-element.22.pairs_ref, bf16[40,128,512]{2,1,0:T(8,128)(2,1)S(1)} %get-tuple-element.31.weight_ref, f32[9,128,512]{2,1,0:T(8,128)S(1)} %get-tuple-element.32.acc_ref, f32[9,128,128]{2,1,0:T(8,128)S(1)} %get-tuple-element.33.factor_ref, ...), custom_call_target="tpu_custom_call" | custom-call | tf_op jit(solution)/shard_map/chunk_sums_2/pallas_call | solution.py:463
  34.2 1.0 %collective-permute-start.7 = (bf16[1024,128]{1,0:T(8,128)(2,1)S(1)}, bf16[1024,128]{1,0:T(8,128)(2,1)S(1)}, u32[]{:S(2)}, u32[]{:S(2)}) collective-permute-start(bf16[1024,128]{1,0:T(8,128)(2,1)S(1)} %chunk_sums_2.1.refs_2_), channel_id=1, source_target_pairs={{1,0},{0,1},{3,2},{2,3},{5,4},{4,5},{7,6},{6,7},{9,8},{8,9},{11,10... | collective-permute-start | bytes 786440 | tf_op jit(solution)/shard_map/ppermute | solution.py:476
  35.1 1.8 %chunk_sums_3.1.refs_0_ = bf16[1024,128]{1,0:T(8,128)(2,1)S(1)} custom-call(s32[256]{0:T(256)S(1)} %get-tuple-element.22.pairs_ref, bf16[40,128,512]{2,1,0:T(8,128)(2,1)S(1)} %get-tuple-element.31.weight_ref, f32[9,128,512]{2,1,0:T(8,128)S(1)} %get-tuple-element.32.acc_ref, f32[9,128,128]{2,1,0:T(8,128)S(1)} %get-tuple-element.33.factor_ref, ...), custom_call_target="tpu_custom_call" | custom-call | tf_op jit(solution)/shard_map/chunk_sums_3/pallas_call | solution.py:463
  36.9 0.6 %collective-permute-start.4 = (bf16[1024,128]{1,0:T(8,128)(2,1)S(1)}, bf16[1024,128]{1,0:T(8,128)(2,1)S(1)}, u32[]{:S(2)}, u32[]{:S(2)}) collective-permute-start(bf16[1024,128]{1,0:T(8,128)(2,1)S(1)} %chunk_sums_3.1.refs_0_), channel_id=1, source_target_pairs={{1,0},{0,1},{3,2},{2,3},{5,4},{4,5},{7,6},{6,7},{9,8},{8,9},{11,10... | collective-permute-start | bytes 786440 | tf_op jit(solution)/shard_map/ppermute | solution.py:476
  37.5 0.0 collective-permute-done.6.refs_4_
  37.5 3.8 %collective-permute-done.7.refs_5_ = bf16[1024,128]{1,0:T(8,128)(2,1)S(1)} collective-permute-done((bf16[1024,128]{1,0:T(8,128)(2,1)S(1)}, bf16[1024,128]{1,0:T(8,128)(2,1)S(1)}, u32[]{:S(2)}, u32[]{:S(2)}) %collective-permute-start.7) | collective-permute-done | bytes 262176 | tf_op jit(solution)/shard_map/ppermute | solution.py:476
  41.3 1.3 %combine_first.1 = (bf16[1024,512]{1,0:T(8,128)(2,1)}, f32[2,1024,128]{2,1,0:T(8,128)S(1)}) custom-call(bf16[1072,128]{1,0:T(8,128)(2,1)S(1)} %chunk_sums_0.1.refs_0_, bf16[1024,128]{1,0:T(8,128)(2,1)S(1)} %chunk_sums_1.1.refs_1_, bf16[1024,128]{1,0:T(8,128)(2,1)S(1)} %chunk_sums_2.1.refs_2_, bf16[1072,128]{1,0:T(8,128)(2,1)S(1)} %collective-permute-done.3.refs_0_.refs_3_, ...), custom_call_target="tpu_custom_call" | custom-call | tf_op jit(solution)/shard_map/combine_first/pallas_call | solution.py:480
  42.6 1.5 %collective-permute-done.4.refs_1_ = bf16[1024,128]{1,0:T(8,128)(2,1)S(1)} collective-permute-done((bf16[1024,128]{1,0:T(8,128)(2,1)S(1)}, bf16[1024,128]{1,0:T(8,128)(2,1)S(1)}, u32[]{:S(2)}, u32[]{:S(2)}) %collective-permute-start.4) | collective-permute-done | bytes 262176 | tf_op jit(solution)/shard_map/ppermute | solution.py:476
  44.1 0.8 %combine_last.1 = bf16[1024,512]{1,0:T(8,128)(2,1)} custom-call(bf16[1024,128]{1,0:T(8,128)(2,1)S(1)} %chunk_sums_3.1.refs_0_, bf16[1024,128]{1,0:T(8,128)(2,1)S(1)} %collective-permute-done.4.refs_1_, f32[2,1024,128]{2,1,0:T(8,128)S(1)} %get-tuple-element.37.refs_2_, bf16[1024,512]{1,0:T(8,128)(2,1)} %get-tuple-element.38.refs_3_), custom_call_target="tpu_custom_call", output_to_operand_aliasing={{}: (3, {})} | custom-call | tf_op jit(solution)/shard_map/combine_last/pallas_call | solution.py:489
  (2 shorter events, 0.0 us)
Async XLA Ops:
  2.4 15.3 %collective-permute-start = (bf16[4,336,512]{2,1,0:T(8,128)(2,1)S(1)}, bf16[4,336,512]{2,1,0:T(8,128)(2,1)S(1)}, u32[]{:S(2)}, u32[]{:S(2)}) collective-permute-start(bf16[4,336,512]{2,1,0:T(8,128)(2,1)S(1)} %get-tuple-element.25), channel_id=1, source_target_pairs={{2,0},{0,2},{6,4},{4,6},{10,8},{8,10},{14,12},{12,14},{18,16},{16,... | collective-permute-start | bytes 4128776 | tf_op jit(solution)/shard_map/ppermute | solution.py:399
  3.1 14.6 %collective-permute-start.1 = (bf16[4,400,128]{2,1,0:T(8,128)(2,1)S(1)}, bf16[4,400,128]{2,1,0:T(8,128)(2,1)S(1)}, u32[]{:S(2)}, u32[]{:S(2)}) collective-permute-start(bf16[4,400,128]{2,1,0:T(8,128)(2,1)S(1)} %get-tuple-element.26), channel_id=1, source_target_pairs={{1,0},{0,1},{4,2},{5,3},{2,4},{3,5},{8,6},{9,7},{6,8},{7,9},{12,10... | collective-permute-start | bytes 1228808 | tf_op jit(solution)/shard_map/ppermute | solution.py:398
  9.8 13.7 %collective-permute-start.5 = (bf16[4,256,128]{2,1,0:T(8,128)(2,1)S(1)}, bf16[4,256,128]{2,1,0:T(8,128)(2,1)S(1)}, u32[]{:S(2)}, u32[]{:S(2)}) collective-permute-start(bf16[4,256,128]{2,1,0:T(8,128)(2,1)S(1)} %gate.3), channel_id=1, source_target_pairs={{1,0},{0,1},{4,2},{5,3},{2,4},{3,5},{8,6},{9,7},{6,8},{7,9},{12,10... | collective-permute-start | bytes 786440 | tf_op jit(solution)/shard_map/ppermute | solution.py:430
  22.2 7.0 %collective-permute-start.3 = (bf16[1072,128]{1,0:T(8,128)(2,1)S(1)}, bf16[1072,128]{1,0:T(8,128)(2,1)S(1)}, u32[]{:S(2)}, u32[]{:S(2)}) collective-permute-start(bf16[1072,128]{1,0:T(8,128)(2,1)S(1)} %chunk_sums_0.1.refs_0_), channel_id=1, source_target_pairs={{1,0},{0,1},{3,2},{2,3},{5,4},{4,5},{7,6},{6,7},{9,8},{8,9},{11,10... | collective-permute-start | bytes 823304 | tf_op jit(solution)/shard_map/ppermute | solution.py:476
  23.5 8.9 %collective-permute-start.2 = (bf16[4,256,256]{2,1,0:T(8,128)(2,1)S(1)}, bf16[4,256,256]{2,1,0:T(8,128)(2,1)S(1)}, u32[]{:S(2)}, u32[]{:S(2)}) collective-permute-start(bf16[4,256,256]{2,1,0:T(8,128)(2,1)S(1)} %gate.2), channel_id=1, source_target_pairs={{30,0},{4,2},{2,4},{8,6},{6,8},{12,10},{10,12},{16,14},{14,16},{20... | collective-permute-start | bytes 1572872 | tf_op jit(solution)/shard_map/ppermute | solution.py:430
  25.2 12.4 %collective-permute-start.6 = (bf16[1024,128]{1,0:T(8,128)(2,1)S(1)}, bf16[1024,128]{1,0:T(8,128)(2,1)S(1)}, u32[]{:S(2)}, u32[]{:S(2)}) collective-permute-start(bf16[1024,128]{1,0:T(8,128)(2,1)S(1)} %chunk_sums_1.1.refs_1_), channel_id=1, source_target_pairs={{1,0},{0,1},{3,2},{2,3},{5,4},{4,5},{7,6},{6,7},{9,8},{8,9},{11,10... | collective-permute-start | bytes 786440 | tf_op jit(solution)/shard_map/ppermute | solution.py:476
  34.2 7.1 %collective-permute-start.7 = (bf16[1024,128]{1,0:T(8,128)(2,1)S(1)}, bf16[1024,128]{1,0:T(8,128)(2,1)S(1)}, u32[]{:S(2)}, u32[]{:S(2)}) collective-permute-start(bf16[1024,128]{1,0:T(8,128)(2,1)S(1)} %chunk_sums_2.1.refs_2_), channel_id=1, source_target_pairs={{1,0},{0,1},{3,2},{2,3},{5,4},{4,5},{7,6},{6,7},{9,8},{8,9},{11,10... | collective-permute-start | bytes 786440 | tf_op jit(solution)/shard_map/ppermute | solution.py:476
  36.9 7.2 %collective-permute-start.4 = (bf16[1024,128]{1,0:T(8,128)(2,1)S(1)}, bf16[1024,128]{1,0:T(8,128)(2,1)S(1)}, u32[]{:S(2)}, u32[]{:S(2)}) collective-permute-start(bf16[1024,128]{1,0:T(8,128)(2,1)S(1)} %chunk_sums_3.1.refs_0_), channel_id=1, source_target_pairs={{1,0},{0,1},{3,2},{2,3},{5,4},{4,5},{7,6},{6,7},{9,8},{8,9},{11,10... | collective-permute-start | bytes 786440 | tf_op jit(solution)/shard_map/ppermute | solution.py:476
